TPU v7x, 128 devices: a whole 4x4x4 slice. The times are simulated.
128 devices in a mesh: lon: 16 (over y_hi, x, core), ch: 8 (over y_lo, z).
Axes of the slice: x: 4, y: 4 (y_hi: 2, y_lo: 2; y = y_hi * 2 + y_lo), z: 4, core: 2. Of those that a mesh axis runs over, the one named last changes fastest.
Arguments:
- latents: bfloat16 [96, 2, 1024, 640], P(None, None, 'lon', 'ch'), may hold values from -11 to 11
- next_latents: bfloat16 [96, 2, 1024, 640], P('ch', None, 'lon'), may hold values from -18 to 18
- timesteps: int32 [2], replicated, may hold values from 400 to 900
- resume_steps: int32 [2], replicated, may hold values from 40 to 100
- conv_weights: bfloat16 [2, 3, 3, 640, 640], replicated, may hold values from -0.078125 to 0.078125
- conv_bias: float32 [2, 640], replicated, may hold values from -1.5 to 1.5
- norm_gain: float32 [2, 640], replicated, may hold values from 0.1 to 1.9
- norm_shift: float32 [2, 640], replicated, may hold values from -1.5 to 1.5
- time_w1: float32 [320, 1280], replicated, may hold values from -0.3125 to 0.3125
- time_w2: float32 [1280, 640], replicated, may hold values from -0.15625 to 0.15625
Outputs:
- predicted_noise: bfloat16 [96, 2, 1024, 640], P('ch', None, 'lon')
- logprob: float32 [2], replicated
All inputs are finite; a program needn't handle non-finite values.
Results may differ from a plain program's by a relative error of at most 0.0044.
Values may be sent and summed in bfloat16 or wider, within the bound.
No kernel may reach another device: no remote copies, remote signals or barrier semaphores. Data moves between devices by JAX's collectives and lax.ppermute only.
A program may use at most 576 MiB of HBM per device.

v0:
```python
import functools
import math

import jax
import jax.numpy as jnp
import numpy as np
from jax import lax
from jax.experimental import pallas as pl
from jax.experimental.pallas import tpu as pltpu
from jax.sharding import PartitionSpec as P

GROUPS = 32
C = 640
LAT = 96
ROWS = 12
COLS = 64
SRC = 8
PART = C // SRC
WIDTH = C // GROUPS
TAPS = 9
F32 = jnp.float32
BF16 = jnp.bfloat16
VMEM = pl.BlockSpec(memory_space=pltpu.VMEM)
SMEM = pl.BlockSpec(memory_space=pltpu.SMEM)
ANY = pl.BlockSpec(memory_space=pl.ANY)
CHUNK = 16
LIMIT = 56 * 2**20


def roll(x, by):
    by %= 128
    return x if by == 0 else pltpu.roll(x, by, 1)


def place(q):
    return 2 * q + 3


def side_lanes(of_left, of_right):
    out = np.zeros((128, 128), np.float32)
    for q in range(-1, 7):
        p = place(q)
        out[of_left(q), p] = 1
        out[of_left(q + 6), p + 64] = 1
        out[of_right(q), p + 63] = 1
        out[of_right(q + 6), p - 1] = 1
    return out.astype(BF16)


def halo_lane(s, side, row):
    return 32 * s + 16 * side + row + 1


def halo_taps():
    out = np.zeros((256, 3 * 128), np.float32)
    for k in range(3):
        for s in range(2):
            for side in range(2):
                for row in range(-2, 14):
                    source = 128 * s + 16 * (3 * side + k) + row + 2
                    out[source, 128 * k + halo_lane(s, side, row + 1)] = 1
    return out.astype(BF16)


def lanes(rows):
    return lax.broadcasted_iota(jnp.int32, (rows, 128), 1)


def members(rows, first, base):
    chan = lax.broadcasted_iota(jnp.int32, (rows, 128), 0) + first
    low = (lanes(rows) - base) * WIDTH
    return (chan >= low) & (chan < low + WIDTH)


def silu(x):
    return 0.5 * x * (1.0 + jnp.tanh(0.5 * x))


PARAMS = pltpu.CompilerParams(vmem_limit_bytes=LIMIT)


def sums_kernel(part_ref, cells_hbm, sums_ref, first_ref, last_ref, x, sems):
    half = COLS // 2
    copies = []
    for s in range(2):
        for c in range(2):
            cut = slice(c * half, (c + 1) * half)
            copies.append(
                pltpu.make_async_copy(cells_hbm.at[s, cut], x.at[s, cut], sems.at[2 * s + c])
            )
            copies[-1].start()
    row = jnp.zeros((1, 128), F32)
    for s in range(2):
        total = jnp.zeros((PART, LAT), F32)
        square = jnp.zeros((PART, LAT), F32)
        for c in range(2):
            copies[2 * s + c].wait()

            def add(i, carry):
                total, square = carry
                for j in range(4):
                    v = x[s, c * half + 4 * i + j].astype(F32)
                    total, square = total + v, square + v * v
                return total, square

            total, square = lax.fori_loop(0, half // 4, add, (total, square))
        for k, acc in enumerate((total, square)):
            column = jnp.sum(acc, axis=1, keepdims=True)
            own = members(PART, part_ref[0] * PART, 64 * k + 32 * s)
            row += jnp.sum(jnp.where(own, column, 0.0), axis=0, keepdims=True)
        first_ref[s] = x[s, 0:2]
        last_ref[s] = x[s, COLS - 2 : COLS]
    sums_ref[...] = row


def local_sums(part, cells):
    return pl.pallas_call(
        sums_kernel,
        in_specs=[SMEM, ANY],
        out_specs=[VMEM] * 3,
        out_shape=[
            jax.ShapeDtypeStruct((1, 128), F32),
            jax.ShapeDtypeStruct((2, 2, PART, LAT), BF16),
            jax.ShapeDtypeStruct((2, 2, PART, LAT), BF16),
        ],
        scratch_shapes=[pltpu.VMEM((2, COLS, PART, LAT), BF16), pltpu.SemaphoreType.DMA((4,))],
        compiler_params=PARAMS,
        name="local_sums",
    )(part, cells)


def pack_kernel(cells_hbm, pay_hbm, x, out, taken, turned, sems):
    fetches = [pltpu.make_async_copy(cells_hbm.at[s], x.at[s], sems.at[s]) for s in range(2)]
    for copy in fetches:
        copy.start()
    taken[...] = jnp.zeros_like(taken)
    turned[...] = jnp.zeros_like(turned)
    stores = [
        pltpu.make_async_copy(out.at[s], pay_hbm.at[:, 8 * s : 8 * s + 7], sems.at[2 + s])
        for s in range(2)
    ]
    fetches[0].wait()

    @pl.loop(0, 2 * PART // CHUNK)
    def _(step):
        s, e = step // (PART // CHUNK), step % (PART // CHUNK)

        @pl.when(step == PART // CHUNK)
        def _():
            stores[0].start()
            fetches[1].wait()

        own = pl.ds(pl.multiple_of(e * CHUNK, CHUNK), CHUNK)
        taken[:, 0:LAT] = x[s, :, own, :].astype(F32).reshape(COLS * CHUNK, LAT)
        for j in range(CHUNK):
            across = taken[pl.ds(j, COLS, stride=CHUNK), :].T
            turned[pl.ds(CHUNK + j, LAT, stride=CHUNK), 0:COLS] = across[0:LAT, :]

        def tile(r):
            return turned[CHUNK * (r + 1) : CHUNK * (r + 2), :]

        for d in range(SRC):
            for q in range(7):
                upper, lower = (d * ROWS + q, d * ROWS + q + 6)
                if q == 6:
                    upper, lower = (d * ROWS - 1, d * ROWS + ROWS)
                out[s, d, q, own, :] = (tile(upper) + roll(tile(lower), 64)).astype(BF16)

    stores[1].start()
    for store in stores:
        store.wait()


def pack(cells):
    return pl.pallas_call(
        pack_kernel,
        in_specs=[ANY],
        out_specs=ANY,
        out_shape=jax.ShapeDtypeStruct((SRC, 16, PART, 128), BF16),
        scratch_shapes=[
            pltpu.VMEM((2, COLS, PART, LAT), BF16),
            pltpu.VMEM((2, SRC, 7, PART, 128), BF16),
            pltpu.VMEM((COLS * CHUNK, 128), F32),
            pltpu.VMEM(((LAT + 8) * CHUNK, 128), F32),
            pltpu.SemaphoreType.DMA((4,)),
        ],
        compiler_params=PARAMS,
        cost_estimate=pl.CostEstimate(
            flops=1_000_000_000, bytes_accessed=8_000_000, transcendentals=0
        ),
        name="pack_latents",
    )(cells)


def halo_kernel(first_ref, last_ref, left_ref, right_ref, _, pay_hbm, out, sems):
    lane = lanes(PART)
    pad = jnp.zeros((PART, 128 - LAT), F32)

    @pl.loop(0, 2)
    def _(s):
        near = [left_ref[s, 0], left_ref[s, 1], first_ref[s, 0], last_ref[s, 1],
                right_ref[s, 0], right_ref[s, 1]]
        near = [jnp.concatenate([col.astype(F32), pad], axis=1) for col in near]
        for d in range(SRC):
            halo = jnp.zeros((PART, 128), F32)
            for kind in range(6):
                own = (lane >= 16 * kind) & (lane < 16 * kind + 16)
                halo = jnp.where(own, roll(near[kind], 16 * kind + 2 - d * ROWS), halo)
            out[s, d] = halo.astype(BF16)
        pltpu.make_async_copy(out.at[s], pay_hbm.at[:, 8 * s + 7], sems.at[s]).start()

    for s in range(2):
        pltpu.make_async_copy(out.at[s], pay_hbm.at[:, 8 * s + 7], sems.at[s]).wait()


def pack_halo(first, last, left, right, pay):
    return pl.pallas_call(
        halo_kernel,
        in_specs=[VMEM] * 4 + [ANY],
        out_specs=ANY,
        out_shape=jax.ShapeDtypeStruct((SRC, 16, PART, 128), BF16),
        scratch_shapes=[
            pltpu.VMEM((2, SRC, PART, 128), BF16),
            pltpu.SemaphoreType.DMA((2,)),
        ],
        input_output_aliases={4: 0},
        compiler_params=PARAMS,
        name="pack_halo",
    )(first, last, left, right, pay)


def weight_kernel(j, w_hbm, o_hbm, x, out, sems):
    for t in range(TAPS):
        pltpu.make_async_copy(w_hbm.at[j, t], x.at[t], sems.at[t]).start()

    @pl.loop(0, TAPS)
    def _(t):
        pltpu.make_async_copy(w_hbm.at[j, t], x.at[t], sems.at[t]).wait()
        out[t] = x[t].T
        cut = pl.ds(pl.multiple_of(t * C, 128), C)
        pltpu.make_async_copy(out.at[t], o_hbm.at[:, cut], sems.at[TAPS + t]).start()

    for t in range(TAPS):
        cut = slice(t * C, (t + 1) * C)
        pltpu.make_async_copy(out.at[t], o_hbm.at[:, cut], sems.at[TAPS + t]).wait()


def turn_weights(j, weights):
    return pl.pallas_call(
        functools.partial(weight_kernel, j),
        in_specs=[ANY],
        out_specs=ANY,
        out_shape=jax.ShapeDtypeStruct((C, TAPS * C), BF16),
        scratch_shapes=[
            pltpu.VMEM((TAPS, C, C), BF16),
            pltpu.VMEM((TAPS, C, C), BF16),
            pltpu.SemaphoreType.DMA((2 * TAPS,)),
        ],
        compiler_params=PARAMS,
        cost_estimate=pl.CostEstimate(
            flops=TAPS * 2 * C * C * 256, bytes_accessed=15_000_000, transcendentals=0
        ),
        name=f"turn_weights_{j}",
    )(weights.reshape(2, TAPS, C, C))


def target_kernel(target_hbm, o_hbm, x, out, sems):
    fetch = pltpu.make_async_copy(target_hbm, x, sems.at[0])
    fetch.start()
    fetch.wait()

    @pl.loop(0, 6)
    def _(q):
        for s in range(2):
            out[s, q] = jnp.concatenate([x[q, s], x[q + 6, s]], axis=0).T

    store = pltpu.make_async_copy(out, o_hbm, sems.at[1])
    store.start()
    store.wait()


def turn_target(target):
    return pl.pallas_call(
        target_kernel,
        in_specs=[ANY],
        out_specs=ANY,
        out_shape=jax.ShapeDtypeStruct((2, 6, C, 128), BF16),
        scratch_shapes=[
            pltpu.VMEM((ROWS, 2, COLS, C), BF16),
            pltpu.VMEM((2, 6, C, 128), BF16),
            pltpu.SemaphoreType.DMA((2,)),
        ],
        compiler_params=PARAMS,
        name="turn_target",
    )(target)


def affine(row, par_ref, s, j, scale, offset):
    count = float(LAT * 1024 * WIDTH)

    def of_channel(base):
        picked = jnp.where(members(C, 0, base), row, 0.0)
        return jnp.sum(picked, axis=1, keepdims=True) / count

    mean = of_channel(32 * s)
    spread = of_channel(64 + 32 * s) - mean * mean
    factor = lax.rsqrt(spread + 1e-05) * par_ref[:, 2 * j : 2 * j + 1]
    rest = par_ref[:, 2 * j + 1 : 2 * j + 2] - mean * factor
    scale[...] = jnp.broadcast_to(factor, scale.shape)
    offset[...] = jnp.broadcast_to(rest, offset.shape)


def spread_taps(xs, at, tiles, edge, sides, part):
    rows = PART
    lane = lanes(rows)
    low = lane < 64
    first = (lane == 0) | (lane == 64)
    last = (lane == 63) | (lane == 127)
    for q in range(-1, 7):
        if q == -1:
            tile = jnp.where(low, edge, roll(tiles[5], 64))
        elif q == 6:
            tile = jnp.where(low, roll(tiles[0], 64), edge)
        else:
            tile = tiles[q]
        side = roll(sides[pl.ds(at, rows), :], -place(q))
        taps = (jnp.where(first, side, roll(tile, 1)), tile, jnp.where(last, side, roll(tile, -1)))
        for k, tap in enumerate(taps):
            if q == -1:
                tap = jnp.where(low & (part == 0), 0.0, tap)
            elif q == 6:
                tap = jnp.where((~low) & (part == SRC - 1), 0.0, tap)
            xs[pl.ds(k * C + at, rows), 128 * (q + 1) : 128 * (q + 2)] = tap.astype(BF16)


def product(wv, xs, n, more=None):
    x = jnp.concatenate([xs[:, n + 128 * i : n + 128 * i + 256] for i in range(3)], axis=0)
    if more is not None:
        x = jnp.concatenate([x, more], axis=1)
    return jnp.dot(wv[...], x, preferred_element_type=F32)


def first_kernel(
    part_ref, sums_ref, par_ref, pick_ref, taps_ref, recv_hbm, w_hbm,
    hid_hbm, out_sums, to_next, to_prev, out_halo,
    xs, wv, scale, offset, recv, hid, sides, xh, sems,
):
    fetches = [
        pltpu.make_async_copy(recv_hbm.at[:, 8 * s : 8 * s + 8], recv.at[s], sems.at[s])
        for s in range(2)
    ]
    weights = pltpu.make_async_copy(w_hbm, wv, sems.at[2])
    for copy in (fetches[0], weights, fetches[1]):
        copy.start()
    part = part_ref[0]
    lane = lanes(C)

    def act(x, a, o):
        return silu(x.astype(F32) * a + o)

    def columns(s):
        fetches[s].wait()
        affine(sums_ref[...], par_ref, s, 0, scale.at[s], offset.at[s])
        r = (lane & 15) - 2
        outside = ((part == 0) & (r < 0)) | ((part == SRC - 1) & (r >= ROWS))
        x = act(recv[s, :, 7].reshape(C, 128), scale[s], offset[s])
        halo = jnp.where(outside, 0.0, x).astype(BF16)
        sides[s] = jnp.dot(halo, pick_ref[...], preferred_element_type=F32)
        return halo

    def prepare(s, b):
        at = b * PART if isinstance(b, int) else pl.multiple_of(b * PART, PART)
        a, o = scale[s, pl.ds(at, PART), :], offset[s, pl.ds(at, PART), :]
        tiles = [act(recv[s, b, q], a, o) for q in range(7)]
        spread_taps(xs.at[s], at, tiles[:6], tiles[6], sides.at[s], part)

    halo = columns(0)

    @pl.loop(0, SRC)
    def _(b):
        prepare(0, b)

    weights.wait()
    stores = []

    def put(s, n, value):
        part = hid.at[s, :, n : n + 256]
        part[...] = value + par_ref[:, 5 + s : 6 + s]
        store = pltpu.make_async_copy(
            part, hid_hbm.at[s, :, n : n + 256], sems.at[3 + 3 * s + n // 256]
        )
        store.start()
        stores.append(store)

    put(0, 0, product(wv, xs.at[0], 0))
    both = jnp.concatenate([halo, columns(1)], axis=1)
    for k in range(3):
        picked = jnp.dot(both, taps_ref[:, 128 * k : 128 * k + 128], preferred_element_type=F32)
        for i in range(3):
            t = 3 * i + k
            xh[C * t : C * (t + 1), :] = roll(picked, -i).astype(BF16)
    for n, blocks in ((256, (0, 1, 2, 3)), (512, (4, 5, 6, 7))):
        put(0, n, product(wv, xs.at[0], n))
        for b in blocks:
            prepare(1, b)
    put(1, 0, product(wv, xs.at[1], 0))
    put(1, 256, product(wv, xs.at[1], 256))
    out = product(wv, xs.at[1], 512, xh[...])
    put(1, 512, out[:, 0:256])
    bias = jnp.where(lane < 32, par_ref[:, 5:6], par_ref[:, 6:7])
    out_halo[...] = (out[:, 256:384] + bias).astype(BF16)

    row = jnp.zeros((1, 128), F32)
    low = lanes(128) < 64
    for at in range(0, C, 128):
        for s in range(2):
            pieces = [hid[s, at : at + 128, 128 * q : 128 * (q + 1)] for q in range(6)]
            for k in range(2):
                column = jnp.sum(sum(p * p if k else p for p in pieces), axis=1, keepdims=True)
                own = members(128, at, 64 * k + 32 * s)
                row += jnp.sum(jnp.where(own, column, 0.0), axis=0, keepdims=True)
        start, end = hid.at[:, at : at + 128, 0:128], hid.at[:, at : at + 128, 640:768]
        to_next[at : at + 128, :] = jnp.where(low, roll(end[0], 64), end[1]).astype(BF16)
        to_prev[at : at + 128, :] = jnp.where(low, start[0], roll(start[1], 64)).astype(BF16)
    out_sums[...] = jnp.broadcast_to(row, out_sums.shape)
    for store in stores:
        store.wait()


def first_conv(part, sums, params, pick, taps, recv, weights):
    tile = jax.ShapeDtypeStruct((C, 128), BF16)
    return pl.pallas_call(
        first_kernel,
        in_specs=[SMEM] + [VMEM] * 4 + [ANY] * 2,
        out_specs=[ANY] + [VMEM] * 4,
        out_shape=[
            jax.ShapeDtypeStruct((2, C, 768), F32),
            jax.ShapeDtypeStruct((128, 128), F32),
            tile, tile, tile,
        ],
        scratch_shapes=[
            pltpu.VMEM((2, 3 * C, 1024), BF16),
            pltpu.VMEM((C, TAPS * C), BF16),
            pltpu.VMEM((2, C, 128), F32),
            pltpu.VMEM((2, C, 128), F32),
            pltpu.VMEM((2, SRC, 8, PART, 128), BF16),
            pltpu.VMEM((2, C, 768), F32),
            pltpu.VMEM((2, C, 128), F32),
            pltpu.VMEM((TAPS * C, 128), BF16),
            pltpu.SemaphoreType.DMA((9,)),
        ],
        compiler_params=PARAMS,
        cost_estimate=pl.CostEstimate(
            flops=4 * 768 * C * C * 9, bytes_accessed=20_000_000, transcendentals=0
        ),
        name="first_conv",
    )(part, sums, params, pick, taps, recv, weights)


def second_kernel(
    part_ref, coef_ref, sums_ref, par_ref, pick_ref, near_ref, prev_ref, next_ref,
    hid_hbm, w_hbm, recv_hbm, target_hbm,
    noise_hbm, out_ref,
    xs, wv, hid, lat, target, noise_out, sides, scale, offset, sems,
):
    weights = pltpu.make_async_copy(w_hbm, wv, sems.at[6])
    fetches, later = [], []
    for s in range(2):
        fetches.append(pltpu.make_async_copy(hid_hbm.at[s], hid.at[s], sems.at[s]))
        tiles = recv_hbm.at[:, 8 * s : 8 * s + 6]
        later.append(pltpu.make_async_copy(tiles, lat.at[s], sems.at[2 + s]))
        later.append(pltpu.make_async_copy(target_hbm.at[s], target.at[s], sems.at[4 + s]))
    for copy in (fetches[0], weights, fetches[1], *later):
        copy.start()
    part = part_ref[0]
    row = jnp.sum(sums_ref[...], axis=0, keepdims=True)
    low = lanes(PART) < 64

    def columns(s):
        affine(row, par_ref, s, 1, scale.at[s], offset.at[s])
        halo = silu(near_ref[...].astype(F32) * scale[s] + offset[s]).astype(BF16)
        sides[s] = jnp.dot(halo, pick_ref[s], preferred_element_type=F32)
        fetches[s].wait()

    def prepare(s, b):
        at = b * PART if isinstance(b, int) else pl.multiple_of(b * PART, PART)
        rows = pl.ds(at, PART)
        a, o = scale[s, rows, :], offset[s, rows, :]

        def act(x):
            return silu(x * a + o)

        tiles = [act(hid[s, rows, 128 * q : 128 * (q + 1)]) for q in range(6)]
        above, below = prev_ref[rows, :].astype(F32), next_ref[rows, :].astype(F32)
        if s == 0:
            edge = jnp.where(low, above, roll(below, 64))
        else:
            edge = jnp.where(low, roll(above, 64), below)
        spread_taps(xs.at[s], at, tiles, act(edge), sides.at[s], part)

    def finish(s, n, acc):
        keep, gain = coef_ref[2 * s], coef_ref[2 * s + 1]
        out = product(wv, xs.at[s], n) + par_ref[:, 4:5]
        for h in range(2):
            q = n // 128 + h
            mine = lat[s, :, q].reshape(C, 128).astype(F32)
            noise = (out[:, 128 * h : 128 * h + 128] + mine).astype(BF16)
            center = keep * mine + gain * noise.astype(F32)
            diff = target[s, q].astype(F32) - center
            acc += jnp.sum((diff * diff).reshape(C // 8, 8, 128), axis=0)
            plain = noise.T
            noise_out[s, q] = plain[0:64]
            noise_out[s, q + 6] = plain[64:128]
        return acc

    columns(0)

    @pl.loop(0, SRC)
    def _(b):
        prepare(0, b)

    columns(1)
    weights.wait()
    for copy in later:
        copy.wait()
    result = jnp.zeros((1, 128), F32)
    stores = []
    for s in range(2):
        acc = jnp.zeros((8, 128), F32)
        for n, blocks in ((0, (0, 1, 2)), (256, (3, 4, 5)), (512, (6, 7))):
            acc = finish(s, n, acc)
            if s == 0:
                for b in blocks:
                    prepare(1, b)
        store = pltpu.make_async_copy(noise_out.at[s], noise_hbm.at[:, s], sems.at[7 + s])
        store.start()
        stores.append(store)
        value = jnp.sum(acc, axis=(0, 1), keepdims=True)
        result = jnp.where(lanes(1) == s, value, result)
    out_ref[...] = jnp.broadcast_to(result, out_ref.shape)
    for store in stores:
        store.wait()


def second_conv(part, coef, sums, params, pick, tiles, hidden, weights, recv, target):
    return pl.pallas_call(
        second_kernel,
        in_specs=[SMEM, SMEM] + [VMEM] * 6 + [ANY] * 4,
        out_specs=[ANY, VMEM],
        out_shape=[
            jax.ShapeDtypeStruct((ROWS, 2, COLS, C), BF16),
            jax.ShapeDtypeStruct((128, 128), F32),
        ],
        scratch_shapes=[
            pltpu.VMEM((2, 3 * C, 1024), BF16),
            pltpu.VMEM((C, TAPS * C), BF16),
            pltpu.VMEM((2, C, 768), F32),
            pltpu.VMEM((2, SRC, 6, PART, 128), BF16),
            pltpu.VMEM((2, 6, C, 128), BF16),
            pltpu.VMEM((2, ROWS, COLS, C), BF16),
            pltpu.VMEM((2, C, 128), F32),
            pltpu.VMEM((2, C, 128), F32),
            pltpu.VMEM((2, C, 128), F32),
            pltpu.SemaphoreType.DMA((9,)),
        ],
        compiler_params=PARAMS,
        cost_estimate=pl.CostEstimate(
            flops=4 * 768 * C * C * 9, bytes_accessed=20_000_000, transcendentals=0
        ),
        name="second_conv",
    )(part, coef, sums, params, pick, *tiles, hidden, weights, recv, target)


def time_embed(timesteps, time_w1, time_w2):
    half = time_w1.shape[0] // 2
    freqs = jnp.exp(-math.log(10000.0) * jnp.arange(half, dtype=F32) / half)
    angles = timesteps.astype(F32)[:, None] * freqs[None, :]
    features = jnp.concatenate([jnp.cos(angles), jnp.sin(angles)], axis=1)
    hidden = jax.nn.silu(jnp.dot(features, time_w1, precision=lax.Precision.HIGHEST))
    return jnp.dot(hidden, time_w2, precision=lax.Precision.HIGHEST)


def plan(steps):
    frac = steps.astype(F32) / 1000.0
    return jnp.cos((frac + 0.008) / 1.008 * (math.pi / 2.0)) ** 2


def everywhere(rows, axes):
    got = lax.all_to_all(rows.reshape(-1, 1, 128), axes, 0, 0, tiled=True)
    return got.reshape(-1, 128)


def ring(axis, step, wrap):
    size = lax.axis_size(axis)
    return [(i, (i + step) % size) for i in range(size) if wrap or 0 <= i + step < size]


def swap(array, axis):
    return lax.all_to_all(array, axis, split_axis=0, concat_axis=0, tiled=True)


def after(value, *others):
    return lax.optimization_barrier((value,) + others)[0]


def add_partner(x, axis, step):
    size = lax.axis_size(axis)
    return x + lax.ppermute(x, axis, [(i, i ^ step) for i in range(size)])


def body(
    latents, next_latents, timesteps, resume_steps, conv_weights, conv_bias,
    norm_gain, norm_shift, time_w1, time_w2,
):
    part = lax.axis_index("ch").astype(jnp.int32).reshape(1)
    first_pick = jnp.asarray(side_lanes(lambda r: 16 + r + 2, lambda r: 64 + r + 2))
    second_pick = jnp.asarray(
        np.stack(
            [
                side_lanes(lambda r: halo_lane(s, 0, r), lambda r: halo_lane(s, 1, r))
                for s in range(2)
            ]
        )
    )
    tap_pick = jnp.asarray(halo_taps())

    cells = latents.transpose(1, 2, 3, 0)
    sums, first, last = local_sums(part, cells)
    left = lax.ppermute(last, "lon", ring("lon", 1, True))
    right = lax.ppermute(first, "lon", ring("lon", -1, True))
    for step in (1, 2, 4):
        sums = add_partner(sums, "ch", step)
    pay = pack(after(cells, first))
    sums = add_partner(after(sums, pay), "lon", 8)
    pay = pack_halo(first, last, left, right, pay)
    pay, sums = lax.optimization_barrier((pay, sums))
    recv = swap(pay, "ch")
    for step in (1, 2, 4):
        sums = add_partner(sums, "lon", step)
    conv_weights, time_w1, following = after((conv_weights, time_w1, next_latents), pay)
    turned = [turn_weights(j, conv_weights) for j in range(2)]
    target = turn_target(following)

    temb = time_embed(timesteps, time_w1, time_w2)
    columns = [
        norm_gain[0], norm_shift[0], norm_gain[1], norm_shift[1], conv_bias[1],
        conv_bias[0] + temb[0], conv_bias[0] + temb[1],
    ]
    params = jnp.pad(jnp.stack(columns, axis=1), ((0, 0), (0, 128 - len(columns))))

    alpha = plan(timesteps)
    prior = plan(timesteps - resume_steps)
    variance = (1.0 - prior) / (1.0 - alpha) * (1.0 - alpha / prior)
    keep = (1.0 - prior) * jnp.sqrt(alpha / (prior * (1.0 - alpha)))
    ratio = jnp.sqrt(prior) / jnp.sqrt(alpha)
    coef = jnp.stack([ratio, keep - ratio * jnp.sqrt(1.0 - alpha)], axis=1).reshape(4)

    recv, turned, target = lax.optimization_barrier((recv, turned, target))
    hidden, sums, to_next, to_prev, near = first_conv(
        part, sums, params, first_pick, tap_pick, recv, turned[0]
    )
    from_prev = lax.ppermute(to_next, "ch", ring("ch", 1, False))
    from_next = lax.ppermute(to_prev, "ch", ring("ch", -1, False))
    sums = everywhere(sums, ("lon", "ch"))
    noise, terms = second_conv(
        part, coef, sums, params, second_pick, (near, from_prev, from_next),
        hidden, turned[1], recv, target,
    )
    squares = jnp.sum(everywhere(terms, ("lon", "ch")), axis=0)[:2]
    logprob = (
        -squares / (2.0 * variance) / float(LAT * 1024 * C)
        - 0.5 * jnp.log(variance)
        - 0.5 * math.log(2.0 * math.pi)
    )
    return (noise, logprob)


def solution(mesh):
    return jax.shard_map(
        body,
        mesh=mesh,
        in_specs=(
            P(None, None, "lon", "ch"),
            P("ch", None, "lon", None),
            P(), P(), P(), P(), P(), P(), P(), P(),
        ),
        out_specs=(P("ch", None, "lon", None), P()),
        check_vma=False,
    )
```

profile of v0, /device:TPU:1, one launch (start us, length us, event | category | flops | bytes accessed | tf_op | source)
XLA Modules:
  0.0 157.3 jit_solution(15012940559433108887)
XLA Ops:
  0.6 0.0 copy-start
  0.6 2.9 %local_sums.1 = (f32[1,128]{1,0:T(1,128)}, bf16[2,2,80,96]{3,2,1,0:T(8,128)(2,1)}, bf16[2,2,80,96]{3,2,1,0:T(8,128)(2,1)}) custom-call(s32[1]{0:T(128)} %bitcast.part_ref, bf16[2,64,80,96]{3,2,1,0:T(8,128)(2,1)} %bitcast.32), custom_call_target="tpu_custom_call" | custom-call | tf_op jit(solution)/shard_map/local_sums/pallas_call | solution.py:117
  3.6 2.5 %collective-permute-start.2 = (f32[1,128]{1,0:T(1,128)}, f32[1,128]{1,0:T(1,128)S(1)}, u32[]{:S(2)}, u32[]{:S(2)}) collective-permute-start(f32[1,128]{1,0:T(1,128)} %get-tuple-element.26), channel_id=1, source_target_pairs={{0,1},{1,0},{2,3},{3,2},{4,5},{5,4},{6,7},{7,6},{8,9},{9,8},{10,11... | collective-permute-start | bytes 1544 | tf_op jit(solution)/shard_map/ppermute | solution.py:608
  6.1 1.1 collective-permute-done.2
  7.2 0.6 add.62
  7.9 3.4 %collective-permute-start.3 = (f32[1,128]{1,0:T(1,128)S(1)}, f32[1,128]{1,0:T(1,128)S(1)}, u32[]{:S(2)}, u32[]{:S(2)}) collective-permute-start(f32[1,128]{1,0:T(1,128)S(1)} %add.62), channel_id=1, source_target_pairs={{0,2},{1,3},{2,0},{3,1},{4,6},{5,7},{6,4},{7,5},{8,10},{9,11},{10,... | collective-permute-start | bytes 1544 | tf_op jit(solution)/shard_map/ppermute | solution.py:608
  11.3 2.0 %collective-permute-start.1 = (bf16[2,2,80,96]{3,2,1,0:T(8,128)(2,1)}, bf16[2,2,80,96]{3,2,1,0:T(8,128)(2,1)S(1)}, u32[]{:S(2)}, u32[]{:S(2)}) collective-permute-start(bf16[2,2,80,96]{3,2,1,0:T(8,128)(2,1)} %get-tuple-element.23.first_ref), channel_id=1, source_target_pairs={{0,120},{8,0},{16,8},{24,16},{32,24},{40,32},{48,40},{56,48},{64,5... | collective-permute-start | bytes 184328 | tf_op jit(solution)/shard_map/ppermute | solution.py:630
  13.3 1.1 collective-permute-start
  14.4 0.0 collective-permute-done.3
  14.4 1.3 collective-permute-start.4
  15.7 8.3 %pack_latents.1._ = bf16[8,16,80,128]{3,2,1,0:T(8,128)(2,1)} custom-call(bf16[2,64,80,96]{3,2,1,0:T(8,128)(2,1)} %bitcast.33), custom_call_target="tpu_custom_call" | custom-call | flops 1000000000 | bytes 8000000 | tf_op jit(solution)/shard_map/pack_latents/pallas_call | solution.py:175
  23.9 0.0 collective-permute-done.4
  24.0 2.7 %collective-permute-start.5 = (f32[1,128]{1,0:T(1,128)S(1)}, f32[1,128]{1,0:T(1,128)S(1)}, u32[]{:S(2)}, u32[]{:S(2)}) collective-permute-start(f32[1,128]{1,0:T(1,128)S(1)} %add.64), channel_id=1, source_target_pairs={{0,64},{8,72},{16,80},{24,88},{32,96},{40,104},{48,112},{56,120},{... | collective-permute-start | bytes 1544 | tf_op jit(solution)/shard_map/ppermute | solution.py:608
  26.7 1.3 collective-permute-done.5
  27.9 0.0 collective-permute-done.1.right_ref
  28.0 0.0 collective-permute-done.left_ref
  28.0 0.6 copy-done.1
  28.6 0.6 copy-done.2
  29.2 2.3 %pack_halo.1 = bf16[8,16,80,128]{3,2,1,0:T(8,128)(2,1)} custom-call(bf16[2,2,80,96]{3,2,1,0:T(8,128)(2,1)} %get-tuple-element.23.first_ref, bf16[2,2,80,96]{3,2,1,0:T(8,128)(2,1)} %get-tuple-element.24.last_ref, bf16[2,2,80,96]{3,2,1,0:T(8,128)(2,1)} %copy-done.2, bf16[2,2,80,96]{3,2,1,0:T(8,128)(2,1)} %copy-done.1, ...), custom_call_target="tpu_custom_call", output_to_operand_aliasing={{}: (4, {})} | custom-call | tf_op jit(solution)/shard_map/pack_halo/pallas_call | solution.py:217
  31.5 0.0 copy-start.7
  31.6 0.0 copy-start.8
  31.6 0.0 copy-start.6
  31.6 4.5 %all-to-all-start = ((bf16[8,16,80,128]{3,2,1,0:T(8,128)(2,1)}), bf16[8,16,80,128]{3,2,1,0:T(8,128)(2,1)}, u32[]{:S(2)}, u32[]{:S(2)}) async-start(bf16[8,16,80,128]{3,2,1,0:T(8,128)(2,1)} %pack_halo.1), calls=%async_computation | async-start | bytes 5242880 | tf_op jit(solution)/shard_map/all_to_all | solution.py:599
  36.1 0.0 copy-done.7
  36.1 0.0 copy-start.4
  36.2 0.0 copy-start.5
  36.2 0.0 copy-done.8
  36.2 0.1 fusion.11
  36.3 0.1 multiply_cosine_fusion
  36.4 0.0 copy-done.6
  36.4 3.1 %collective-permute-start.6 = (f32[1,128]{1,0:T(1,128)S(1)}, f32[1,128]{1,0:T(1,128)S(1)}, u32[]{:S(2)}, u32[]{:S(2)}) collective-permute-start(f32[1,128]{1,0:T(1,128)S(1)} %add.65), channel_id=1, source_target_pairs={{0,8},{8,0},{16,24},{24,16},{32,40},{40,32},{48,56},{56,48},{64,72... | collective-permute-start | bytes 1544 | tf_op jit(solution)/shard_map/ppermute | solution.py:608
  39.6 2.3 %fusion.5 = f32[2,1280]{1,0:T(2,128)S(1)} fusion(f32[320,1280]{1,0:T(8,128)} %param.21, f32[2,160]{1,0:T(2,128)S(1)} %get-tuple-element.54, f32[2,160]{1,0:T(2,128)S(1)} %get-tuple-element.53), kind=kOutput, calls=%fused_computation.6 | convolution fusion | flops 9831040 | bytes 1651200 | tf_op jit(solution)/shard_map/dot_general | solution.py:579
  41.8 0.0 copy-done
  41.8 1.7 %fusion = f32[2,640]{1,0:T(2,128)S(1)} fusion(f32[1280,640]{1,0:T(8,128)S(1)} %copy-done, f32[2,1280]{1,0:T(2,128)S(1)} %fusion.5), kind=kOutput, calls=%fused_computation.1 | convolution fusion | flops 19671040 | bytes 3292160 | tf_op jit(solution)/shard_map/dot_general | solution.py:580
  43.5 0.0 copy-done.4
  43.5 0.0 copy-done.5
  43.5 6.4 %turn_weights_0.1.w_hbm = bf16[640,5760]{1,0:T(8,128)(2,1)} custom-call(bf16[2,9,640,640]{3,2,1,0:T(8,128)(2,1)} %bitcast.30), custom_call_target="tpu_custom_call" | custom-call | flops 1887436800 | bytes 15000000 | tf_op jit(solution)/shard_map/turn_weights_0/pallas_call | solution.py:249
  49.9 0.0 collective-permute-done.6
  49.9 0.6 collective-permute-start.7
  50.6 6.3 %turn_weights_1.1.w_hbm = bf16[640,5760]{1,0:T(8,128)(2,1)} custom-call(bf16[2,9,640,640]{3,2,1,0:T(8,128)(2,1)} %bitcast.31), custom_call_target="tpu_custom_call" | custom-call | flops 1887436800 | bytes 15000000 | tf_op jit(solution)/shard_map/turn_weights_1/pallas_call | solution.py:249
  56.9 3.7 %turn_target.1.target_hbm = bf16[2,6,640,128]{3,2,1,0:T(8,128)(2,1)} custom-call(bf16[12,2,64,640]{3,2,1,0:T(8,128)(2,1)} %target_hbm), custom_call_target="tpu_custom_call" | custom-call | tf_op jit(solution)/shard_map/turn_target/pallas_call | solution.py:283
  60.6 0.0 collective-permute-done.7
  60.7 2.5 %collective-permute-start.8 = (f32[1,128]{1,0:T(1,128)S(1)}, f32[1,128]{1,0:T(1,128)S(1)}, u32[]{:S(2)}, u32[]{:S(2)}) collective-permute-start(f32[1,128]{1,0:T(1,128)S(1)} %add.67), channel_id=1, source_target_pairs={{0,32},{8,40},{16,48},{24,56},{32,0},{40,8},{48,16},{56,24},{64,96... | collective-permute-start | bytes 1544 | tf_op jit(solution)/shard_map/ppermute | solution.py:608
  63.2 0.9 copy.26
  64.1 1.7 %pad.4.par_ref = f32[640,128]{1,0:T(8,128)} pad(f32[640,7]{1,0:T(8,128)} %copy.26, f32[]{:T(128)} %constant.41.clone.1), padding=0_0x0_121 | pad | bytes 345604 | tf_op jit(solution)/shard_map/jit(_pad)/pad | solution.py:649
  65.9 0.0 collective-permute-done.8
  65.9 0.6 add.68.sums_ref
  66.5 1.4 all-to-all-done.recv_hbm
  67.9 24.3 %first_conv.1 = (f32[2,640,768]{2,1,0:T(8,128)}, f32[128,128]{1,0:T(8,128)}, bf16[640,128]{1,0:T(8,128)(2,1)}, bf16[640,128]{1,0:T(8,128)(2,1)}, bf16[640,128]{1,0:T(8,128)(2,1)}) custom-call(s32[1]{0:T(128)} %bitcast.part_ref, f32[1,128]{1,0:T(1,128)} %add.68.sums_ref, f32[640,128]{1,0:T(8,128)} %pad.4.par_ref, bf16[128,128]{1,0:T(8,128)(2,1)} %constant.46.clone.pick_ref, ...), custom_call_target="tpu_custom_call" | custom-call | flops 11324620800 | bytes 20000000 | tf_op jit(solution)/shard_map/first_conv/pallas_call | solution.py:432
  92.2 1.3 collective-permute-start.10
  93.5 4.6 %collective-permute-start.9 = (bf16[640,128]{1,0:T(8,128)(2,1)}, bf16[640,128]{1,0:T(8,128)(2,1)}, u32[]{:S(2)}, u32[]{:S(2)}) collective-permute-start(bf16[640,128]{1,0:T(8,128)(2,1)} %get-tuple-element.37), channel_id=1, source_target_pairs={{0,1},{1,2},{2,3},{3,4},{4,5},{5,6},{6,7},{8,9},{9,10},{10,11},{11... | collective-permute-start | bytes 491528 | tf_op jit(solution)/shard_map/ppermute | solution.py:662
  98.2 0.1 subtract_bitcast_fusion
  98.2 12.5 %all-to-all-start.1 = ((f32[128,1,128]{2,1,0:T(1,128)}), f32[128,1,128]{2,1,0:T(1,128)S(1)}, u32[]{:S(2)}, u32[]{:S(2)}) async-start(f32[128,1,128]{2,1,0:T(1,128)} %bitcast.35), calls=%async_computation.1 | async-start | bytes 131072 | tf_op jit(solution)/shard_map/all_to_all | solution.py:589
  110.8 0.1 copy.25
  110.9 0.6 reshape.67.coef_ref
  111.5 8.8 %all-to-all-done.1 = f32[128,1,128]{2,1,0:T(1,128)S(1)} async-done(((f32[128,1,128]{2,1,0:T(1,128)}), f32[128,1,128]{2,1,0:T(1,128)S(1)}, u32[]{:S(2)}, u32[]{:S(2)}) %all-to-all-start.1) | async-done | bytes 65568 | tf_op jit(solution)/shard_map/all_to_all | solution.py:589
  120.3 0.0 collective-permute-done.10.next_ref
  120.3 0.0 collective-permute-done.9.prev_ref
  120.3 0.6 copy-done.3
  120.9 0.1 copy-done.9
  121.0 21.2 %second_conv.1 = (bf16[12,2,64,640]{3,2,1,0:T(8,128)(2,1)}, f32[128,128]{1,0:T(8,128)}) custom-call(s32[1]{0:T(128)} %bitcast.part_ref, f32[4]{0:T(128)} %reshape.67.coef_ref, f32[128,128]{1,0:T(8,128)} %bitcast.34, f32[640,128]{1,0:T(8,128)} %pad.4.par_ref, bf16[2,128,128]{2,1,0:T(8,128)(2,1)} %constant.47.clone.pick_ref, ...), custom_call_target="tpu_custom_call" | custom-call | flops 11324620800 | bytes 20000000 | tf_op jit(solution)/shard_map/second_conv/pallas_call | solution.py:546
  142.3 14.3 %all_to_all.15 = f32[128,1,128]{2,1,0:T(1,128)S(1)} all-to-all(f32[128,1,128]{2,1,0:T(1,128)} %bitcast.36), channel_id=1, replica_groups=mesh['lon'=16,'ch'=8] {'lon','ch'}, dimensions={0} | all-to-all | bytes 131072 | tf_op jit(solution)/shard_map/all_to_all | solution.py:589
  156.6 0.2 reduce_sum.9
  156.7 0.6 subtract_add_fusion
  (15 shorter events, 0.1 us)
Async XLA Ops:
  0.6 41.2 %copy-start = (f32[1280,640]{1,0:T(8,128)S(1)}, f32[1280,640]{1,0:T(8,128)}, u32[]{:S(2)}) copy-start(f32[1280,640]{1,0:T(8,128)} %param.22) | copy-start | bytes 9830404
  3.6 3.7 %collective-permute-start.2 = (f32[1,128]{1,0:T(1,128)}, f32[1,128]{1,0:T(1,128)S(1)}, u32[]{:S(2)}, u32[]{:S(2)}) collective-permute-start(f32[1,128]{1,0:T(1,128)} %get-tuple-element.26), channel_id=1, source_target_pairs={{0,1},{1,0},{2,3},{3,2},{4,5},{5,4},{6,7},{7,6},{8,9},{9,8},{10,11... | collective-permute-start | bytes 1544 | tf_op jit(solution)/shard_map/ppermute | solution.py:608
  7.9 6.5 %collective-permute-start.3 = (f32[1,128]{1,0:T(1,128)S(1)}, f32[1,128]{1,0:T(1,128)S(1)}, u32[]{:S(2)}, u32[]{:S(2)}) collective-permute-start(f32[1,128]{1,0:T(1,128)S(1)} %add.62), channel_id=1, source_target_pairs={{0,2},{1,3},{2,0},{3,1},{4,6},{5,7},{6,4},{7,5},{8,10},{9,11},{10,... | collective-permute-start | bytes 1544 | tf_op jit(solution)/shard_map/ppermute | solution.py:608
  11.3 16.6 %collective-permute-start.1 = (bf16[2,2,80,96]{3,2,1,0:T(8,128)(2,1)}, bf16[2,2,80,96]{3,2,1,0:T(8,128)(2,1)S(1)}, u32[]{:S(2)}, u32[]{:S(2)}) collective-permute-start(bf16[2,2,80,96]{3,2,1,0:T(8,128)(2,1)} %get-tuple-element.23.first_ref), channel_id=1, source_target_pairs={{0,120},{8,0},{16,8},{24,16},{32,24},{40,32},{48,40},{56,48},{64,5... | collective-permute-start | bytes 184328 | tf_op jit(solution)/shard_map/ppermute | solution.py:630
  13.3 14.7 %collective-permute-start = (bf16[2,2,80,96]{3,2,1,0:T(8,128)(2,1)}, bf16[2,2,80,96]{3,2,1,0:T(8,128)(2,1)S(1)}, u32[]{:S(2)}, u32[]{:S(2)}) collective-permute-start(bf16[2,2,80,96]{3,2,1,0:T(8,128)(2,1)} %get-tuple-element.24.last_ref), channel_id=1, source_target_pairs={{0,8},{8,16},{16,24},{24,32},{32,40},{40,48},{48,56},{56,64},{64,7... | collective-permute-start | bytes 184328 | tf_op jit(solution)/shard_map/ppermute | solution.py:629
  14.4 9.6 %collective-permute-start.4 = (f32[1,128]{1,0:T(1,128)S(1)}, f32[1,128]{1,0:T(1,128)S(1)}, u32[]{:S(2)}, u32[]{:S(2)}) collective-permute-start(f32[1,128]{1,0:T(1,128)S(1)} %add.63), channel_id=1, source_target_pairs={{0,4},{1,5},{2,6},{3,7},{4,0},{5,1},{6,2},{7,3},{8,12},{9,13},{10,... | collective-permute-start | bytes 1544 | tf_op jit(solution)/shard_map/ppermute | solution.py:608
  24.0 4.0 %collective-permute-start.5 = (f32[1,128]{1,0:T(1,128)S(1)}, f32[1,128]{1,0:T(1,128)S(1)}, u32[]{:S(2)}, u32[]{:S(2)}) collective-permute-start(f32[1,128]{1,0:T(1,128)S(1)} %add.64), channel_id=1, source_target_pairs={{0,64},{8,72},{16,80},{24,88},{32,96},{40,104},{48,112},{56,120},{... | collective-permute-start | bytes 1544 | tf_op jit(solution)/shard_map/ppermute | solution.py:608
  27.9 0.6 copy-start.1
  28.6 0.6 copy-start.2
  31.5 4.6 %copy-start.7 = (s32[2]{0:T(128)S(1)}, s32[2]{0:T(128)}, u32[]{:S(2)}) copy-start(s32[2]{0:T(128)} %param.15) | copy-start | bytes 28
  31.6 4.6 %copy-start.8 = (s32[2]{0:T(128)S(1)}, s32[2]{0:T(128)}, u32[]{:S(2)}) copy-start(s32[2]{0:T(128)} %param.16) | copy-start | bytes 28
  31.6 4.8 %copy-start.6 = (f32[2,640]{1,0:T(2,128)S(1)}, f32[2,640]{1,0:T(2,128)}, u32[]{:S(2)}) copy-start(f32[2,640]{1,0:T(2,128)} %param.19) | copy-start | bytes 15364
  31.6 36.3 %all-to-all-start = ((bf16[8,16,80,128]{3,2,1,0:T(8,128)(2,1)}), bf16[8,16,80,128]{3,2,1,0:T(8,128)(2,1)}, u32[]{:S(2)}, u32[]{:S(2)}) async-start(bf16[8,16,80,128]{3,2,1,0:T(8,128)(2,1)} %pack_halo.1), calls=%async_computation | async-start | bytes 5242880 | tf_op jit(solution)/shard_map/all_to_all | solution.py:599
  36.1 7.4 %copy-start.4 = (f32[2,640]{1,0:T(2,128)S(1)}, f32[2,640]{1,0:T(2,128)}, u32[]{:S(2)}) copy-start(f32[2,640]{1,0:T(2,128)} %param.18) | copy-start | bytes 15364
  36.2 7.3 %copy-start.5 = (f32[2,640]{1,0:T(2,128)S(1)}, f32[2,640]{1,0:T(2,128)}, u32[]{:S(2)}) copy-start(f32[2,640]{1,0:T(2,128)} %param.20) | copy-start | bytes 15364
  36.4 13.5 %collective-permute-start.6 = (f32[1,128]{1,0:T(1,128)S(1)}, f32[1,128]{1,0:T(1,128)S(1)}, u32[]{:S(2)}, u32[]{:S(2)}) collective-permute-start(f32[1,128]{1,0:T(1,128)S(1)} %add.65), channel_id=1, source_target_pairs={{0,8},{8,0},{16,24},{24,16},{32,40},{40,32},{48,56},{56,48},{64,72... | collective-permute-start | bytes 1544 | tf_op jit(solution)/shard_map/ppermute | solution.py:608
  49.9 10.7 %collective-permute-start.7 = (f32[1,128]{1,0:T(1,128)S(1)}, f32[1,128]{1,0:T(1,128)S(1)}, u32[]{:S(2)}, u32[]{:S(2)}) collective-permute-start(f32[1,128]{1,0:T(1,128)S(1)} %add.66), channel_id=1, source_target_pairs={{0,16},{8,24},{16,0},{24,8},{32,48},{40,56},{48,32},{56,40},{64,80... | collective-permute-start | bytes 1544 | tf_op jit(solution)/shard_map/ppermute | solution.py:608
  60.7 5.2 %collective-permute-start.8 = (f32[1,128]{1,0:T(1,128)S(1)}, f32[1,128]{1,0:T(1,128)S(1)}, u32[]{:S(2)}, u32[]{:S(2)}) collective-permute-start(f32[1,128]{1,0:T(1,128)S(1)} %add.67), channel_id=1, source_target_pairs={{0,32},{8,40},{16,48},{24,56},{32,0},{40,8},{48,16},{56,24},{64,96... | collective-permute-start | bytes 1544 | tf_op jit(solution)/shard_map/ppermute | solution.py:608
  92.2 28.1 %collective-permute-start.10 = (bf16[640,128]{1,0:T(8,128)(2,1)}, bf16[640,128]{1,0:T(8,128)(2,1)S(1)}, u32[]{:S(2)}, u32[]{:S(2)}) collective-permute-start(bf16[640,128]{1,0:T(8,128)(2,1)} %get-tuple-element.38), channel_id=1, source_target_pairs={{1,0},{2,1},{3,2},{4,3},{5,4},{6,5},{7,6},{9,8},{10,9},{11,10},{12... | collective-permute-start | bytes 491528 | tf_op jit(solution)/shard_map/ppermute | solution.py:663
  93.5 26.8 %collective-permute-start.9 = (bf16[640,128]{1,0:T(8,128)(2,1)}, bf16[640,128]{1,0:T(8,128)(2,1)}, u32[]{:S(2)}, u32[]{:S(2)}) collective-permute-start(bf16[640,128]{1,0:T(8,128)(2,1)} %get-tuple-element.37), channel_id=1, source_target_pairs={{0,1},{1,2},{2,3},{3,4},{4,5},{5,6},{6,7},{8,9},{9,10},{10,11},{11... | collective-permute-start | bytes 491528 | tf_op jit(solution)/shard_map/ppermute | solution.py:662
  98.2 22.1 %all-to-all-start.1 = ((f32[128,1,128]{2,1,0:T(1,128)}), f32[128,1,128]{2,1,0:T(1,128)S(1)}, u32[]{:S(2)}, u32[]{:S(2)}) async-start(f32[128,1,128]{2,1,0:T(1,128)} %bitcast.35), calls=%async_computation.1 | async-start | bytes 131072 | tf_op jit(solution)/shard_map/all_to_all | solution.py:589
  120.3 0.6 copy-start.3
  120.3 0.7 copy-start.9
where the time goes:
time: 158 us; the launch traced here: 157 us
  Pallas kernels  75.6 us (48%)
  starting transfers between devices  42.3 us (27%)
  blocking collectives  14.3 us (9%)
  waiting for transfers between devices  12.7 us (8%)
  local copies, waits for them, and re-layouts  5.34 us (3%)
  matrix products  3.93 us (2%)
  other arithmetic  2.24 us (1%)
    pallas_call x1, Pallas kernels, first_conv(): pl.pallas_call(first_kernel, in_specs=[SMEM] + [VMEM] * 4 + [ANY] * 2, ou...  24.3 us
    pallas_call x1, Pallas kernels, second_conv(): pl.pallas_call(second_kernel, in_specs=[SMEM, SMEM] + [VMEM] * 6 + [ANY]...  21.2 us
    ppermute x7, starting transfers between devices, add_partner(): return x + lax.ppermute(x, axis, [(i, i ^ step) for i in range(size)])  16.3 us
    all_to_all x1, blocking collectives, everywhere(): got = lax.all_to_all(rows.reshape(-1, 1, 128), axes, 0, 0, tiled=True)  14.3 us
    pallas_call x2, Pallas kernels, turn_weights(): pl.pallas_call(functools.partial(weight_kernel, j), in_specs=[ANY], out_s...  12.7 us
    all_to_all x1, starting transfers between devices, everywhere(): got = lax.all_to_all(rows.reshape(-1, 1, 128), axes, 0, 0, tiled=True)  12.5 us
    all_to_all x1, waiting for transfers between devices, everywhere(): got = lax.all_to_all(rows.reshape(-1, 1, 128), axes, 0, 0, tiled=True)  8.85 us
    pallas_call x1, Pallas kernels, pack(): pl.pallas_call(pack_kernel, in_specs=[ANY], out_specs=ANY, out_shape=jax....  8.28 us
  transfers between devices with their start and end apart: 13, of which 4 were waited for; matrix products, arithmetic and copies ran while one was open for 5% of the time, Pallas kernels for 16%

commit v1 on v0

--- a/solution.py
+++ b/solution.py
@@ -25,6 +25,7 @@
 ANY = pl.BlockSpec(memory_space=pl.ANY)
 CHUNK = 16
 LIMIT = 56 * 2**20
+SUMS = 96
 
 
 def roll(x, by):
@@ -79,7 +80,7 @@
 PARAMS = pltpu.CompilerParams(vmem_limit_bytes=LIMIT)
 
 
-def sums_kernel(part_ref, cells_hbm, sums_ref, first_ref, last_ref, x, sems):
+def sums_kernel(cells_hbm, sums_ref, first_ref, last_ref, x, sems):
     half = COLS // 2
     copies = []
     for s in range(2):
@@ -106,27 +107,27 @@
             total, square = lax.fori_loop(0, half // 4, add, (total, square))
         for k, acc in enumerate((total, square)):
             column = jnp.sum(acc, axis=1, keepdims=True)
-            own = members(PART, part_ref[0] * PART, 64 * k + 32 * s)
+            own = members(PART, 0, 64 * k + 32 * s)
             row += jnp.sum(jnp.where(own, column, 0.0), axis=0, keepdims=True)
         first_ref[s] = x[s, 0:2]
         last_ref[s] = x[s, COLS - 2 : COLS]
-    sums_ref[...] = row
-
-
-def local_sums(part, cells):
+    sums_ref[...] = jnp.broadcast_to(row, sums_ref.shape)
+
+
+def local_sums(cells):
     return pl.pallas_call(
         sums_kernel,
-        in_specs=[SMEM, ANY],
+        in_specs=[ANY],
         out_specs=[VMEM] * 3,
         out_shape=[
-            jax.ShapeDtypeStruct((1, 128), F32),
+            jax.ShapeDtypeStruct((16, 128), F32),
             jax.ShapeDtypeStruct((2, 2, PART, LAT), BF16),
             jax.ShapeDtypeStruct((2, 2, PART, LAT), BF16),
         ],
         scratch_shapes=[pltpu.VMEM((2, COLS, PART, LAT), BF16), pltpu.SemaphoreType.DMA((4,))],
         compiler_params=PARAMS,
         name="local_sums",
-    )(part, cells)
+    )(cells)
 
 
 def pack_kernel(cells_hbm, pay_hbm, x, out, taken, turned, sems):
@@ -192,17 +193,26 @@
     )(cells)
 
 
-def halo_kernel(first_ref, last_ref, left_ref, right_ref, _, pay_hbm, out, sems):
+def halo_kernel(sums_ref, first_ref, last_ref, left_ref, right_ref, _, pay_hbm, out, sems):
     lane = lanes(PART)
     pad = jnp.zeros((PART, 128 - LAT), F32)
+    row = jnp.sum(sums_ref[...], axis=0, keepdims=True)
 
     @pl.loop(0, 2)
     def _(s):
         near = [left_ref[s, 0], left_ref[s, 1], first_ref[s, 0], last_ref[s, 1],
                 right_ref[s, 0], right_ref[s, 1]]
         near = [jnp.concatenate([col.astype(F32), pad], axis=1) for col in near]
+        carried = jnp.zeros((PART, 128), F32)
+        for k in range(2):
+            own = members(PART, 0, 64 * k + 32 * s)
+            value = jnp.sum(jnp.where(own, row, 0.0), axis=1, keepdims=True)
+            for piece in range(3):
+                part = value.astype(BF16).astype(F32)
+                carried = jnp.where(lane == SUMS + 3 * k + piece, part, carried)
+                value = value - part
         for d in range(SRC):
-            halo = jnp.zeros((PART, 128), F32)
+            halo = carried
             for kind in range(6):
                 own = (lane >= 16 * kind) & (lane < 16 * kind + 16)
                 halo = jnp.where(own, roll(near[kind], 16 * kind + 2 - d * ROWS), halo)
@@ -213,20 +223,20 @@
         pltpu.make_async_copy(out.at[s], pay_hbm.at[:, 8 * s + 7], sems.at[s]).wait()
 
 
-def pack_halo(first, last, left, right, pay):
+def pack_halo(sums, first, last, left, right, pay):
     return pl.pallas_call(
         halo_kernel,
-        in_specs=[VMEM] * 4 + [ANY],
+        in_specs=[VMEM] * 5 + [ANY],
         out_specs=ANY,
         out_shape=jax.ShapeDtypeStruct((SRC, 16, PART, 128), BF16),
         scratch_shapes=[
             pltpu.VMEM((2, SRC, PART, 128), BF16),
             pltpu.SemaphoreType.DMA((2,)),
         ],
-        input_output_aliases={4: 0},
+        input_output_aliases={5: 0},
         compiler_params=PARAMS,
         name="pack_halo",
-    )(first, last, left, right, pay)
+    )(sums, first, last, left, right, pay)
 
 
 def weight_kernel(j, w_hbm, o_hbm, x, out, sems):
@@ -295,15 +305,10 @@
     )(target)
 
 
-def affine(row, par_ref, s, j, scale, offset):
+def affine(total, square, par_ref, j, scale, offset):
     count = float(LAT * 1024 * WIDTH)
-
-    def of_channel(base):
-        picked = jnp.where(members(C, 0, base), row, 0.0)
-        return jnp.sum(picked, axis=1, keepdims=True) / count
-
-    mean = of_channel(32 * s)
-    spread = of_channel(64 + 32 * s) - mean * mean
+    mean = total / count
+    spread = square / count - mean * mean
     factor = lax.rsqrt(spread + 1e-05) * par_ref[:, 2 * j : 2 * j + 1]
     rest = par_ref[:, 2 * j + 1 : 2 * j + 2] - mean * factor
     scale[...] = jnp.broadcast_to(factor, scale.shape)
@@ -341,7 +346,7 @@
 
 
 def first_kernel(
-    part_ref, sums_ref, par_ref, pick_ref, taps_ref, recv_hbm, w_hbm,
+    part_ref, par_ref, pick_ref, taps_ref, recv_hbm, w_hbm,
     hid_hbm, out_sums, to_next, to_prev, out_halo,
     xs, wv, scale, offset, recv, hid, sides, xh, sems,
 ):
@@ -360,10 +365,16 @@
 
     def columns(s):
         fetches[s].wait()
-        affine(sums_ref[...], par_ref, s, 0, scale.at[s], offset.at[s])
+        tile = recv[s, :, 7].reshape(C, 128).astype(F32)
+        total, square = (
+            jnp.sum(jnp.where((lane >= at) & (lane < at + 3), tile, 0.0), axis=1, keepdims=True)
+            for at in (SUMS, SUMS + 3)
+        )
+        affine(total, square, par_ref, 0, scale.at[s], offset.at[s])
         r = (lane & 15) - 2
-        outside = ((part == 0) & (r < 0)) | ((part == SRC - 1) & (r >= ROWS))
-        x = act(recv[s, :, 7].reshape(C, 128), scale[s], offset[s])
+        unused = lane >= SUMS
+        outside = ((part == 0) & (r < 0)) | ((part == SRC - 1) & (r >= ROWS)) | unused
+        x = act(jnp.where(unused, 0.0, tile), scale[s], offset[s])
         halo = jnp.where(outside, 0.0, x).astype(BF16)
         sides[s] = jnp.dot(halo, pick_ref[...], preferred_element_type=F32)
         return halo
@@ -427,11 +438,11 @@
         store.wait()
 
 
-def first_conv(part, sums, params, pick, taps, recv, weights):
+def first_conv(part, params, pick, taps, recv, weights):
     tile = jax.ShapeDtypeStruct((C, 128), BF16)
     return pl.pallas_call(
         first_kernel,
-        in_specs=[SMEM] + [VMEM] * 4 + [ANY] * 2,
+        in_specs=[SMEM] + [VMEM] * 3 + [ANY] * 2,
         out_specs=[ANY] + [VMEM] * 4,
         out_shape=[
             jax.ShapeDtypeStruct((2, C, 768), F32),
@@ -454,7 +465,7 @@
             flops=4 * 768 * C * C * 9, bytes_accessed=20_000_000, transcendentals=0
         ),
         name="first_conv",
-    )(part, sums, params, pick, taps, recv, weights)
+    )(part, params, pick, taps, recv, weights)
 
 
 def second_kernel(
@@ -477,7 +488,11 @@
     low = lanes(PART) < 64
 
     def columns(s):
-        affine(row, par_ref, s, 1, scale.at[s], offset.at[s])
+        total, square = (
+            jnp.sum(jnp.where(members(C, 0, base), row, 0.0), axis=1, keepdims=True)
+            for base in (32 * s, 64 + 32 * s)
+        )
+        affine(total, square, par_ref, 1, scale.at[s], offset.at[s])
         halo = silu(near_ref[...].astype(F32) * scale[s] + offset[s]).astype(BF16)
         sides[s] = jnp.dot(halo, pick_ref[s], preferred_element_type=F32)
         fetches[s].wait()
@@ -603,11 +618,6 @@
     return lax.optimization_barrier((value,) + others)[0]
 
 
-def add_partner(x, axis, step):
-    size = lax.axis_size(axis)
-    return x + lax.ppermute(x, axis, [(i, i ^ step) for i in range(size)])
-
-
 def body(
     latents, next_latents, timesteps, resume_steps, conv_weights, conv_bias,
     norm_gain, norm_shift, time_w1, time_w2,
@@ -625,18 +635,13 @@
     tap_pick = jnp.asarray(halo_taps())
 
     cells = latents.transpose(1, 2, 3, 0)
-    sums, first, last = local_sums(part, cells)
+    sums, first, last = local_sums(cells)
+    sums = everywhere(sums, "lon")
     left = lax.ppermute(last, "lon", ring("lon", 1, True))
     right = lax.ppermute(first, "lon", ring("lon", -1, True))
-    for step in (1, 2, 4):
-        sums = add_partner(sums, "ch", step)
     pay = pack(after(cells, first))
-    sums = add_partner(after(sums, pay), "lon", 8)
-    pay = pack_halo(first, last, left, right, pay)
-    pay, sums = lax.optimization_barrier((pay, sums))
+    pay = pack_halo(sums, first, last, left, right, pay)
     recv = swap(pay, "ch")
-    for step in (1, 2, 4):
-        sums = add_partner(sums, "lon", step)
     conv_weights, time_w1, following = after((conv_weights, time_w1, next_latents), pay)
     turned = [turn_weights(j, conv_weights) for j in range(2)]
     target = turn_target(following)
@@ -657,7 +662,7 @@
 
     recv, turned, target = lax.optimization_barrier((recv, turned, target))
     hidden, sums, to_next, to_prev, near = first_conv(
-        part, sums, params, first_pick, tap_pick, recv, turned[0]
+        part, params, first_pick, tap_pick, recv, turned[0]
     )
     from_prev = lax.ppermute(to_next, "ch", ring("ch", 1, False))
     from_next = lax.ppermute(to_prev, "ch", ring("ch", -1, False))

time: 158 us -> 152 us (0.962)
  starting transfers between devices: 42.3 us -> 33.7 us
  waiting for transfers between devices: 12.7 us -> 19.1 us
    ppermute x7 -> x0, starting transfers between devices: 16.3 us -> none  [add_partner(): return x + lax.ppermute(x, axis, [(i, i ^ step) for i in range(size)])]
    all_to_all x1 -> x2, starting transfers between devices: 12.5 us -> 22.3 us  [everywhere(): got = lax.all_to_all(rows.reshape(-1, 1, 128), axes, 0, 0, tiled=True)]
    all_to_all x1, waiting for transfers between devices: 1.42 us -> 10.3 us  [swap(): return lax.all_to_all(array, axis, split_axis=0, concat_axis=0, tiled=True)]
    ppermute x1, starting transfers between devices: 4.65 us -> 2.03 us  [body(): from_prev = lax.ppermute(to_next, 'ch', ring('ch', 1, False))]
    ppermute x7 -> x0, waiting for transfers between devices: 2.43 us -> none  [add_partner(): return x + lax.ppermute(x, axis, [(i, i ^ step) for i in range(size)])]
    all_to_all x1 -> x2, waiting for transfers between devices: 8.85 us -> 8.82 us  [everywhere(): got = lax.all_to_all(rows.reshape(-1, 1, 128), axes, 0, 0, tiled=True)]
  transfers between devices with their start and end apart: 13 -> 7, of which waited for: 4 -> 2; matrix products, arithmetic and copies ran while one was open for 5% -> 4% of each run, Pallas kernels for 16% -> 16%
where the time goes in v1:
time: 152 us
  Pallas kernels  75.7 us (50%)
  starting transfers between devices  33.7 us (22%)
  waiting for transfers between devices  19.1 us (13%)
  blocking collectives  14.1 us (9%)
  local copies, waits for them, and re-layouts  4.83 us (3%)
  matrix products  2.51 us (2%)
    pallas_call x1, Pallas kernels, first_conv(): pl.pallas_call(first_kernel, in_specs=[SMEM] + [VMEM] * 3 + [ANY] * 2, ou...  24.3 us
    all_to_all x2, starting transfers between devices, everywhere(): got = lax.all_to_all(rows.reshape(-1, 1, 128), axes, 0, 0, tiled=True)  22.3 us
    pallas_call x1, Pallas kernels, second_conv(): pl.pallas_call(second_kernel, in_specs=[SMEM, SMEM] + [VMEM] * 6 + [ANY]...  21.2 us
    all_to_all x1, blocking collectives, everywhere(): got = lax.all_to_all(rows.reshape(-1, 1, 128), axes, 0, 0, tiled=True)  14.1 us
    pallas_call x2, Pallas kernels, turn_weights(): pl.pallas_call(functools.partial(weight_kernel, j), in_specs=[ANY], out_s...  12.7 us
    all_to_all x1, waiting for transfers between devices, swap(): return lax.all_to_all(array, axis, split_axis=0, concat_axis=0, tiled=True)  10.3 us
    all_to_all x2, waiting for transfers between devices, everywhere(): got = lax.all_to_all(rows.reshape(-1, 1, 128), axes, 0, 0, tiled=True)  8.82 us
    pallas_call x1, Pallas kernels, pack(): pl.pallas_call(pack_kernel, in_specs=[ANY], out_specs=ANY, out_shape=jax....  8.29 us
  transfers between devices with their start and end apart: 7, of which 2 were waited for; matrix products, arithmetic and copies ran while one was open for 4% of the time, Pallas kernels for 16%

profile of v1, /device:TPU:1, one launch (start us, length us, event | category | flops | bytes accessed | tf_op | source)
XLA Modules:
  0.0 151.9 jit_solution(14365189866344681641)
XLA Ops:
  0.6 0.0 copy-start
  0.6 2.9 %local_sums.1 = (f32[16,128]{1,0:T(8,128)}, bf16[2,2,80,96]{3,2,1,0:T(8,128)(2,1)}, bf16[2,2,80,96]{3,2,1,0:T(8,128)(2,1)}) custom-call(bf16[2,64,80,96]{3,2,1,0:T(8,128)(2,1)} %bitcast.36), custom_call_target="tpu_custom_call" | custom-call | tf_op jit(solution)/shard_map/local_sums/pallas_call | solution.py:118
  3.6 1.5 collective-permute-start.1
  5.1 1.3 collective-permute-start
  6.3 10.3 %all-to-all-start = ((f32[16,1,128]{2,1,0:T(1,128)}), f32[16,1,128]{2,1,0:T(1,128)S(1)}, u32[]{:S(2)}, u32[]{:S(2)}) async-start(f32[16,1,128]{2,1,0:T(1,128)} %bitcast.42), calls=%async_computation | async-start | bytes 16384 | tf_op jit(solution)/shard_map/all_to_all | solution.py:604
  16.6 8.3 %pack_latents.1._ = bf16[8,16,80,128]{3,2,1,0:T(8,128)(2,1)} custom-call(bf16[2,64,80,96]{3,2,1,0:T(8,128)(2,1)} %bitcast.37), custom_call_target="tpu_custom_call" | custom-call | flops 1000000000 | bytes 8000000 | tf_op jit(solution)/shard_map/pack_latents/pallas_call | solution.py:176
  24.9 0.0 all-to-all-done
  24.9 0.0 copy-start.5
  24.9 0.0 collective-permute-done.1.right_ref
  25.0 0.0 copy-start.2
  25.0 0.0 collective-permute-done.left_ref
  25.0 0.0 copy-start.3
  25.0 0.5 copy-done.5
  25.5 0.1 copy-done.2
  25.6 0.0 copy-done.3
  25.6 2.4 %pack_halo.1 = bf16[8,16,80,128]{3,2,1,0:T(8,128)(2,1)} custom-call(f32[16,128]{1,0:T(8,128)} %bitcast.41, bf16[2,2,80,96]{3,2,1,0:T(8,128)(2,1)} %get-tuple-element.21.first_ref, bf16[2,2,80,96]{3,2,1,0:T(8,128)(2,1)} %get-tuple-element.22.last_ref, bf16[2,2,80,96]{3,2,1,0:T(8,128)(2,1)} %copy-done.3, ...), custom_call_target="tpu_custom_call", output_to_operand_aliasing={{}: (5, {})} | custom-call | tf_op jit(solution)/shard_map/pack_halo/pallas_call | solution.py:227
  28.1 0.0 copy-start.9
  28.1 0.0 copy-start.10
  28.1 0.0 copy-start.8
  28.1 5.3 %all-to-all-start.1 = ((bf16[8,16,80,128]{3,2,1,0:T(8,128)(2,1)}), bf16[8,16,80,128]{3,2,1,0:T(8,128)(2,1)}, u32[]{:S(2)}, u32[]{:S(2)}) async-start(bf16[8,16,80,128]{3,2,1,0:T(8,128)(2,1)} %pack_halo.1), calls=%async_computation.1 | async-start | bytes 5242880 | tf_op jit(solution)/shard_map/all_to_all | solution.py:614
  33.4 0.0 copy-done.9
  33.4 0.0 copy-start.1
  33.5 0.0 copy-done.10
  33.5 0.1 fusion.11
  33.5 0.1 multiply_cosine_fusion
  33.7 0.0 copy-done.8
  33.7 3.9 %turn_target.1.target_hbm = bf16[2,6,640,128]{3,2,1,0:T(8,128)(2,1)} custom-call(bf16[12,2,64,640]{3,2,1,0:T(8,128)(2,1)} %target_hbm), custom_call_target="tpu_custom_call" | custom-call | tf_op jit(solution)/shard_map/turn_target/pallas_call | solution.py:293
  37.5 0.0 copy-start.6
  37.6 0.0 copy-start.7
  37.6 0.0 copy-done.1
  37.6 0.8 fusion.5
  38.4 0.0 copy-done
  38.4 1.7 %fusion = f32[2,640]{1,0:T(2,128)S(1)} fusion(f32[1280,640]{1,0:T(8,128)S(1)} %copy-done, f32[2,1280]{1,0:T(2,128)S(1)} %fusion.5), kind=kOutput, calls=%fused_computation.1 | convolution fusion | flops 19671040 | bytes 3292160 | tf_op jit(solution)/shard_map/dot_general | solution.py:595
  40.1 0.0 copy-done.6
  40.1 0.0 copy-done.7
  40.2 0.9 copy.27
  41.1 1.7 %pad.4.par_ref = f32[640,128]{1,0:T(8,128)} pad(f32[640,7]{1,0:T(8,128)} %copy.27, f32[]{:T(128)} %constant.41.clone.1), padding=0_0x0_121 | pad | bytes 345604 | tf_op jit(solution)/shard_map/jit(_pad)/pad | solution.py:654
  42.8 6.3 %turn_weights_0.1.w_hbm = bf16[640,5760]{1,0:T(8,128)(2,1)} custom-call(bf16[2,9,640,640]{3,2,1,0:T(8,128)(2,1)} %bitcast.34), custom_call_target="tpu_custom_call" | custom-call | flops 1887436800 | bytes 15000000 | tf_op jit(solution)/shard_map/turn_weights_0/pallas_call | solution.py:259
  49.1 6.4 %turn_weights_1.1.w_hbm = bf16[640,5760]{1,0:T(8,128)(2,1)} custom-call(bf16[2,9,640,640]{3,2,1,0:T(8,128)(2,1)} %bitcast.35), custom_call_target="tpu_custom_call" | custom-call | flops 1887436800 | bytes 15000000 | tf_op jit(solution)/shard_map/turn_weights_1/pallas_call | solution.py:259
  55.5 10.3 %all-to-all-done.1.recv_hbm = bf16[8,16,80,128]{3,2,1,0:T(8,128)(2,1)} async-done(((bf16[8,16,80,128]{3,2,1,0:T(8,128)(2,1)}), bf16[8,16,80,128]{3,2,1,0:T(8,128)(2,1)}, u32[]{:S(2)}, u32[]{:S(2)}) %all-to-all-start.1) | async-done | bytes 2621472 | tf_op jit(solution)/shard_map/all_to_all | solution.py:614
  65.8 24.3 %first_conv.1 = (f32[2,640,768]{2,1,0:T(8,128)}, f32[128,128]{1,0:T(8,128)}, bf16[640,128]{1,0:T(8,128)(2,1)}, bf16[640,128]{1,0:T(8,128)(2,1)}, bf16[640,128]{1,0:T(8,128)(2,1)}) custom-call(s32[1]{0:T(128)} %bitcast.part_ref, f32[640,128]{1,0:T(8,128)} %pad.4.par_ref, bf16[128,128]{1,0:T(8,128)(2,1)} %constant.46.clone.pick_ref, ...), custom_call_target="tpu_custom_call" | custom-call | flops 11324620800 | bytes 20000000 | tf_op jit(solution)/shard_map/first_conv/pallas_call | solution.py:443
  90.1 2.0 %collective-permute-start.2 = (bf16[640,128]{1,0:T(8,128)(2,1)}, bf16[640,128]{1,0:T(8,128)(2,1)S(1)}, u32[]{:S(2)}, u32[]{:S(2)}) collective-permute-start(bf16[640,128]{1,0:T(8,128)(2,1)} %get-tuple-element.31), channel_id=1, source_target_pairs={{0,1},{1,2},{2,3},{3,4},{4,5},{5,6},{6,7},{8,9},{9,10},{10,11},{11... | collective-permute-start | bytes 491528 | tf_op jit(solution)/shard_map/ppermute | solution.py:667
  92.1 1.3 collective-permute-start.3
  93.4 0.1 subtract_bitcast_fusion
  93.5 12.0 %all-to-all-start.2 = ((f32[128,1,128]{2,1,0:T(1,128)}), f32[128,1,128]{2,1,0:T(1,128)S(1)}, u32[]{:S(2)}, u32[]{:S(2)}) async-start(f32[128,1,128]{2,1,0:T(1,128)} %bitcast.39), calls=%async_computation.2 | async-start | bytes 131072 | tf_op jit(solution)/shard_map/all_to_all | solution.py:604
  105.5 0.1 copy.25
  105.6 0.7 reshape.73.coef_ref
  106.3 8.8 %all-to-all-done.2 = f32[128,1,128]{2,1,0:T(1,128)S(1)} async-done(((f32[128,1,128]{2,1,0:T(1,128)}), f32[128,1,128]{2,1,0:T(1,128)S(1)}, u32[]{:S(2)}, u32[]{:S(2)}) %all-to-all-start.2) | async-done | bytes 65568 | tf_op jit(solution)/shard_map/all_to_all | solution.py:604
  115.1 0.0 copy-start.4
  115.1 0.0 collective-permute-done.2.prev_ref
  115.1 0.0 copy-start.11
  115.1 0.0 collective-permute-done.3.next_ref
  115.1 0.6 copy-done.4
  115.7 0.1 copy-done.11
  115.8 21.2 %second_conv.1 = (bf16[12,2,64,640]{3,2,1,0:T(8,128)(2,1)}, f32[128,128]{1,0:T(8,128)}) custom-call(s32[1]{0:T(128)} %bitcast.part_ref, f32[4]{0:T(128)} %reshape.73.coef_ref, f32[128,128]{1,0:T(8,128)} %bitcast.38, f32[640,128]{1,0:T(8,128)} %pad.4.par_ref, bf16[2,128,128]{2,1,0:T(8,128)(2,1)} %constant.47.clone.pick_ref, ...), custom_call_target="tpu_custom_call" | custom-call | flops 11324620800 | bytes 20000000 | tf_op jit(solution)/shard_map/second_conv/pallas_call | solution.py:561
  137.1 14.1 %all_to_all.20 = f32[128,1,128]{2,1,0:T(1,128)S(1)} all-to-all(f32[128,1,128]{2,1,0:T(1,128)} %bitcast.40), channel_id=1, replica_groups=mesh['lon'=16,'ch'=8] {'lon','ch'}, dimensions={0} | all-to-all | bytes 131072 | tf_op jit(solution)/shard_map/all_to_all | solution.py:604
  151.2 0.2 reduce_sum.9
  151.3 0.6 subtract_add_fusion
  (6 shorter events, 0.1 us)
Async XLA Ops:
  0.6 37.8 %copy-start = (f32[1280,640]{1,0:T(8,128)S(1)}, f32[1280,640]{1,0:T(8,128)}, u32[]{:S(2)}) copy-start(f32[1280,640]{1,0:T(8,128)} %param.22) | copy-start | bytes 9830404
  3.6 21.4 %collective-permute-start.1 = (bf16[2,2,80,96]{3,2,1,0:T(8,128)(2,1)}, bf16[2,2,80,96]{3,2,1,0:T(8,128)(2,1)S(1)}, u32[]{:S(2)}, u32[]{:S(2)}) collective-permute-start(bf16[2,2,80,96]{3,2,1,0:T(8,128)(2,1)} %get-tuple-element.21.first_ref), channel_id=1, source_target_pairs={{0,120},{8,0},{16,8},{24,16},{32,24},{40,32},{48,40},{56,48},{64,5... | collective-permute-start | bytes 184328 | tf_op jit(solution)/shard_map/ppermute | solution.py:641
  5.1 19.9 %collective-permute-start = (bf16[2,2,80,96]{3,2,1,0:T(8,128)(2,1)}, bf16[2,2,80,96]{3,2,1,0:T(8,128)(2,1)S(1)}, u32[]{:S(2)}, u32[]{:S(2)}) collective-permute-start(bf16[2,2,80,96]{3,2,1,0:T(8,128)(2,1)} %get-tuple-element.22.last_ref), channel_id=1, source_target_pairs={{0,8},{8,16},{16,24},{24,32},{32,40},{40,48},{48,56},{56,64},{64,7... | collective-permute-start | bytes 184328 | tf_op jit(solution)/shard_map/ppermute | solution.py:640
  6.3 18.6 %all-to-all-start = ((f32[16,1,128]{2,1,0:T(1,128)}), f32[16,1,128]{2,1,0:T(1,128)S(1)}, u32[]{:S(2)}, u32[]{:S(2)}) async-start(f32[16,1,128]{2,1,0:T(1,128)} %bitcast.42), calls=%async_computation | async-start | bytes 16384 | tf_op jit(solution)/shard_map/all_to_all | solution.py:604
  24.9 0.6 copy-start.5
  25.0 0.6 copy-start.2
  25.0 0.7 copy-start.3
  28.1 5.4 %copy-start.9 = (s32[2]{0:T(128)S(1)}, s32[2]{0:T(128)}, u32[]{:S(2)}) copy-start(s32[2]{0:T(128)} %param.15) | copy-start | bytes 28
  28.1 5.4 %copy-start.10 = (s32[2]{0:T(128)S(1)}, s32[2]{0:T(128)}, u32[]{:S(2)}) copy-start(s32[2]{0:T(128)} %param.16) | copy-start | bytes 28
  28.1 5.6 %copy-start.8 = (f32[2,640]{1,0:T(2,128)S(1)}, f32[2,640]{1,0:T(2,128)}, u32[]{:S(2)}) copy-start(f32[2,640]{1,0:T(2,128)} %param.19) | copy-start | bytes 15364
  28.1 37.7 %all-to-all-start.1 = ((bf16[8,16,80,128]{3,2,1,0:T(8,128)(2,1)}), bf16[8,16,80,128]{3,2,1,0:T(8,128)(2,1)}, u32[]{:S(2)}, u32[]{:S(2)}) async-start(bf16[8,16,80,128]{3,2,1,0:T(8,128)(2,1)} %pack_halo.1), calls=%async_computation.1 | async-start | bytes 5242880 | tf_op jit(solution)/shard_map/all_to_all | solution.py:614
  33.4 4.1 %copy-start.1 = (f32[320,1280]{1,0:T(8,128)S(1)}, f32[320,1280]{1,0:T(8,128)}, u32[]{:S(2)}) copy-start(f32[320,1280]{1,0:T(8,128)} %param.21) | copy-start | bytes 4915204
  37.5 2.5 %copy-start.6 = (f32[2,640]{1,0:T(2,128)S(1)}, f32[2,640]{1,0:T(2,128)}, u32[]{:S(2)}) copy-start(f32[2,640]{1,0:T(2,128)} %param.18) | copy-start | bytes 15364
  37.6 2.5 %copy-start.7 = (f32[2,640]{1,0:T(2,128)S(1)}, f32[2,640]{1,0:T(2,128)}, u32[]{:S(2)}) copy-start(f32[2,640]{1,0:T(2,128)} %param.20) | copy-start | bytes 15364
  90.1 25.0 %collective-permute-start.2 = (bf16[640,128]{1,0:T(8,128)(2,1)}, bf16[640,128]{1,0:T(8,128)(2,1)S(1)}, u32[]{:S(2)}, u32[]{:S(2)}) collective-permute-start(bf16[640,128]{1,0:T(8,128)(2,1)} %get-tuple-element.31), channel_id=1, source_target_pairs={{0,1},{1,2},{2,3},{3,4},{4,5},{5,6},{6,7},{8,9},{9,10},{10,11},{11... | collective-permute-start | bytes 491528 | tf_op jit(solution)/shard_map/ppermute | solution.py:667
  92.1 23.0 %collective-permute-start.3 = (bf16[640,128]{1,0:T(8,128)(2,1)}, bf16[640,128]{1,0:T(8,128)(2,1)}, u32[]{:S(2)}, u32[]{:S(2)}) collective-permute-start(bf16[640,128]{1,0:T(8,128)(2,1)} %get-tuple-element.32), channel_id=1, source_target_pairs={{1,0},{2,1},{3,2},{4,3},{5,4},{6,5},{7,6},{9,8},{10,9},{11,10},{12... | collective-permute-start | bytes 491528 | tf_op jit(solution)/shard_map/ppermute | solution.py:668
  93.5 21.6 %all-to-all-start.2 = ((f32[128,1,128]{2,1,0:T(1,128)}), f32[128,1,128]{2,1,0:T(1,128)S(1)}, u32[]{:S(2)}, u32[]{:S(2)}) async-start(f32[128,1,128]{2,1,0:T(1,128)} %bitcast.39), calls=%async_computation.2 | async-start | bytes 131072 | tf_op jit(solution)/shard_map/all_to_all | solution.py:604
  115.1 0.6 copy-start.4
  115.1 0.7 copy-start.11

commit v2 on v1

--- a/solution.py
+++ b/solution.py
@@ -136,6 +136,7 @@
         copy.start()
     taken[...] = jnp.zeros_like(taken)
     turned[...] = jnp.zeros_like(turned)
+    low = lanes(8) < 64
     stores = [
         pltpu.make_async_copy(out.at[s], pay_hbm.at[:, 8 * s : 8 * s + 7], sems.at[2 + s])
         for s in range(2)
@@ -153,19 +154,21 @@
 
         own = pl.ds(pl.multiple_of(e * CHUNK, CHUNK), CHUNK)
         taken[:, 0:LAT] = x[s, :, own, :].astype(F32).reshape(COLS * CHUNK, LAT)
-        for j in range(CHUNK):
-            across = taken[pl.ds(j, COLS, stride=CHUNK), :].T
-            turned[pl.ds(CHUNK + j, LAT, stride=CHUNK), 0:COLS] = across[0:LAT, :]
-
-        def tile(r):
-            return turned[CHUNK * (r + 1) : CHUNK * (r + 2), :]
+        for j in range(8):
+            pair = [taken[pl.ds(j + 8 * h, COLS, stride=CHUNK), :] for h in range(2)]
+            turned[pl.ds(8 + j, LAT, stride=8), :] = jnp.concatenate(pair, axis=0).T[0:LAT, :]
+
+        def tile(upper, lower):
+            upper, lower = (turned[8 * (r + 1) : 8 * (r + 2), :] for r in (upper, lower))
+            halves = (jnp.where(low, upper, roll(lower, 64)), jnp.where(low, roll(upper, 64), lower))
+            return jnp.concatenate(halves, axis=0).astype(BF16)
 
         for d in range(SRC):
             for q in range(7):
                 upper, lower = (d * ROWS + q, d * ROWS + q + 6)
                 if q == 6:
                     upper, lower = (d * ROWS - 1, d * ROWS + ROWS)
-                out[s, d, q, own, :] = (tile(upper) + roll(tile(lower), 64)).astype(BF16)
+                out[s, d, q, own, :] = tile(upper, lower)
 
     stores[1].start()
     for store in stores:
@@ -182,7 +185,7 @@
             pltpu.VMEM((2, COLS, PART, LAT), BF16),
             pltpu.VMEM((2, SRC, 7, PART, 128), BF16),
             pltpu.VMEM((COLS * CHUNK, 128), F32),
-            pltpu.VMEM(((LAT + 8) * CHUNK, 128), F32),
+            pltpu.VMEM(((LAT + 8) * 8, 128), F32),
             pltpu.SemaphoreType.DMA((4,)),
         ],
         compiler_params=PARAMS,
@@ -391,6 +394,12 @@
     def _(b):
         prepare(0, b)
 
+    both = jnp.concatenate([halo, columns(1)], axis=1)
+    for k in range(3):
+        picked = jnp.dot(both, taps_ref[:, 128 * k : 128 * k + 128], preferred_element_type=F32)
+        for i in range(3):
+            t = 3 * i + k
+            xh[C * t : C * (t + 1), :] = roll(picked, -i).astype(BF16)
     weights.wait()
     stores = []
 
@@ -404,12 +413,6 @@
         stores.append(store)
 
     put(0, 0, product(wv, xs.at[0], 0))
-    both = jnp.concatenate([halo, columns(1)], axis=1)
-    for k in range(3):
-        picked = jnp.dot(both, taps_ref[:, 128 * k : 128 * k + 128], preferred_element_type=F32)
-        for i in range(3):
-            t = 3 * i + k
-            xh[C * t : C * (t + 1), :] = roll(picked, -i).astype(BF16)
     for n, blocks in ((256, (0, 1, 2, 3)), (512, (4, 5, 6, 7))):
         put(0, n, product(wv, xs.at[0], n))
         for b in blocks:

time: 152 us -> 149 us (0.980)
  Pallas kernels: 75.7 us -> 72.3 us
    pallas_call x1, Pallas kernels: 8.29 us -> 6.45 us  [pack(): pl.pallas_call(pack_kernel, in_specs=[ANY], out_specs=ANY, out_shape=jax....]
    pallas_call x1, Pallas kernels: 24.3 us -> 22.7 us  [first_conv(): pl.pallas_call(first_kernel, in_specs=[SMEM] + [VMEM] * 3 + [ANY] * 2, ou...]
  transfers between devices with their start and end apart: 7 -> 7, of which waited for: 2 -> 3; matrix products, arithmetic and copies ran while one was open for 4% -> 4% of each run, Pallas kernels for 16% -> 15%
where the time goes in v2:
time: 149 us; the launch traced here: 148 us
  Pallas kernels  72.3 us (49%)
  starting transfers between devices  33.1 us (22%)
  waiting for transfers between devices  19.7 us (13%)
  blocking collectives  14.1 us (9%)
  local copies, waits for them, and re-layouts  4.84 us (3%)
  matrix products  2.51 us (2%)
    pallas_call x1, Pallas kernels, first_conv(): pl.pallas_call(first_kernel, in_specs=[SMEM] + [VMEM] * 3 + [ANY] * 2, ou...  22.7 us
    all_to_all x2, starting transfers between devices, everywhere(): got = lax.all_to_all(rows.reshape(-1, 1, 128), axes, 0, 0, tiled=True)  22 us
    pallas_call x1, Pallas kernels, second_conv(): pl.pallas_call(second_kernel, in_specs=[SMEM, SMEM] + [VMEM] * 6 + [ANY]...  21.2 us
    all_to_all x1, blocking collectives, everywhere(): got = lax.all_to_all(rows.reshape(-1, 1, 128), axes, 0, 0, tiled=True)  14.1 us
    pallas_call x2, Pallas kernels, turn_weights(): pl.pallas_call(functools.partial(weight_kernel, j), in_specs=[ANY], out_s...  12.7 us
    all_to_all x1, waiting for transfers between devices, swap(): return lax.all_to_all(array, axis, split_axis=0, concat_axis=0, tiled=True)  10.4 us
    all_to_all x2, waiting for transfers between devices, everywhere(): got = lax.all_to_all(rows.reshape(-1, 1, 128), axes, 0, 0, tiled=True)  9.34 us
    pallas_call x1, Pallas kernels, pack(): pl.pallas_call(pack_kernel, in_specs=[ANY], out_specs=ANY, out_shape=jax....  6.45 us
  transfers between devices with their start and end apart: 7, of which 3 were waited for; matrix products, arithmetic and copies ran while one was open for 4% of the time, Pallas kernels for 15%

profile of v2, /device:TPU:1, one launch (start us, length us, event | category | flops | bytes accessed | tf_op | source)
XLA Modules:
  0.0 148.4 jit_solution(5362023000928129934)
XLA Ops:
  0.6 0.0 copy-start
  0.6 2.9 %local_sums.1 = (f32[16,128]{1,0:T(8,128)}, bf16[2,2,80,96]{3,2,1,0:T(8,128)(2,1)}, bf16[2,2,80,96]{3,2,1,0:T(8,128)(2,1)}) custom-call(bf16[2,64,80,96]{3,2,1,0:T(8,128)(2,1)} %bitcast.36), custom_call_target="tpu_custom_call" | custom-call | tf_op jit(solution)/shard_map/local_sums/pallas_call | solution.py:118
  3.6 1.5 %collective-permute-start.1 = (bf16[2,2,80,96]{3,2,1,0:T(8,128)(2,1)}, bf16[2,2,80,96]{3,2,1,0:T(8,128)(2,1)S(1)}, u32[]{:S(2)}, u32[]{:S(2)}) collective-permute-start(bf16[2,2,80,96]{3,2,1,0:T(8,128)(2,1)} %get-tuple-element.21.first_ref), channel_id=1, source_target_pairs={{0,120},{8,0},{16,8},{24,16},{32,24},{40,32},{48,40},{56,48},{64,5... | collective-permute-start | bytes 184328 | tf_op jit(solution)/shard_map/ppermute | solution.py:644
  5.1 1.3 collective-permute-start
  6.3 10.3 %all-to-all-start = ((f32[16,1,128]{2,1,0:T(1,128)}), f32[16,1,128]{2,1,0:T(1,128)S(1)}, u32[]{:S(2)}, u32[]{:S(2)}) async-start(f32[16,1,128]{2,1,0:T(1,128)} %bitcast.42), calls=%async_computation | async-start | bytes 16384 | tf_op jit(solution)/shard_map/all_to_all | solution.py:607
  16.6 6.4 %pack_latents.1._ = bf16[8,16,80,128]{3,2,1,0:T(8,128)(2,1)} custom-call(bf16[2,64,80,96]{3,2,1,0:T(8,128)(2,1)} %bitcast.37), custom_call_target="tpu_custom_call" | custom-call | flops 1000000000 | bytes 8000000 | tf_op jit(solution)/shard_map/pack_latents/pallas_call | solution.py:179
  23.1 0.5 all-to-all-done
  23.6 0.0 copy-start.5
  23.6 0.0 collective-permute-done.1.right_ref
  23.6 0.0 copy-start.2
  23.6 0.0 collective-permute-done.left_ref
  23.6 0.0 copy-start.3
  23.6 0.6 copy-done.5
  24.2 0.1 copy-done.2
  24.3 0.0 copy-done.3
  24.3 2.4 %pack_halo.1 = bf16[8,16,80,128]{3,2,1,0:T(8,128)(2,1)} custom-call(f32[16,128]{1,0:T(8,128)} %bitcast.41, bf16[2,2,80,96]{3,2,1,0:T(8,128)(2,1)} %get-tuple-element.21.first_ref, bf16[2,2,80,96]{3,2,1,0:T(8,128)(2,1)} %get-tuple-element.22.last_ref, bf16[2,2,80,96]{3,2,1,0:T(8,128)(2,1)} %copy-done.3, ...), custom_call_target="tpu_custom_call", output_to_operand_aliasing={{}: (5, {})} | custom-call | tf_op jit(solution)/shard_map/pack_halo/pallas_call | solution.py:230
  26.7 0.0 copy-start.9
  26.7 0.0 copy-start.10
  26.7 0.0 copy-start.8
  26.8 5.3 %all-to-all-start.1 = ((bf16[8,16,80,128]{3,2,1,0:T(8,128)(2,1)}), bf16[8,16,80,128]{3,2,1,0:T(8,128)(2,1)}, u32[]{:S(2)}, u32[]{:S(2)}) async-start(bf16[8,16,80,128]{3,2,1,0:T(8,128)(2,1)} %pack_halo.1), calls=%async_computation.1 | async-start | bytes 5242880 | tf_op jit(solution)/shard_map/all_to_all | solution.py:617
  32.1 0.0 copy-done.9
  32.1 0.0 copy-start.1
  32.1 0.0 copy-done.10
  32.1 0.1 fusion.11
  32.2 0.1 multiply_cosine_fusion
  32.3 0.0 copy-done.8
  32.3 3.9 %turn_target.1.target_hbm = bf16[2,6,640,128]{3,2,1,0:T(8,128)(2,1)} custom-call(bf16[12,2,64,640]{3,2,1,0:T(8,128)(2,1)} %target_hbm), custom_call_target="tpu_custom_call" | custom-call | tf_op jit(solution)/shard_map/turn_target/pallas_call | solution.py:296
  36.2 0.0 copy-start.6
  36.2 0.0 copy-start.7
  36.2 0.0 copy-done.1
  36.2 0.8 fusion.5
  37.0 0.0 copy-done
  37.0 1.7 %fusion = f32[2,640]{1,0:T(2,128)S(1)} fusion(f32[1280,640]{1,0:T(8,128)S(1)} %copy-done, f32[2,1280]{1,0:T(2,128)S(1)} %fusion.5), kind=kOutput, calls=%fused_computation.1 | convolution fusion | flops 19671040 | bytes 3292160 | tf_op jit(solution)/shard_map/dot_general | solution.py:598
  38.7 0.0 copy-done.6
  38.7 0.0 copy-done.7
  38.8 0.9 copy.27
  39.7 1.7 %pad.4.par_ref = f32[640,128]{1,0:T(8,128)} pad(f32[640,7]{1,0:T(8,128)} %copy.27, f32[]{:T(128)} %constant.41.clone.1), padding=0_0x0_121 | pad | bytes 345604 | tf_op jit(solution)/shard_map/jit(_pad)/pad | solution.py:657
  41.4 6.3 %turn_weights_0.1.w_hbm = bf16[640,5760]{1,0:T(8,128)(2,1)} custom-call(bf16[2,9,640,640]{3,2,1,0:T(8,128)(2,1)} %bitcast.34), custom_call_target="tpu_custom_call" | custom-call | flops 1887436800 | bytes 15000000 | tf_op jit(solution)/shard_map/turn_weights_0/pallas_call | solution.py:262
  47.8 6.4 %turn_weights_1.1.w_hbm = bf16[640,5760]{1,0:T(8,128)(2,1)} custom-call(bf16[2,9,640,640]{3,2,1,0:T(8,128)(2,1)} %bitcast.35), custom_call_target="tpu_custom_call" | custom-call | flops 1887436800 | bytes 15000000 | tf_op jit(solution)/shard_map/turn_weights_1/pallas_call | solution.py:262
  54.1 10.4 %all-to-all-done.1.recv_hbm = bf16[8,16,80,128]{3,2,1,0:T(8,128)(2,1)} async-done(((bf16[8,16,80,128]{3,2,1,0:T(8,128)(2,1)}), bf16[8,16,80,128]{3,2,1,0:T(8,128)(2,1)}, u32[]{:S(2)}, u32[]{:S(2)}) %all-to-all-start.1) | async-done | bytes 2621472 | tf_op jit(solution)/shard_map/all_to_all | solution.py:617
  64.5 22.7 %first_conv.1 = (f32[2,640,768]{2,1,0:T(8,128)}, f32[128,128]{1,0:T(8,128)}, bf16[640,128]{1,0:T(8,128)(2,1)}, bf16[640,128]{1,0:T(8,128)(2,1)}, bf16[640,128]{1,0:T(8,128)(2,1)}) custom-call(s32[1]{0:T(128)} %bitcast.part_ref, f32[640,128]{1,0:T(8,128)} %pad.4.par_ref, bf16[128,128]{1,0:T(8,128)(2,1)} %constant.46.clone.pick_ref, ...), custom_call_target="tpu_custom_call" | custom-call | flops 11324620800 | bytes 20000000 | tf_op jit(solution)/shard_map/first_conv/pallas_call | solution.py:446
  87.2 1.8 %collective-permute-start.2 = (bf16[640,128]{1,0:T(8,128)(2,1)}, bf16[640,128]{1,0:T(8,128)(2,1)S(1)}, u32[]{:S(2)}, u32[]{:S(2)}) collective-permute-start(bf16[640,128]{1,0:T(8,128)(2,1)} %get-tuple-element.31), channel_id=1, source_target_pairs={{0,1},{1,2},{2,3},{3,4},{4,5},{5,6},{6,7},{8,9},{9,10},{10,11},{11... | collective-permute-start | bytes 491528 | tf_op jit(solution)/shard_map/ppermute | solution.py:670
  89.0 1.3 collective-permute-start.3
  90.3 0.1 subtract_bitcast_fusion
  90.3 11.7 %all-to-all-start.2 = ((f32[128,1,128]{2,1,0:T(1,128)}), f32[128,1,128]{2,1,0:T(1,128)S(1)}, u32[]{:S(2)}, u32[]{:S(2)}) async-start(f32[128,1,128]{2,1,0:T(1,128)} %bitcast.39), calls=%async_computation.2 | async-start | bytes 131072 | tf_op jit(solution)/shard_map/all_to_all | solution.py:607
  102.1 0.1 copy.25
  102.2 0.7 reshape.73.coef_ref
  102.9 8.8 %all-to-all-done.2 = f32[128,1,128]{2,1,0:T(1,128)S(1)} async-done(((f32[128,1,128]{2,1,0:T(1,128)}), f32[128,1,128]{2,1,0:T(1,128)S(1)}, u32[]{:S(2)}, u32[]{:S(2)}) %all-to-all-start.2) | async-done | bytes 65568 | tf_op jit(solution)/shard_map/all_to_all | solution.py:607
  111.7 0.0 copy-start.4
  111.7 0.0 collective-permute-done.2.prev_ref
  111.7 0.0 copy-start.11
  111.7 0.0 collective-permute-done.3.next_ref
  111.7 0.6 copy-done.4
  112.3 0.1 copy-done.11
  112.4 21.2 %second_conv.1 = (bf16[12,2,64,640]{3,2,1,0:T(8,128)(2,1)}, f32[128,128]{1,0:T(8,128)}) custom-call(s32[1]{0:T(128)} %bitcast.part_ref, f32[4]{0:T(128)} %reshape.73.coef_ref, f32[128,128]{1,0:T(8,128)} %bitcast.38, f32[640,128]{1,0:T(8,128)} %pad.4.par_ref, bf16[2,128,128]{2,1,0:T(8,128)(2,1)} %constant.47.clone.pick_ref, ...), custom_call_target="tpu_custom_call" | custom-call | flops 11324620800 | bytes 20000000 | tf_op jit(solution)/shard_map/second_conv/pallas_call | solution.py:564
  133.6 14.1 %all_to_all.20 = f32[128,1,128]{2,1,0:T(1,128)S(1)} all-to-all(f32[128,1,128]{2,1,0:T(1,128)} %bitcast.40), channel_id=1, replica_groups=mesh['lon'=16,'ch'=8] {'lon','ch'}, dimensions={0} | all-to-all | bytes 131072 | tf_op jit(solution)/shard_map/all_to_all | solution.py:607
  147.7 0.2 reduce_sum.9
  147.9 0.6 subtract_add_fusion
  (6 shorter events, 0.1 us)
Async XLA Ops:
  0.6 36.4 %copy-start = (f32[1280,640]{1,0:T(8,128)S(1)}, f32[1280,640]{1,0:T(8,128)}, u32[]{:S(2)}) copy-start(f32[1280,640]{1,0:T(8,128)} %param.22) | copy-start | bytes 9830404
  3.6 20.0 %collective-permute-start.1 = (bf16[2,2,80,96]{3,2,1,0:T(8,128)(2,1)}, bf16[2,2,80,96]{3,2,1,0:T(8,128)(2,1)S(1)}, u32[]{:S(2)}, u32[]{:S(2)}) collective-permute-start(bf16[2,2,80,96]{3,2,1,0:T(8,128)(2,1)} %get-tuple-element.21.first_ref), channel_id=1, source_target_pairs={{0,120},{8,0},{16,8},{24,16},{32,24},{40,32},{48,40},{56,48},{64,5... | collective-permute-start | bytes 184328 | tf_op jit(solution)/shard_map/ppermute | solution.py:644
  5.1 18.6 %collective-permute-start = (bf16[2,2,80,96]{3,2,1,0:T(8,128)(2,1)}, bf16[2,2,80,96]{3,2,1,0:T(8,128)(2,1)S(1)}, u32[]{:S(2)}, u32[]{:S(2)}) collective-permute-start(bf16[2,2,80,96]{3,2,1,0:T(8,128)(2,1)} %get-tuple-element.22.last_ref), channel_id=1, source_target_pairs={{0,8},{8,16},{16,24},{24,32},{32,40},{40,48},{48,56},{56,64},{64,7... | collective-permute-start | bytes 184328 | tf_op jit(solution)/shard_map/ppermute | solution.py:643
  6.3 17.3 %all-to-all-start = ((f32[16,1,128]{2,1,0:T(1,128)}), f32[16,1,128]{2,1,0:T(1,128)S(1)}, u32[]{:S(2)}, u32[]{:S(2)}) async-start(f32[16,1,128]{2,1,0:T(1,128)} %bitcast.42), calls=%async_computation | async-start | bytes 16384 | tf_op jit(solution)/shard_map/all_to_all | solution.py:607
  23.6 0.6 copy-start.5
  23.6 0.6 copy-start.2
  23.6 0.7 copy-start.3
  26.7 5.3 %copy-start.9 = (s32[2]{0:T(128)S(1)}, s32[2]{0:T(128)}, u32[]{:S(2)}) copy-start(s32[2]{0:T(128)} %param.15) | copy-start | bytes 28
  26.7 5.4 %copy-start.10 = (s32[2]{0:T(128)S(1)}, s32[2]{0:T(128)}, u32[]{:S(2)}) copy-start(s32[2]{0:T(128)} %param.16) | copy-start | bytes 28
  26.7 5.5 %copy-start.8 = (f32[2,640]{1,0:T(2,128)S(1)}, f32[2,640]{1,0:T(2,128)}, u32[]{:S(2)}) copy-start(f32[2,640]{1,0:T(2,128)} %param.19) | copy-start | bytes 15364
  26.8 37.7 %all-to-all-start.1 = ((bf16[8,16,80,128]{3,2,1,0:T(8,128)(2,1)}), bf16[8,16,80,128]{3,2,1,0:T(8,128)(2,1)}, u32[]{:S(2)}, u32[]{:S(2)}) async-start(bf16[8,16,80,128]{3,2,1,0:T(8,128)(2,1)} %pack_halo.1), calls=%async_computation.1 | async-start | bytes 5242880 | tf_op jit(solution)/shard_map/all_to_all | solution.py:617
  32.1 4.1 %copy-start.1 = (f32[320,1280]{1,0:T(8,128)S(1)}, f32[320,1280]{1,0:T(8,128)}, u32[]{:S(2)}) copy-start(f32[320,1280]{1,0:T(8,128)} %param.21) | copy-start | bytes 4915204
  36.2 2.5 %copy-start.6 = (f32[2,640]{1,0:T(2,128)S(1)}, f32[2,640]{1,0:T(2,128)}, u32[]{:S(2)}) copy-start(f32[2,640]{1,0:T(2,128)} %param.18) | copy-start | bytes 15364
  36.2 2.5 %copy-start.7 = (f32[2,640]{1,0:T(2,128)S(1)}, f32[2,640]{1,0:T(2,128)}, u32[]{:S(2)}) copy-start(f32[2,640]{1,0:T(2,128)} %param.20) | copy-start | bytes 15364
  87.2 24.5 %collective-permute-start.2 = (bf16[640,128]{1,0:T(8,128)(2,1)}, bf16[640,128]{1,0:T(8,128)(2,1)S(1)}, u32[]{:S(2)}, u32[]{:S(2)}) collective-permute-start(bf16[640,128]{1,0:T(8,128)(2,1)} %get-tuple-element.31), channel_id=1, source_target_pairs={{0,1},{1,2},{2,3},{3,4},{4,5},{5,6},{6,7},{8,9},{9,10},{10,11},{11... | collective-permute-start | bytes 491528 | tf_op jit(solution)/shard_map/ppermute | solution.py:670
  89.0 22.7 %collective-permute-start.3 = (bf16[640,128]{1,0:T(8,128)(2,1)}, bf16[640,128]{1,0:T(8,128)(2,1)}, u32[]{:S(2)}, u32[]{:S(2)}) collective-permute-start(bf16[640,128]{1,0:T(8,128)(2,1)} %get-tuple-element.32), channel_id=1, source_target_pairs={{1,0},{2,1},{3,2},{4,3},{5,4},{6,5},{7,6},{9,8},{10,9},{11,10},{12... | collective-permute-start | bytes 491528 | tf_op jit(solution)/shard_map/ppermute | solution.py:671
  90.3 21.3 %all-to-all-start.2 = ((f32[128,1,128]{2,1,0:T(1,128)}), f32[128,1,128]{2,1,0:T(1,128)S(1)}, u32[]{:S(2)}, u32[]{:S(2)}) async-start(f32[128,1,128]{2,1,0:T(1,128)} %bitcast.39), calls=%async_computation.2 | async-start | bytes 131072 | tf_op jit(solution)/shard_map/all_to_all | solution.py:607
  111.7 0.6 copy-start.4
  111.7 0.7 copy-start.11

commit v3 on v2

--- a/solution.py
+++ b/solution.py
@@ -80,7 +80,7 @@
 PARAMS = pltpu.CompilerParams(vmem_limit_bytes=LIMIT)
 
 
-def sums_kernel(cells_hbm, sums_ref, first_ref, last_ref, x, sems):
+def sums_kernel(place_ref, cells_hbm, sums_ref, one_ref, other_ref, x, sems):
     half = COLS // 2
     copies = []
     for s in range(2):
@@ -109,15 +109,17 @@
             column = jnp.sum(acc, axis=1, keepdims=True)
             own = members(PART, 0, 64 * k + 32 * s)
             row += jnp.sum(jnp.where(own, column, 0.0), axis=0, keepdims=True)
-        first_ref[s] = x[s, 0:2]
-        last_ref[s] = x[s, COLS - 2 : COLS]
+        even = place_ref[0] % 2 == 0
+        first, last = x[s, 0:2].astype(F32), x[s, COLS - 2 : COLS].astype(F32)
+        one_ref[s] = jnp.where(even, last, first).astype(BF16)
+        other_ref[s] = jnp.where(even, first, last).astype(BF16)
     sums_ref[...] = jnp.broadcast_to(row, sums_ref.shape)
 
 
-def local_sums(cells):
+def local_sums(place, cells):
     return pl.pallas_call(
         sums_kernel,
-        in_specs=[ANY],
+        in_specs=[SMEM, ANY],
         out_specs=[VMEM] * 3,
         out_shape=[
             jax.ShapeDtypeStruct((16, 128), F32),
@@ -127,7 +129,7 @@
         scratch_shapes=[pltpu.VMEM((2, COLS, PART, LAT), BF16), pltpu.SemaphoreType.DMA((4,))],
         compiler_params=PARAMS,
         name="local_sums",
-    )(cells)
+    )(place, cells)
 
 
 def pack_kernel(cells_hbm, pay_hbm, x, out, taken, turned, sems):
@@ -196,16 +198,22 @@
     )(cells)
 
 
-def halo_kernel(sums_ref, first_ref, last_ref, left_ref, right_ref, _, pay_hbm, out, sems):
+def halo_kernel(
+    place_ref, sums_ref, one_ref, other_ref, from_one, from_other, _, pay_hbm, out, sems,
+):
     lane = lanes(PART)
     pad = jnp.zeros((PART, 128 - LAT), F32)
     row = jnp.sum(sums_ref[...], axis=0, keepdims=True)
 
     @pl.loop(0, 2)
     def _(s):
-        near = [left_ref[s, 0], left_ref[s, 1], first_ref[s, 0], last_ref[s, 1],
-                right_ref[s, 0], right_ref[s, 1]]
-        near = [jnp.concatenate([col.astype(F32), pad], axis=1) for col in near]
+        even = place_ref[0] % 2 == 0
+        one, other = one_ref[s].astype(F32), other_ref[s].astype(F32)
+        first, last = jnp.where(even, other, one), jnp.where(even, one, other)
+        one, other = from_one[s].astype(F32), from_other[s].astype(F32)
+        left, right = jnp.where(even, other, one), jnp.where(even, one, other)
+        near = [left[0], left[1], first[0], last[1], right[0], right[1]]
+        near = [jnp.concatenate([col, pad], axis=1) for col in near]
         carried = jnp.zeros((PART, 128), F32)
         for k in range(2):
             own = members(PART, 0, 64 * k + 32 * s)
@@ -226,20 +234,20 @@
         pltpu.make_async_copy(out.at[s], pay_hbm.at[:, 8 * s + 7], sems.at[s]).wait()
 
 
-def pack_halo(sums, first, last, left, right, pay):
+def pack_halo(place, sums, ours, theirs, pay):
     return pl.pallas_call(
         halo_kernel,
-        in_specs=[VMEM] * 5 + [ANY],
+        in_specs=[SMEM] + [VMEM] * 5 + [ANY],
         out_specs=ANY,
         out_shape=jax.ShapeDtypeStruct((SRC, 16, PART, 128), BF16),
         scratch_shapes=[
             pltpu.VMEM((2, SRC, PART, 128), BF16),
             pltpu.SemaphoreType.DMA((2,)),
         ],
-        input_output_aliases={5: 0},
+        input_output_aliases={6: 0},
         compiler_params=PARAMS,
         name="pack_halo",
-    )(sums, first, last, left, right, pay)
+    )(place, sums, *ours, *theirs, pay)
 
 
 def weight_kernel(j, w_hbm, o_hbm, x, out, sems):
@@ -350,7 +358,7 @@
 
 def first_kernel(
     part_ref, par_ref, pick_ref, taps_ref, recv_hbm, w_hbm,
-    hid_hbm, out_sums, to_next, to_prev, out_halo,
+    hid_hbm, out_sums, one, other, out_halo,
     xs, wv, scale, offset, recv, hid, sides, xh, sems,
 ):
     fetches = [
@@ -426,6 +434,7 @@
 
     row = jnp.zeros((1, 128), F32)
     low = lanes(128) < 64
+    even = part % 2 == 0
     for at in range(0, C, 128):
         for s in range(2):
             pieces = [hid[s, at : at + 128, 128 * q : 128 * (q + 1)] for q in range(6)]
@@ -434,8 +443,10 @@
                 own = members(128, at, 64 * k + 32 * s)
                 row += jnp.sum(jnp.where(own, column, 0.0), axis=0, keepdims=True)
         start, end = hid.at[:, at : at + 128, 0:128], hid.at[:, at : at + 128, 640:768]
-        to_next[at : at + 128, :] = jnp.where(low, roll(end[0], 64), end[1]).astype(BF16)
-        to_prev[at : at + 128, :] = jnp.where(low, start[0], roll(start[1], 64)).astype(BF16)
+        after = jnp.where(low, roll(end[0], 64), end[1])
+        ahead = jnp.where(low, start[0], roll(start[1], 64))
+        one[at : at + 128, :] = jnp.where(even, after, ahead).astype(BF16)
+        other[at : at + 128, :] = jnp.where(even, ahead, after).astype(BF16)
     out_sums[...] = jnp.broadcast_to(row, out_sums.shape)
     for store in stores:
         store.wait()
@@ -472,7 +483,7 @@
 
 
 def second_kernel(
-    part_ref, coef_ref, sums_ref, par_ref, pick_ref, near_ref, prev_ref, next_ref,
+    part_ref, coef_ref, sums_ref, par_ref, pick_ref, near_ref, one_ref, other_ref,
     hid_hbm, w_hbm, recv_hbm, target_hbm,
     noise_hbm, out_ref,
     xs, wv, hid, lat, target, noise_out, sides, scale, offset, sems,
@@ -489,6 +500,7 @@
     part = part_ref[0]
     row = jnp.sum(sums_ref[...], axis=0, keepdims=True)
     low = lanes(PART) < 64
+    even = part % 2 == 0
 
     def columns(s):
         total, square = (
@@ -509,7 +521,8 @@
             return silu(x * a + o)
 
         tiles = [act(hid[s, rows, 128 * q : 128 * (q + 1)]) for q in range(6)]
-        above, below = prev_ref[rows, :].astype(F32), next_ref[rows, :].astype(F32)
+        below, above = one_ref[rows, :].astype(F32), other_ref[rows, :].astype(F32)
+        above, below = jnp.where(even, above, below), jnp.where(even, below, above)
         if s == 0:
             edge = jnp.where(low, above, roll(below, 64))
         else:
@@ -608,9 +621,13 @@
     return got.reshape(-1, 128)
 
 
-def ring(axis, step, wrap):
+def swap_neighbours(one, other, axis, wrap):
     size = lax.axis_size(axis)
-    return [(i, (i + step) % size) for i in range(size) if wrap or 0 <= i + step < size]
+    pairs = [(i, i ^ 1) for i in range(size)]
+    rest = [(i, (i + 1 if i % 2 else i - 1) % size) for i in range(size)]
+    if not wrap:
+        rest = rest[1:-1]
+    return lax.ppermute(one, axis, pairs), lax.ppermute(other, axis, rest)
 
 
 def swap(array, axis):
@@ -638,12 +655,12 @@
     tap_pick = jnp.asarray(halo_taps())
 
     cells = latents.transpose(1, 2, 3, 0)
-    sums, first, last = local_sums(cells)
+    place = lax.axis_index("lon").astype(jnp.int32).reshape(1)
+    sums, *ours = local_sums(place, cells)
     sums = everywhere(sums, "lon")
-    left = lax.ppermute(last, "lon", ring("lon", 1, True))
-    right = lax.ppermute(first, "lon", ring("lon", -1, True))
-    pay = pack(after(cells, first))
-    pay = pack_halo(sums, first, last, left, right, pay)
+    theirs = swap_neighbours(*ours, "lon", True)
+    pay = pack(after(cells, ours[0]))
+    pay = pack_halo(place, sums, ours, theirs, pay)
     recv = swap(pay, "ch")
     conv_weights, time_w1, following = after((conv_weights, time_w1, next_latents), pay)
     turned = [turn_weights(j, conv_weights) for j in range(2)]
@@ -664,14 +681,13 @@
     coef = jnp.stack([ratio, keep - ratio * jnp.sqrt(1.0 - alpha)], axis=1).reshape(4)
 
     recv, turned, target = lax.optimization_barrier((recv, turned, target))
-    hidden, sums, to_next, to_prev, near = first_conv(
+    hidden, sums, one, other, near = first_conv(
         part, params, first_pick, tap_pick, recv, turned[0]
     )
-    from_prev = lax.ppermute(to_next, "ch", ring("ch", 1, False))
-    from_next = lax.ppermute(to_prev, "ch", ring("ch", -1, False))
+    one, other = swap_neighbours(one, other, "ch", False)
     sums = everywhere(sums, ("lon", "ch"))
     noise, terms = second_conv(
-        part, coef, sums, params, second_pick, (near, from_prev, from_next),
+        part, coef, sums, params, second_pick, (near, one, other),
         hidden, turned[1], recv, target,
     )
     squares = jnp.sum(everywhere(terms, ("lon", "ch")), axis=0)[:2]

time: 149 us -> 145 us (0.973)
  starting transfers between devices: 33.1 us -> 28.9 us
    all_to_all x2, starting transfers between devices: 22 us -> 19.4 us  [everywhere(): got = lax.all_to_all(rows.reshape(-1, 1, 128), axes, 0, 0, tiled=True)]
    ppermute x4, starting transfers between devices: 5.83 us -> 4.2 us  [swap_neighbours(): return (lax.ppermute(one, axis, pairs), lax.ppermute(other, axis, rest))]
  transfers between devices with their start and end apart: 7 -> 7, of which waited for: 3 -> 3; matrix products, arithmetic and copies ran while one was open for 4% -> 4% of each run, Pallas kernels for 15% -> 16%
where the time goes in v3:
time: 145 us; the launch traced here: 144 us
  Pallas kernels  72.4 us (50%)
  starting transfers between devices  28.9 us (20%)
  waiting for transfers between devices  19.8 us (14%)
  blocking collectives  14.1 us (10%)
  local copies, waits for them, and re-layouts  4.84 us (3%)
  matrix products  2.51 us (2%)
    pallas_call x1, Pallas kernels, first_conv(): pl.pallas_call(first_kernel, in_specs=[SMEM] + [VMEM] * 3 + [ANY] * 2, ou...  22.7 us
    pallas_call x1, Pallas kernels, second_conv(): pl.pallas_call(second_kernel, in_specs=[SMEM, SMEM] + [VMEM] * 6 + [ANY]...  21.3 us
    all_to_all x2, starting transfers between devices, everywhere(): got = lax.all_to_all(rows.reshape(-1, 1, 128), axes, 0, 0, tiled=True)  19.4 us
    all_to_all x1, blocking collectives, everywhere(): got = lax.all_to_all(rows.reshape(-1, 1, 128), axes, 0, 0, tiled=True)  14.1 us
    pallas_call x2, Pallas kernels, turn_weights(): pl.pallas_call(functools.partial(weight_kernel, j), in_specs=[ANY], out_s...  12.7 us
    all_to_all x1, waiting for transfers between devices, swap(): return lax.all_to_all(array, axis, split_axis=0, concat_axis=0, tiled=True)  10.4 us
    all_to_all x2, waiting for transfers between devices, everywhere(): got = lax.all_to_all(rows.reshape(-1, 1, 128), axes, 0, 0, tiled=True)  9.41 us
    pallas_call x1, Pallas kernels, pack(): pl.pallas_call(pack_kernel, in_specs=[ANY], out_specs=ANY, out_shape=jax....  6.45 us
  transfers between devices with their start and end apart: 7, of which 3 were waited for; matrix products, arithmetic and copies ran while one was open for 4% of the time, Pallas kernels for 16%

profile of v3, /device:TPU:1, one launch (start us, length us, event | category | flops | bytes accessed | tf_op | source)
XLA Modules:
  0.0 144.4 jit_solution(10657170873020465073)
XLA Ops:
  0.6 0.0 copy-start
  0.7 2.9 %local_sums.1 = (f32[16,128]{1,0:T(8,128)}, bf16[2,2,80,96]{3,2,1,0:T(8,128)(2,1)}, bf16[2,2,80,96]{3,2,1,0:T(8,128)(2,1)}) custom-call(s32[1]{0:T(128)} %bitcast.8.place_ref, bf16[2,64,80,96]{3,2,1,0:T(8,128)(2,1)} %bitcast.37), custom_call_target="tpu_custom_call" | custom-call | tf_op jit(solution)/shard_map/local_sums/pallas_call | solution.py:120
  3.6 1.5 %collective-permute-start = (bf16[2,2,80,96]{3,2,1,0:T(8,128)(2,1)}, bf16[2,2,80,96]{3,2,1,0:T(8,128)(2,1)S(1)}, u32[]{:S(2)}, u32[]{:S(2)}) collective-permute-start(bf16[2,2,80,96]{3,2,1,0:T(8,128)(2,1)} %get-tuple-element.21.one_ref), channel_id=1, source_target_pairs={{0,8},{8,0},{16,24},{24,16},{32,40},{40,32},{48,56},{56,48},{64,72... | collective-permute-start | bytes 184328 | tf_op jit(solution)/shard_map/ppermute | solution.py:630
  5.1 1.3 collective-permute-start.1
  6.4 7.6 %all-to-all-start = ((f32[16,1,128]{2,1,0:T(1,128)}), f32[16,1,128]{2,1,0:T(1,128)S(1)}, u32[]{:S(2)}, u32[]{:S(2)}) async-start(f32[16,1,128]{2,1,0:T(1,128)} %bitcast.43), calls=%async_computation | async-start | bytes 16384 | tf_op jit(solution)/shard_map/all_to_all | solution.py:620
  14.0 6.4 %pack_latents.1._ = bf16[8,16,80,128]{3,2,1,0:T(8,128)(2,1)} custom-call(bf16[2,64,80,96]{3,2,1,0:T(8,128)(2,1)} %bitcast.38), custom_call_target="tpu_custom_call" | custom-call | flops 1000000000 | bytes 8000000 | tf_op jit(solution)/shard_map/pack_latents/pallas_call | solution.py:181
  20.4 0.6 all-to-all-done
  21.0 0.0 copy-start.5
  21.0 0.0 collective-permute-done.from_one
  21.0 0.0 copy-start.2
  21.0 0.0 collective-permute-done.1.from_other
  21.0 0.0 copy-start.3
  21.0 0.6 copy-done.5
  21.6 0.1 copy-done.2
  21.7 0.0 copy-done.3
  21.7 2.4 %pack_halo.1 = bf16[8,16,80,128]{3,2,1,0:T(8,128)(2,1)} custom-call(s32[1]{0:T(128)} %bitcast.8.place_ref, f32[16,128]{1,0:T(8,128)} %bitcast.42, bf16[2,2,80,96]{3,2,1,0:T(8,128)(2,1)} %get-tuple-element.21.one_ref, bf16[2,2,80,96]{3,2,1,0:T(8,128)(2,1)} %get-tuple-element.22.other_ref, ...), custom_call_target="tpu_custom_call", output_to_operand_aliasing={{}: (6, {})} | custom-call | tf_op jit(solution)/shard_map/pack_halo/pallas_call | solution.py:238
  24.1 0.0 copy-start.9
  24.1 0.0 copy-start.10
  24.1 0.0 copy-start.8
  24.2 5.3 %all-to-all-start.1 = ((bf16[8,16,80,128]{3,2,1,0:T(8,128)(2,1)}), bf16[8,16,80,128]{3,2,1,0:T(8,128)(2,1)}, u32[]{:S(2)}, u32[]{:S(2)}) async-start(bf16[8,16,80,128]{3,2,1,0:T(8,128)(2,1)} %pack_halo.1), calls=%async_computation.1 | async-start | bytes 5242880 | tf_op jit(solution)/shard_map/all_to_all | solution.py:634
  29.5 0.0 copy-done.9
  29.5 0.0 copy-start.1
  29.5 0.0 copy-done.10
  29.5 0.1 fusion.11
  29.6 0.1 multiply_cosine_fusion
  29.7 0.0 copy-done.8
  29.7 3.9 %turn_target.1.target_hbm = bf16[2,6,640,128]{3,2,1,0:T(8,128)(2,1)} custom-call(bf16[12,2,64,640]{3,2,1,0:T(8,128)(2,1)} %target_hbm), custom_call_target="tpu_custom_call" | custom-call | tf_op jit(solution)/shard_map/turn_target/pallas_call | solution.py:304
  33.6 0.0 copy-start.6
  33.6 0.0 copy-start.7
  33.6 0.0 copy-done.1
  33.6 0.8 fusion.5
  34.4 0.0 copy-done
  34.4 1.7 %fusion = f32[2,640]{1,0:T(2,128)S(1)} fusion(f32[1280,640]{1,0:T(8,128)S(1)} %copy-done, f32[2,1280]{1,0:T(2,128)S(1)} %fusion.5), kind=kOutput, calls=%fused_computation.1 | convolution fusion | flops 19671040 | bytes 3292160 | tf_op jit(solution)/shard_map/dot_general | solution.py:611
  36.1 0.0 copy-done.6
  36.1 0.0 copy-done.7
  36.2 0.9 copy.27
  37.1 1.7 %pad.4.par_ref = f32[640,128]{1,0:T(8,128)} pad(f32[640,7]{1,0:T(8,128)} %copy.27, f32[]{:T(128)} %constant.46.clone.1), padding=0_0x0_121 | pad | bytes 345604 | tf_op jit(solution)/shard_map/jit(_pad)/pad | solution.py:674
  38.8 6.3 %turn_weights_0.1.w_hbm = bf16[640,5760]{1,0:T(8,128)(2,1)} custom-call(bf16[2,9,640,640]{3,2,1,0:T(8,128)(2,1)} %bitcast.35), custom_call_target="tpu_custom_call" | custom-call | flops 1887436800 | bytes 15000000 | tf_op jit(solution)/shard_map/turn_weights_0/pallas_call | solution.py:270
  45.2 6.4 %turn_weights_1.1.w_hbm = bf16[640,5760]{1,0:T(8,128)(2,1)} custom-call(bf16[2,9,640,640]{3,2,1,0:T(8,128)(2,1)} %bitcast.36), custom_call_target="tpu_custom_call" | custom-call | flops 1887436800 | bytes 15000000 | tf_op jit(solution)/shard_map/turn_weights_1/pallas_call | solution.py:270
  51.5 10.4 %all-to-all-done.1.recv_hbm = bf16[8,16,80,128]{3,2,1,0:T(8,128)(2,1)} async-done(((bf16[8,16,80,128]{3,2,1,0:T(8,128)(2,1)}), bf16[8,16,80,128]{3,2,1,0:T(8,128)(2,1)}, u32[]{:S(2)}, u32[]{:S(2)}) %all-to-all-start.1) | async-done | bytes 2621472 | tf_op jit(solution)/shard_map/all_to_all | solution.py:634
  61.9 22.7 %first_conv.1 = (f32[2,640,768]{2,1,0:T(8,128)}, f32[128,128]{1,0:T(8,128)}, bf16[640,128]{1,0:T(8,128)(2,1)}, bf16[640,128]{1,0:T(8,128)(2,1)}, bf16[640,128]{1,0:T(8,128)(2,1)}) custom-call(s32[1]{0:T(128)} %bitcast.part_ref, f32[640,128]{1,0:T(8,128)} %pad.4.par_ref, bf16[128,128]{1,0:T(8,128)(2,1)} %constant.51.clone.pick_ref, ...), custom_call_target="tpu_custom_call" | custom-call | flops 11324620800 | bytes 20000000 | tf_op jit(solution)/shard_map/first_conv/pallas_call | solution.py:457
  84.6 0.1 collective-permute-start.2
  84.7 1.3 collective-permute-start.3
  86.1 0.1 subtract_bitcast_fusion
  86.1 11.8 %all-to-all-start.2 = ((f32[128,1,128]{2,1,0:T(1,128)}), f32[128,1,128]{2,1,0:T(1,128)S(1)}, u32[]{:S(2)}, u32[]{:S(2)}) async-start(f32[128,1,128]{2,1,0:T(1,128)} %bitcast.40), calls=%async_computation.2 | async-start | bytes 131072 | tf_op jit(solution)/shard_map/all_to_all | solution.py:620
  98.0 0.1 copy.25
  98.1 0.7 reshape.76.coef_ref
  98.7 8.8 %all-to-all-done.2 = f32[128,1,128]{2,1,0:T(1,128)S(1)} async-done(((f32[128,1,128]{2,1,0:T(1,128)}), f32[128,1,128]{2,1,0:T(1,128)S(1)}, u32[]{:S(2)}, u32[]{:S(2)}) %all-to-all-start.2) | async-done | bytes 65568 | tf_op jit(solution)/shard_map/all_to_all | solution.py:620
  107.6 0.0 copy-start.4
  107.6 0.0 collective-permute-done.2.one_ref
  107.6 0.0 copy-start.11
  107.6 0.0 collective-permute-done.3.other_ref
  107.6 0.6 copy-done.4
  108.2 0.1 copy-done.11
  108.3 21.3 %second_conv.1 = (bf16[12,2,64,640]{3,2,1,0:T(8,128)(2,1)}, f32[128,128]{1,0:T(8,128)}) custom-call(s32[1]{0:T(128)} %bitcast.part_ref, f32[4]{0:T(128)} %reshape.76.coef_ref, f32[128,128]{1,0:T(8,128)} %bitcast.39, f32[640,128]{1,0:T(8,128)} %pad.4.par_ref, bf16[2,128,128]{2,1,0:T(8,128)(2,1)} %constant.52.clone.pick_ref, ...), custom_call_target="tpu_custom_call" | custom-call | flops 11324620800 | bytes 20000000 | tf_op jit(solution)/shard_map/second_conv/pallas_call | solution.py:577
  129.6 14.1 %all_to_all.20 = f32[128,1,128]{2,1,0:T(1,128)S(1)} all-to-all(f32[128,1,128]{2,1,0:T(1,128)} %bitcast.41), channel_id=1, replica_groups=mesh['lon'=16,'ch'=8] {'lon','ch'}, dimensions={0} | all-to-all | bytes 131072 | tf_op jit(solution)/shard_map/all_to_all | solution.py:620
  143.6 0.2 reduce_sum.9
  143.8 0.6 subtract_add_fusion
  (6 shorter events, 0.1 us)
Async XLA Ops:
  0.6 33.8 %copy-start = (f32[1280,640]{1,0:T(8,128)S(1)}, f32[1280,640]{1,0:T(8,128)}, u32[]{:S(2)}) copy-start(f32[1280,640]{1,0:T(8,128)} %param.22) | copy-start | bytes 9830404
  3.6 17.4 %collective-permute-start = (bf16[2,2,80,96]{3,2,1,0:T(8,128)(2,1)}, bf16[2,2,80,96]{3,2,1,0:T(8,128)(2,1)S(1)}, u32[]{:S(2)}, u32[]{:S(2)}) collective-permute-start(bf16[2,2,80,96]{3,2,1,0:T(8,128)(2,1)} %get-tuple-element.21.one_ref), channel_id=1, source_target_pairs={{0,8},{8,0},{16,24},{24,16},{32,40},{40,32},{48,56},{56,48},{64,72... | collective-permute-start | bytes 184328 | tf_op jit(solution)/shard_map/ppermute | solution.py:630
  5.1 15.9 %collective-permute-start.1 = (bf16[2,2,80,96]{3,2,1,0:T(8,128)(2,1)}, bf16[2,2,80,96]{3,2,1,0:T(8,128)(2,1)S(1)}, u32[]{:S(2)}, u32[]{:S(2)}) collective-permute-start(bf16[2,2,80,96]{3,2,1,0:T(8,128)(2,1)} %get-tuple-element.22.other_ref), channel_id=1, source_target_pairs={{0,120},{8,16},{16,8},{24,32},{32,24},{40,48},{48,40},{56,64},{64,... | collective-permute-start | bytes 184328 | tf_op jit(solution)/shard_map/ppermute | solution.py:630
  6.4 14.6 %all-to-all-start = ((f32[16,1,128]{2,1,0:T(1,128)}), f32[16,1,128]{2,1,0:T(1,128)S(1)}, u32[]{:S(2)}, u32[]{:S(2)}) async-start(f32[16,1,128]{2,1,0:T(1,128)} %bitcast.43), calls=%async_computation | async-start | bytes 16384 | tf_op jit(solution)/shard_map/all_to_all | solution.py:620
  21.0 0.6 copy-start.5
  21.0 0.6 copy-start.2
  21.0 0.7 copy-start.3
  24.1 5.3 %copy-start.9 = (s32[2]{0:T(128)S(1)}, s32[2]{0:T(128)}, u32[]{:S(2)}) copy-start(s32[2]{0:T(128)} %param.15) | copy-start | bytes 28
  24.1 5.4 %copy-start.10 = (s32[2]{0:T(128)S(1)}, s32[2]{0:T(128)}, u32[]{:S(2)}) copy-start(s32[2]{0:T(128)} %param.16) | copy-start | bytes 28
  24.1 5.5 %copy-start.8 = (f32[2,640]{1,0:T(2,128)S(1)}, f32[2,640]{1,0:T(2,128)}, u32[]{:S(2)}) copy-start(f32[2,640]{1,0:T(2,128)} %param.19) | copy-start | bytes 15364
  24.2 37.7 %all-to-all-start.1 = ((bf16[8,16,80,128]{3,2,1,0:T(8,128)(2,1)}), bf16[8,16,80,128]{3,2,1,0:T(8,128)(2,1)}, u32[]{:S(2)}, u32[]{:S(2)}) async-start(bf16[8,16,80,128]{3,2,1,0:T(8,128)(2,1)} %pack_halo.1), calls=%async_computation.1 | async-start | bytes 5242880 | tf_op jit(solution)/shard_map/all_to_all | solution.py:634
  29.5 4.1 %copy-start.1 = (f32[320,1280]{1,0:T(8,128)S(1)}, f32[320,1280]{1,0:T(8,128)}, u32[]{:S(2)}) copy-start(f32[320,1280]{1,0:T(8,128)} %param.21) | copy-start | bytes 4915204
  33.6 2.5 %copy-start.6 = (f32[2,640]{1,0:T(2,128)S(1)}, f32[2,640]{1,0:T(2,128)}, u32[]{:S(2)}) copy-start(f32[2,640]{1,0:T(2,128)} %param.18) | copy-start | bytes 15364
  33.6 2.5 %copy-start.7 = (f32[2,640]{1,0:T(2,128)S(1)}, f32[2,640]{1,0:T(2,128)}, u32[]{:S(2)}) copy-start(f32[2,640]{1,0:T(2,128)} %param.20) | copy-start | bytes 15364
  84.6 22.9 %collective-permute-start.2 = (bf16[640,128]{1,0:T(8,128)(2,1)}, bf16[640,128]{1,0:T(8,128)(2,1)S(1)}, u32[]{:S(2)}, u32[]{:S(2)}) collective-permute-start(bf16[640,128]{1,0:T(8,128)(2,1)} %get-tuple-element.31), channel_id=1, source_target_pairs={{0,1},{1,0},{2,3},{3,2},{4,5},{5,4},{6,7},{7,6},{8,9},{9,8},{10,11... | collective-permute-start | bytes 491528 | tf_op jit(solution)/shard_map/ppermute | solution.py:630
  84.7 22.9 %collective-permute-start.3 = (bf16[640,128]{1,0:T(8,128)(2,1)}, bf16[640,128]{1,0:T(8,128)(2,1)}, u32[]{:S(2)}, u32[]{:S(2)}) collective-permute-start(bf16[640,128]{1,0:T(8,128)(2,1)} %get-tuple-element.32), channel_id=1, source_target_pairs={{1,2},{2,1},{3,4},{4,3},{5,6},{6,5},{9,10},{10,9},{11,12},{12,11},... | collective-permute-start | bytes 491528 | tf_op jit(solution)/shard_map/ppermute | solution.py:630
  86.1 21.4 %all-to-all-start.2 = ((f32[128,1,128]{2,1,0:T(1,128)}), f32[128,1,128]{2,1,0:T(1,128)S(1)}, u32[]{:S(2)}, u32[]{:S(2)}) async-start(f32[128,1,128]{2,1,0:T(1,128)} %bitcast.40), calls=%async_computation.2 | async-start | bytes 131072 | tf_op jit(solution)/shard_map/all_to_all | solution.py:620
  107.6 0.6 copy-start.4
  107.6 0.7 copy-start.11

commit v4 on v3

--- a/solution.py
+++ b/solution.py
@@ -73,8 +73,8 @@
     return (chan >= low) & (chan < low + WIDTH)
 
 
-def silu(x):
-    return 0.5 * x * (1.0 + jnp.tanh(0.5 * x))
+def silu_of_half(h):
+    return h + h * jnp.tanh(h)
 
 
 PARAMS = pltpu.CompilerParams(vmem_limit_bytes=LIMIT)
@@ -322,8 +322,8 @@
     spread = square / count - mean * mean
     factor = lax.rsqrt(spread + 1e-05) * par_ref[:, 2 * j : 2 * j + 1]
     rest = par_ref[:, 2 * j + 1 : 2 * j + 2] - mean * factor
-    scale[...] = jnp.broadcast_to(factor, scale.shape)
-    offset[...] = jnp.broadcast_to(rest, offset.shape)
+    scale[...] = jnp.broadcast_to(0.5 * factor, scale.shape)
+    offset[...] = jnp.broadcast_to(0.5 * rest, offset.shape)
 
 
 def spread_taps(xs, at, tiles, edge, sides, part):
@@ -332,6 +332,8 @@
     low = lane < 64
     first = (lane == 0) | (lane == 64)
     last = (lane == 63) | (lane == 127)
+    tiles, edge = [tile.astype(BF16) for tile in tiles], edge.astype(BF16)
+    zero = jnp.zeros((rows, 128), BF16)
     for q in range(-1, 7):
         if q == -1:
             tile = jnp.where(low, edge, roll(tiles[5], 64))
@@ -343,10 +345,10 @@
         taps = (jnp.where(first, side, roll(tile, 1)), tile, jnp.where(last, side, roll(tile, -1)))
         for k, tap in enumerate(taps):
             if q == -1:
-                tap = jnp.where(low & (part == 0), 0.0, tap)
+                tap = jnp.where(low & (part == 0), zero, tap)
             elif q == 6:
-                tap = jnp.where((~low) & (part == SRC - 1), 0.0, tap)
-            xs[pl.ds(k * C + at, rows), 128 * (q + 1) : 128 * (q + 2)] = tap.astype(BF16)
+                tap = jnp.where((~low) & (part == SRC - 1), zero, tap)
+            xs[pl.ds(k * C + at, rows), 128 * (q + 1) : 128 * (q + 2)] = tap
 
 
 def product(wv, xs, n, more=None):
@@ -372,7 +374,7 @@
     lane = lanes(C)
 
     def act(x, a, o):
-        return silu(x.astype(F32) * a + o)
+        return silu_of_half(x.astype(F32) * a + o)
 
     def columns(s):
         fetches[s].wait()
@@ -387,7 +389,7 @@
         outside = ((part == 0) & (r < 0)) | ((part == SRC - 1) & (r >= ROWS)) | unused
         x = act(jnp.where(unused, 0.0, tile), scale[s], offset[s])
         halo = jnp.where(outside, 0.0, x).astype(BF16)
-        sides[s] = jnp.dot(halo, pick_ref[...], preferred_element_type=F32)
+        sides[s] = jnp.dot(halo, pick_ref[...], preferred_element_type=F32).astype(BF16)
         return halo
 
     def prepare(s, b):
@@ -470,7 +472,7 @@
             pltpu.VMEM((2, C, 128), F32),
             pltpu.VMEM((2, SRC, 8, PART, 128), BF16),
             pltpu.VMEM((2, C, 768), F32),
-            pltpu.VMEM((2, C, 128), F32),
+            pltpu.VMEM((2, C, 128), BF16),
             pltpu.VMEM((TAPS * C, 128), BF16),
             pltpu.SemaphoreType.DMA((9,)),
         ],
@@ -508,8 +510,8 @@
             for base in (32 * s, 64 + 32 * s)
         )
         affine(total, square, par_ref, 1, scale.at[s], offset.at[s])
-        halo = silu(near_ref[...].astype(F32) * scale[s] + offset[s]).astype(BF16)
-        sides[s] = jnp.dot(halo, pick_ref[s], preferred_element_type=F32)
+        halo = silu_of_half(near_ref[...].astype(F32) * scale[s] + offset[s]).astype(BF16)
+        sides[s] = jnp.dot(halo, pick_ref[s], preferred_element_type=F32).astype(BF16)
         fetches[s].wait()
 
     def prepare(s, b):
@@ -518,7 +520,7 @@
         a, o = scale[s, rows, :], offset[s, rows, :]
 
         def act(x):
-            return silu(x * a + o)
+            return silu_of_half(x * a + o)
 
         tiles = [act(hid[s, rows, 128 * q : 128 * (q + 1)]) for q in range(6)]
         below, above = one_ref[rows, :].astype(F32), other_ref[rows, :].astype(F32)
@@ -589,7 +591,7 @@
             pltpu.VMEM((2, SRC, 6, PART, 128), BF16),
             pltpu.VMEM((2, 6, C, 128), BF16),
             pltpu.VMEM((2, ROWS, COLS, C), BF16),
-            pltpu.VMEM((2, C, 128), F32),
+            pltpu.VMEM((2, C, 128), BF16),
             pltpu.VMEM((2, C, 128), F32),
             pltpu.VMEM((2, C, 128), F32),
             pltpu.SemaphoreType.DMA((9,)),

time: 145 us -> 144 us (level)
  no operation moved by 1% of the time
where the time goes in v4:
time: 144 us; the launch traced here: 143 us
  Pallas kernels  71.4 us (50%)
  starting transfers between devices  28.9 us (20%)
  waiting for transfers between devices  19.8 us (14%)
  blocking collectives  14.1 us (10%)
  local copies, waits for them, and re-layouts  4.84 us (3%)
  matrix products  2.51 us (2%)
    pallas_call x1, Pallas kernels, first_conv(): pl.pallas_call(first_kernel, in_specs=[SMEM] + [VMEM] * 3 + [ANY] * 2, ou...  22 us
    pallas_call x1, Pallas kernels, second_conv(): pl.pallas_call(second_kernel, in_specs=[SMEM, SMEM] + [VMEM] * 6 + [ANY]...  21.1 us
    all_to_all x2, starting transfers between devices, everywhere(): got = lax.all_to_all(rows.reshape(-1, 1, 128), axes, 0, 0, tiled=True)  19.4 us
    all_to_all x1, blocking collectives, everywhere(): got = lax.all_to_all(rows.reshape(-1, 1, 128), axes, 0, 0, tiled=True)  14.1 us
    pallas_call x2, Pallas kernels, turn_weights(): pl.pallas_call(functools.partial(weight_kernel, j), in_specs=[ANY], out_s...  12.7 us
    all_to_all x1, waiting for transfers between devices, swap(): return lax.all_to_all(array, axis, split_axis=0, concat_axis=0, tiled=True)  10.4 us
    all_to_all x2, waiting for transfers between devices, everywhere(): got = lax.all_to_all(rows.reshape(-1, 1, 128), axes, 0, 0, tiled=True)  9.41 us
    pallas_call x1, Pallas kernels, pack(): pl.pallas_call(pack_kernel, in_specs=[ANY], out_specs=ANY, out_shape=jax....  6.45 us
  transfers between devices with their start and end apart: 7, of which 3 were waited for; matrix products, arithmetic and copies ran while one was open for 4% of the time, Pallas kernels for 16%

profile of v4, /device:TPU:1, one launch (start us, length us, event | category | flops | bytes accessed | tf_op | source)
XLA Modules:
  0.0 143.4 jit_solution(277218200602863656)
XLA Ops:
  0.6 0.0 copy-start
  0.7 2.9 %local_sums.1 = (f32[16,128]{1,0:T(8,128)}, bf16[2,2,80,96]{3,2,1,0:T(8,128)(2,1)}, bf16[2,2,80,96]{3,2,1,0:T(8,128)(2,1)}) custom-call(s32[1]{0:T(128)} %bitcast.8.place_ref, bf16[2,64,80,96]{3,2,1,0:T(8,128)(2,1)} %bitcast.37), custom_call_target="tpu_custom_call" | custom-call | tf_op jit(solution)/shard_map/local_sums/pallas_call | solution.py:120
  3.6 1.5 %collective-permute-start = (bf16[2,2,80,96]{3,2,1,0:T(8,128)(2,1)}, bf16[2,2,80,96]{3,2,1,0:T(8,128)(2,1)S(1)}, u32[]{:S(2)}, u32[]{:S(2)}) collective-permute-start(bf16[2,2,80,96]{3,2,1,0:T(8,128)(2,1)} %get-tuple-element.21.one_ref), channel_id=1, source_target_pairs={{0,8},{8,0},{16,24},{24,16},{32,40},{40,32},{48,56},{56,48},{64,72... | collective-permute-start | bytes 184328 | tf_op jit(solution)/shard_map/ppermute | solution.py:632
  5.1 1.3 collective-permute-start.1
  6.4 7.6 %all-to-all-start = ((f32[16,1,128]{2,1,0:T(1,128)}), f32[16,1,128]{2,1,0:T(1,128)S(1)}, u32[]{:S(2)}, u32[]{:S(2)}) async-start(f32[16,1,128]{2,1,0:T(1,128)} %bitcast.43), calls=%async_computation | async-start | bytes 16384 | tf_op jit(solution)/shard_map/all_to_all | solution.py:622
  14.0 6.4 %pack_latents.1._ = bf16[8,16,80,128]{3,2,1,0:T(8,128)(2,1)} custom-call(bf16[2,64,80,96]{3,2,1,0:T(8,128)(2,1)} %bitcast.38), custom_call_target="tpu_custom_call" | custom-call | flops 1000000000 | bytes 8000000 | tf_op jit(solution)/shard_map/pack_latents/pallas_call | solution.py:181
  20.4 0.6 all-to-all-done
  21.0 0.0 copy-start.5
  21.0 0.0 collective-permute-done.from_one
  21.0 0.0 copy-start.2
  21.0 0.0 collective-permute-done.1.from_other
  21.0 0.0 copy-start.3
  21.0 0.6 copy-done.5
  21.6 0.1 copy-done.2
  21.7 0.0 copy-done.3
  21.7 2.4 %pack_halo.1 = bf16[8,16,80,128]{3,2,1,0:T(8,128)(2,1)} custom-call(s32[1]{0:T(128)} %bitcast.8.place_ref, f32[16,128]{1,0:T(8,128)} %bitcast.42, bf16[2,2,80,96]{3,2,1,0:T(8,128)(2,1)} %get-tuple-element.21.one_ref, bf16[2,2,80,96]{3,2,1,0:T(8,128)(2,1)} %get-tuple-element.22.other_ref, ...), custom_call_target="tpu_custom_call", output_to_operand_aliasing={{}: (6, {})} | custom-call | tf_op jit(solution)/shard_map/pack_halo/pallas_call | solution.py:238
  24.1 0.0 copy-start.9
  24.1 0.0 copy-start.10
  24.1 0.0 copy-start.8
  24.2 5.3 %all-to-all-start.1 = ((bf16[8,16,80,128]{3,2,1,0:T(8,128)(2,1)}), bf16[8,16,80,128]{3,2,1,0:T(8,128)(2,1)}, u32[]{:S(2)}, u32[]{:S(2)}) async-start(bf16[8,16,80,128]{3,2,1,0:T(8,128)(2,1)} %pack_halo.1), calls=%async_computation.1 | async-start | bytes 5242880 | tf_op jit(solution)/shard_map/all_to_all | solution.py:636
  29.5 0.0 copy-done.9
  29.5 0.0 copy-start.1
  29.5 0.0 copy-done.10
  29.5 0.1 fusion.11
  29.6 0.1 multiply_cosine_fusion
  29.7 0.0 copy-done.8
  29.7 3.9 %turn_target.1.target_hbm = bf16[2,6,640,128]{3,2,1,0:T(8,128)(2,1)} custom-call(bf16[12,2,64,640]{3,2,1,0:T(8,128)(2,1)} %target_hbm), custom_call_target="tpu_custom_call" | custom-call | tf_op jit(solution)/shard_map/turn_target/pallas_call | solution.py:304
  33.6 0.0 copy-start.6
  33.6 0.0 copy-start.7
  33.6 0.0 copy-done.1
  33.6 0.8 fusion.5
  34.4 0.0 copy-done
  34.4 1.7 %fusion = f32[2,640]{1,0:T(2,128)S(1)} fusion(f32[1280,640]{1,0:T(8,128)S(1)} %copy-done, f32[2,1280]{1,0:T(2,128)S(1)} %fusion.5), kind=kOutput, calls=%fused_computation.1 | convolution fusion | flops 19671040 | bytes 3292160 | tf_op jit(solution)/shard_map/dot_general | solution.py:613
  36.1 0.0 copy-done.6
  36.1 0.0 copy-done.7
  36.2 0.9 copy.27
  37.1 1.7 %pad.4.par_ref = f32[640,128]{1,0:T(8,128)} pad(f32[640,7]{1,0:T(8,128)} %copy.27, f32[]{:T(128)} %constant.46.clone.1), padding=0_0x0_121 | pad | bytes 345604 | tf_op jit(solution)/shard_map/jit(_pad)/pad | solution.py:676
  38.8 6.3 %turn_weights_0.1.w_hbm = bf16[640,5760]{1,0:T(8,128)(2,1)} custom-call(bf16[2,9,640,640]{3,2,1,0:T(8,128)(2,1)} %bitcast.35), custom_call_target="tpu_custom_call" | custom-call | flops 1887436800 | bytes 15000000 | tf_op jit(solution)/shard_map/turn_weights_0/pallas_call | solution.py:270
  45.2 6.4 %turn_weights_1.1.w_hbm = bf16[640,5760]{1,0:T(8,128)(2,1)} custom-call(bf16[2,9,640,640]{3,2,1,0:T(8,128)(2,1)} %bitcast.36), custom_call_target="tpu_custom_call" | custom-call | flops 1887436800 | bytes 15000000 | tf_op jit(solution)/shard_map/turn_weights_1/pallas_call | solution.py:270
  51.5 10.4 %all-to-all-done.1.recv_hbm = bf16[8,16,80,128]{3,2,1,0:T(8,128)(2,1)} async-done(((bf16[8,16,80,128]{3,2,1,0:T(8,128)(2,1)}), bf16[8,16,80,128]{3,2,1,0:T(8,128)(2,1)}, u32[]{:S(2)}, u32[]{:S(2)}) %all-to-all-start.1) | async-done | bytes 2621472 | tf_op jit(solution)/shard_map/all_to_all | solution.py:636
  61.9 22.0 %first_conv.1 = (f32[2,640,768]{2,1,0:T(8,128)}, f32[128,128]{1,0:T(8,128)}, bf16[640,128]{1,0:T(8,128)(2,1)}, bf16[640,128]{1,0:T(8,128)(2,1)}, bf16[640,128]{1,0:T(8,128)(2,1)}) custom-call(s32[1]{0:T(128)} %bitcast.part_ref, f32[640,128]{1,0:T(8,128)} %pad.4.par_ref, bf16[128,128]{1,0:T(8,128)(2,1)} %constant.51.clone.pick_ref, ...), custom_call_target="tpu_custom_call" | custom-call | flops 11324620800 | bytes 20000000 | tf_op jit(solution)/shard_map/first_conv/pallas_call | solution.py:459
  83.9 0.1 collective-permute-start.2
  84.0 1.3 collective-permute-start.3
  85.3 0.1 subtract_bitcast_fusion
  85.4 11.8 %all-to-all-start.2 = ((f32[128,1,128]{2,1,0:T(1,128)}), f32[128,1,128]{2,1,0:T(1,128)S(1)}, u32[]{:S(2)}, u32[]{:S(2)}) async-start(f32[128,1,128]{2,1,0:T(1,128)} %bitcast.40), calls=%async_computation.2 | async-start | bytes 131072 | tf_op jit(solution)/shard_map/all_to_all | solution.py:622
  97.2 0.1 copy.25
  97.3 0.7 reshape.76.coef_ref
  98.0 8.8 %all-to-all-done.2 = f32[128,1,128]{2,1,0:T(1,128)S(1)} async-done(((f32[128,1,128]{2,1,0:T(1,128)}), f32[128,1,128]{2,1,0:T(1,128)S(1)}, u32[]{:S(2)}, u32[]{:S(2)}) %all-to-all-start.2) | async-done | bytes 65568 | tf_op jit(solution)/shard_map/all_to_all | solution.py:622
  106.8 0.0 copy-start.4
  106.8 0.0 collective-permute-done.2.one_ref
  106.8 0.0 copy-start.11
  106.8 0.0 collective-permute-done.3.other_ref
  106.8 0.6 copy-done.4
  107.4 0.1 copy-done.11
  107.5 21.1 %second_conv.1 = (bf16[12,2,64,640]{3,2,1,0:T(8,128)(2,1)}, f32[128,128]{1,0:T(8,128)}) custom-call(s32[1]{0:T(128)} %bitcast.part_ref, f32[4]{0:T(128)} %reshape.76.coef_ref, f32[128,128]{1,0:T(8,128)} %bitcast.39, f32[640,128]{1,0:T(8,128)} %pad.4.par_ref, bf16[2,128,128]{2,1,0:T(8,128)(2,1)} %constant.52.clone.pick_ref, ...), custom_call_target="tpu_custom_call" | custom-call | flops 11324620800 | bytes 20000000 | tf_op jit(solution)/shard_map/second_conv/pallas_call | solution.py:579
  128.6 14.1 %all_to_all.20 = f32[128,1,128]{2,1,0:T(1,128)S(1)} all-to-all(f32[128,1,128]{2,1,0:T(1,128)} %bitcast.41), channel_id=1, replica_groups=mesh['lon'=16,'ch'=8] {'lon','ch'}, dimensions={0} | all-to-all | bytes 131072 | tf_op jit(solution)/shard_map/all_to_all | solution.py:622
  142.7 0.2 reduce_sum.9
  142.8 0.6 subtract_add_fusion
  (6 shorter events, 0.1 us)
Async XLA Ops:
  0.6 33.8 %copy-start = (f32[1280,640]{1,0:T(8,128)S(1)}, f32[1280,640]{1,0:T(8,128)}, u32[]{:S(2)}) copy-start(f32[1280,640]{1,0:T(8,128)} %param.22) | copy-start | bytes 9830404
  3.6 17.4 %collective-permute-start = (bf16[2,2,80,96]{3,2,1,0:T(8,128)(2,1)}, bf16[2,2,80,96]{3,2,1,0:T(8,128)(2,1)S(1)}, u32[]{:S(2)}, u32[]{:S(2)}) collective-permute-start(bf16[2,2,80,96]{3,2,1,0:T(8,128)(2,1)} %get-tuple-element.21.one_ref), channel_id=1, source_target_pairs={{0,8},{8,0},{16,24},{24,16},{32,40},{40,32},{48,56},{56,48},{64,72... | collective-permute-start | bytes 184328 | tf_op jit(solution)/shard_map/ppermute | solution.py:632
  5.1 15.9 %collective-permute-start.1 = (bf16[2,2,80,96]{3,2,1,0:T(8,128)(2,1)}, bf16[2,2,80,96]{3,2,1,0:T(8,128)(2,1)S(1)}, u32[]{:S(2)}, u32[]{:S(2)}) collective-permute-start(bf16[2,2,80,96]{3,2,1,0:T(8,128)(2,1)} %get-tuple-element.22.other_ref), channel_id=1, source_target_pairs={{0,120},{8,16},{16,8},{24,32},{32,24},{40,48},{48,40},{56,64},{64,... | collective-permute-start | bytes 184328 | tf_op jit(solution)/shard_map/ppermute | solution.py:632
  6.4 14.6 %all-to-all-start = ((f32[16,1,128]{2,1,0:T(1,128)}), f32[16,1,128]{2,1,0:T(1,128)S(1)}, u32[]{:S(2)}, u32[]{:S(2)}) async-start(f32[16,1,128]{2,1,0:T(1,128)} %bitcast.43), calls=%async_computation | async-start | bytes 16384 | tf_op jit(solution)/shard_map/all_to_all | solution.py:622
  21.0 0.6 copy-start.5
  21.0 0.6 copy-start.2
  21.0 0.7 copy-start.3
  24.1 5.3 %copy-start.9 = (s32[2]{0:T(128)S(1)}, s32[2]{0:T(128)}, u32[]{:S(2)}) copy-start(s32[2]{0:T(128)} %param.15) | copy-start | bytes 28
  24.1 5.4 %copy-start.10 = (s32[2]{0:T(128)S(1)}, s32[2]{0:T(128)}, u32[]{:S(2)}) copy-start(s32[2]{0:T(128)} %param.16) | copy-start | bytes 28
  24.1 5.5 %copy-start.8 = (f32[2,640]{1,0:T(2,128)S(1)}, f32[2,640]{1,0:T(2,128)}, u32[]{:S(2)}) copy-start(f32[2,640]{1,0:T(2,128)} %param.19) | copy-start | bytes 15364
  24.2 37.7 %all-to-all-start.1 = ((bf16[8,16,80,128]{3,2,1,0:T(8,128)(2,1)}), bf16[8,16,80,128]{3,2,1,0:T(8,128)(2,1)}, u32[]{:S(2)}, u32[]{:S(2)}) async-start(bf16[8,16,80,128]{3,2,1,0:T(8,128)(2,1)} %pack_halo.1), calls=%async_computation.1 | async-start | bytes 5242880 | tf_op jit(solution)/shard_map/all_to_all | solution.py:636
  29.5 4.1 %copy-start.1 = (f32[320,1280]{1,0:T(8,128)S(1)}, f32[320,1280]{1,0:T(8,128)}, u32[]{:S(2)}) copy-start(f32[320,1280]{1,0:T(8,128)} %param.21) | copy-start | bytes 4915204
  33.6 2.5 %copy-start.6 = (f32[2,640]{1,0:T(2,128)S(1)}, f32[2,640]{1,0:T(2,128)}, u32[]{:S(2)}) copy-start(f32[2,640]{1,0:T(2,128)} %param.18) | copy-start | bytes 15364
  33.6 2.5 %copy-start.7 = (f32[2,640]{1,0:T(2,128)S(1)}, f32[2,640]{1,0:T(2,128)}, u32[]{:S(2)}) copy-start(f32[2,640]{1,0:T(2,128)} %param.20) | copy-start | bytes 15364
  83.9 22.9 %collective-permute-start.2 = (bf16[640,128]{1,0:T(8,128)(2,1)}, bf16[640,128]{1,0:T(8,128)(2,1)S(1)}, u32[]{:S(2)}, u32[]{:S(2)}) collective-permute-start(bf16[640,128]{1,0:T(8,128)(2,1)} %get-tuple-element.31), channel_id=1, source_target_pairs={{0,1},{1,0},{2,3},{3,2},{4,5},{5,4},{6,7},{7,6},{8,9},{9,8},{10,11... | collective-permute-start | bytes 491528 | tf_op jit(solution)/shard_map/ppermute | solution.py:632
  84.0 22.8 %collective-permute-start.3 = (bf16[640,128]{1,0:T(8,128)(2,1)}, bf16[640,128]{1,0:T(8,128)(2,1)}, u32[]{:S(2)}, u32[]{:S(2)}) collective-permute-start(bf16[640,128]{1,0:T(8,128)(2,1)} %get-tuple-element.32), channel_id=1, source_target_pairs={{1,2},{2,1},{3,4},{4,3},{5,6},{6,5},{9,10},{10,9},{11,12},{12,11},... | collective-permute-start | bytes 491528 | tf_op jit(solution)/shard_map/ppermute | solution.py:632
  85.4 21.4 %all-to-all-start.2 = ((f32[128,1,128]{2,1,0:T(1,128)}), f32[128,1,128]{2,1,0:T(1,128)S(1)}, u32[]{:S(2)}, u32[]{:S(2)}) async-start(f32[128,1,128]{2,1,0:T(1,128)} %bitcast.40), calls=%async_computation.2 | async-start | bytes 131072 | tf_op jit(solution)/shard_map/all_to_all | solution.py:622
  106.8 0.6 copy-start.4
  106.8 0.7 copy-start.11

commit v5 on v4

--- a/solution.py
+++ b/solution.py
@@ -213,7 +213,7 @@
         one, other = from_one[s].astype(F32), from_other[s].astype(F32)
         left, right = jnp.where(even, other, one), jnp.where(even, one, other)
         near = [left[0], left[1], first[0], last[1], right[0], right[1]]
-        near = [jnp.concatenate([col, pad], axis=1) for col in near]
+        near = [jnp.concatenate([col, pad], axis=1).astype(BF16) for col in near]
         carried = jnp.zeros((PART, 128), F32)
         for k in range(2):
             own = members(PART, 0, 64 * k + 32 * s)
@@ -222,12 +222,13 @@
                 part = value.astype(BF16).astype(F32)
                 carried = jnp.where(lane == SUMS + 3 * k + piece, part, carried)
                 value = value - part
+        carried = carried.astype(BF16)
         for d in range(SRC):
             halo = carried
             for kind in range(6):
                 own = (lane >= 16 * kind) & (lane < 16 * kind + 16)
                 halo = jnp.where(own, roll(near[kind], 16 * kind + 2 - d * ROWS), halo)
-            out[s, d] = halo.astype(BF16)
+            out[s, d] = halo
         pltpu.make_async_copy(out.at[s], pay_hbm.at[:, 8 * s + 7], sems.at[s]).start()
 
     for s in range(2):
@@ -623,12 +624,10 @@
     return got.reshape(-1, 128)
 
 
-def swap_neighbours(one, other, axis, wrap):
+def swap_neighbours(one, other, axis):
     size = lax.axis_size(axis)
     pairs = [(i, i ^ 1) for i in range(size)]
     rest = [(i, (i + 1 if i % 2 else i - 1) % size) for i in range(size)]
-    if not wrap:
-        rest = rest[1:-1]
     return lax.ppermute(one, axis, pairs), lax.ppermute(other, axis, rest)
 
 
@@ -660,7 +659,7 @@
     place = lax.axis_index("lon").astype(jnp.int32).reshape(1)
     sums, *ours = local_sums(place, cells)
     sums = everywhere(sums, "lon")
-    theirs = swap_neighbours(*ours, "lon", True)
+    theirs = swap_neighbours(*ours, "lon")
     pay = pack(after(cells, ours[0]))
     pay = pack_halo(place, sums, ours, theirs, pay)
     recv = swap(pay, "ch")
@@ -686,7 +685,7 @@
     hidden, sums, one, other, near = first_conv(
         part, params, first_pick, tap_pick, recv, turned[0]
     )
-    one, other = swap_neighbours(one, other, "ch", False)
+    one, other = swap_neighbours(one, other, "ch")
     sums = everywhere(sums, ("lon", "ch"))
     noise, terms = second_conv(
         part, coef, sums, params, second_pick, (near, one, other),

time: 144 us -> 142 us (0.986)
  starting transfers between devices: 28.9 us -> 27 us
    all_to_all x2, starting transfers between devices: 19.4 us -> 16.9 us  [everywhere(): got = lax.all_to_all(rows.reshape(-1, 1, 128), axes, 0, 0, tiled=True)]
where the time goes in v5:
time: 142 us; the launch traced here: 141 us
  Pallas kernels  71.4 us (50%)
  starting transfers between devices  27 us (19%)
  waiting for transfers between devices  19.8 us (14%)
  blocking collectives  14.1 us (10%)
  local copies, waits for them, and re-layouts  4.84 us (3%)
  matrix products  2.51 us (2%)
    pallas_call x1, Pallas kernels, first_conv(): pl.pallas_call(first_kernel, in_specs=[SMEM] + [VMEM] * 3 + [ANY] * 2, ou...  22 us
    pallas_call x1, Pallas kernels, second_conv(): pl.pallas_call(second_kernel, in_specs=[SMEM, SMEM] + [VMEM] * 6 + [ANY]...  21.1 us
    all_to_all x2, starting transfers between devices, everywhere(): got = lax.all_to_all(rows.reshape(-1, 1, 128), axes, 0, 0, tiled=True)  16.9 us
    all_to_all x1, blocking collectives, everywhere(): got = lax.all_to_all(rows.reshape(-1, 1, 128), axes, 0, 0, tiled=True)  14.1 us
    pallas_call x2, Pallas kernels, turn_weights(): pl.pallas_call(functools.partial(weight_kernel, j), in_specs=[ANY], out_s...  12.7 us
    all_to_all x1, waiting for transfers between devices, swap(): return lax.all_to_all(array, axis, split_axis=0, concat_axis=0, tiled=True)  10.4 us
    all_to_all x2, waiting for transfers between devices, everywhere(): got = lax.all_to_all(rows.reshape(-1, 1, 128), axes, 0, 0, tiled=True)  9.41 us
    pallas_call x1, Pallas kernels, pack(): pl.pallas_call(pack_kernel, in_specs=[ANY], out_specs=ANY, out_shape=jax....  6.45 us
  transfers between devices with their start and end apart: 7, of which 3 were waited for; matrix products, arithmetic and copies ran while one was open for 4% of the time, Pallas kernels for 16%

profile of v5, /device:TPU:1, one launch (start us, length us, event | category | flops | bytes accessed | tf_op | source)
XLA Modules:
  0.0 141.5 jit_solution(5433863616565264227)
XLA Ops:
  0.6 0.0 copy-start
  0.7 2.9 %local_sums.1 = (f32[16,128]{1,0:T(8,128)}, bf16[2,2,80,96]{3,2,1,0:T(8,128)(2,1)}, bf16[2,2,80,96]{3,2,1,0:T(8,128)(2,1)}) custom-call(s32[1]{0:T(128)} %bitcast.8.place_ref, bf16[2,64,80,96]{3,2,1,0:T(8,128)(2,1)} %bitcast.37), custom_call_target="tpu_custom_call" | custom-call | tf_op jit(solution)/shard_map/local_sums/pallas_call | solution.py:120
  3.6 1.5 %collective-permute-start = (bf16[2,2,80,96]{3,2,1,0:T(8,128)(2,1)}, bf16[2,2,80,96]{3,2,1,0:T(8,128)(2,1)S(1)}, u32[]{:S(2)}, u32[]{:S(2)}) collective-permute-start(bf16[2,2,80,96]{3,2,1,0:T(8,128)(2,1)} %get-tuple-element.21.one_ref), channel_id=1, source_target_pairs={{0,8},{8,0},{16,24},{24,16},{32,40},{40,32},{48,56},{56,48},{64,72... | collective-permute-start | bytes 184328 | tf_op jit(solution)/shard_map/ppermute | solution.py:631
  5.1 1.3 collective-permute-start.1
  6.4 7.6 %all-to-all-start = ((f32[16,1,128]{2,1,0:T(1,128)}), f32[16,1,128]{2,1,0:T(1,128)S(1)}, u32[]{:S(2)}, u32[]{:S(2)}) async-start(f32[16,1,128]{2,1,0:T(1,128)} %bitcast.43), calls=%async_computation | async-start | bytes 16384 | tf_op jit(solution)/shard_map/all_to_all | solution.py:623
  14.0 6.4 %pack_latents.1._ = bf16[8,16,80,128]{3,2,1,0:T(8,128)(2,1)} custom-call(bf16[2,64,80,96]{3,2,1,0:T(8,128)(2,1)} %bitcast.38), custom_call_target="tpu_custom_call" | custom-call | flops 1000000000 | bytes 8000000 | tf_op jit(solution)/shard_map/pack_latents/pallas_call | solution.py:181
  20.4 0.6 all-to-all-done
  21.0 0.0 copy-start.5
  21.0 0.0 collective-permute-done.from_one
  21.0 0.0 copy-start.2
  21.0 0.0 collective-permute-done.1.from_other
  21.0 0.0 copy-start.3
  21.0 0.6 copy-done.5
  21.6 0.1 copy-done.2
  21.7 0.0 copy-done.3
  21.7 2.4 %pack_halo.1 = bf16[8,16,80,128]{3,2,1,0:T(8,128)(2,1)} custom-call(s32[1]{0:T(128)} %bitcast.8.place_ref, f32[16,128]{1,0:T(8,128)} %bitcast.42, bf16[2,2,80,96]{3,2,1,0:T(8,128)(2,1)} %get-tuple-element.21.one_ref, bf16[2,2,80,96]{3,2,1,0:T(8,128)(2,1)} %get-tuple-element.22.other_ref, ...), custom_call_target="tpu_custom_call", output_to_operand_aliasing={{}: (6, {})} | custom-call | tf_op jit(solution)/shard_map/pack_halo/pallas_call | solution.py:239
  24.1 0.0 copy-start.9
  24.1 0.0 copy-start.10
  24.1 0.0 copy-start.8
  24.2 5.3 %all-to-all-start.1 = ((bf16[8,16,80,128]{3,2,1,0:T(8,128)(2,1)}), bf16[8,16,80,128]{3,2,1,0:T(8,128)(2,1)}, u32[]{:S(2)}, u32[]{:S(2)}) async-start(bf16[8,16,80,128]{3,2,1,0:T(8,128)(2,1)} %pack_halo.1), calls=%async_computation.1 | async-start | bytes 5242880 | tf_op jit(solution)/shard_map/all_to_all | solution.py:635
  29.5 0.0 copy-done.9
  29.5 0.0 copy-start.1
  29.5 0.0 copy-done.10
  29.5 0.1 fusion.11
  29.6 0.1 multiply_cosine_fusion
  29.7 0.0 copy-done.8
  29.7 3.9 %turn_target.1.target_hbm = bf16[2,6,640,128]{3,2,1,0:T(8,128)(2,1)} custom-call(bf16[12,2,64,640]{3,2,1,0:T(8,128)(2,1)} %target_hbm), custom_call_target="tpu_custom_call" | custom-call | tf_op jit(solution)/shard_map/turn_target/pallas_call | solution.py:305
  33.6 0.0 copy-start.6
  33.6 0.0 copy-start.7
  33.6 0.0 copy-done.1
  33.6 0.8 fusion.5
  34.4 0.0 copy-done
  34.4 1.7 %fusion = f32[2,640]{1,0:T(2,128)S(1)} fusion(f32[1280,640]{1,0:T(8,128)S(1)} %copy-done, f32[2,1280]{1,0:T(2,128)S(1)} %fusion.5), kind=kOutput, calls=%fused_computation.1 | convolution fusion | flops 19671040 | bytes 3292160 | tf_op jit(solution)/shard_map/dot_general | solution.py:614
  36.1 0.0 copy-done.6
  36.1 0.0 copy-done.7
  36.2 0.9 copy.27
  37.1 1.7 %pad.4.par_ref = f32[640,128]{1,0:T(8,128)} pad(f32[640,7]{1,0:T(8,128)} %copy.27, f32[]{:T(128)} %constant.46.clone.1), padding=0_0x0_121 | pad | bytes 345604 | tf_op jit(solution)/shard_map/jit(_pad)/pad | solution.py:675
  38.8 6.3 %turn_weights_0.1.w_hbm = bf16[640,5760]{1,0:T(8,128)(2,1)} custom-call(bf16[2,9,640,640]{3,2,1,0:T(8,128)(2,1)} %bitcast.35), custom_call_target="tpu_custom_call" | custom-call | flops 1887436800 | bytes 15000000 | tf_op jit(solution)/shard_map/turn_weights_0/pallas_call | solution.py:271
  45.2 6.4 %turn_weights_1.1.w_hbm = bf16[640,5760]{1,0:T(8,128)(2,1)} custom-call(bf16[2,9,640,640]{3,2,1,0:T(8,128)(2,1)} %bitcast.36), custom_call_target="tpu_custom_call" | custom-call | flops 1887436800 | bytes 15000000 | tf_op jit(solution)/shard_map/turn_weights_1/pallas_call | solution.py:271
  51.5 10.4 %all-to-all-done.1.recv_hbm = bf16[8,16,80,128]{3,2,1,0:T(8,128)(2,1)} async-done(((bf16[8,16,80,128]{3,2,1,0:T(8,128)(2,1)}), bf16[8,16,80,128]{3,2,1,0:T(8,128)(2,1)}, u32[]{:S(2)}, u32[]{:S(2)}) %all-to-all-start.1) | async-done | bytes 2621472 | tf_op jit(solution)/shard_map/all_to_all | solution.py:635
  61.9 22.0 %first_conv.1 = (f32[2,640,768]{2,1,0:T(8,128)}, f32[128,128]{1,0:T(8,128)}, bf16[640,128]{1,0:T(8,128)(2,1)}, bf16[640,128]{1,0:T(8,128)(2,1)}, bf16[640,128]{1,0:T(8,128)(2,1)}) custom-call(s32[1]{0:T(128)} %bitcast.part_ref, f32[640,128]{1,0:T(8,128)} %pad.4.par_ref, bf16[128,128]{1,0:T(8,128)(2,1)} %constant.51.clone.pick_ref, ...), custom_call_target="tpu_custom_call" | custom-call | flops 11324620800 | bytes 20000000 | tf_op jit(solution)/shard_map/first_conv/pallas_call | solution.py:460
  83.9 0.1 collective-permute-start.2
  84.0 1.9 %collective-permute-start.3 = (bf16[640,128]{1,0:T(8,128)(2,1)}, bf16[640,128]{1,0:T(8,128)(2,1)}, u32[]{:S(2)}, u32[]{:S(2)}) collective-permute-start(bf16[640,128]{1,0:T(8,128)(2,1)} %get-tuple-element.32), channel_id=1, source_target_pairs={{0,7},{1,2},{2,1},{3,4},{4,3},{5,6},{6,5},{7,0},{8,15},{9,10},{10,... | collective-permute-start | bytes 491528 | tf_op jit(solution)/shard_map/ppermute | solution.py:631
  85.9 0.1 subtract_bitcast_fusion
  86.0 9.3 %all-to-all-start.2 = ((f32[128,1,128]{2,1,0:T(1,128)}), f32[128,1,128]{2,1,0:T(1,128)S(1)}, u32[]{:S(2)}, u32[]{:S(2)}) async-start(f32[128,1,128]{2,1,0:T(1,128)} %bitcast.40), calls=%async_computation.2 | async-start | bytes 131072 | tf_op jit(solution)/shard_map/all_to_all | solution.py:623
  95.3 0.1 copy.25
  95.4 0.7 reshape.76.coef_ref
  96.1 8.8 %all-to-all-done.2 = f32[128,1,128]{2,1,0:T(1,128)S(1)} async-done(((f32[128,1,128]{2,1,0:T(1,128)}), f32[128,1,128]{2,1,0:T(1,128)S(1)}, u32[]{:S(2)}, u32[]{:S(2)}) %all-to-all-start.2) | async-done | bytes 65568 | tf_op jit(solution)/shard_map/all_to_all | solution.py:623
  104.9 0.0 copy-start.4
  104.9 0.0 collective-permute-done.2.one_ref
  104.9 0.0 copy-start.11
  104.9 0.0 collective-permute-done.3.other_ref
  104.9 0.6 copy-done.4
  105.5 0.1 copy-done.11
  105.6 21.1 %second_conv.1 = (bf16[12,2,64,640]{3,2,1,0:T(8,128)(2,1)}, f32[128,128]{1,0:T(8,128)}) custom-call(s32[1]{0:T(128)} %bitcast.part_ref, f32[4]{0:T(128)} %reshape.76.coef_ref, f32[128,128]{1,0:T(8,128)} %bitcast.39, f32[640,128]{1,0:T(8,128)} %pad.4.par_ref, bf16[2,128,128]{2,1,0:T(8,128)(2,1)} %constant.52.clone.pick_ref, ...), custom_call_target="tpu_custom_call" | custom-call | flops 11324620800 | bytes 20000000 | tf_op jit(solution)/shard_map/second_conv/pallas_call | solution.py:580
  126.7 14.1 %all_to_all.20 = f32[128,1,128]{2,1,0:T(1,128)S(1)} all-to-all(f32[128,1,128]{2,1,0:T(1,128)} %bitcast.41), channel_id=1, replica_groups=mesh['lon'=16,'ch'=8] {'lon','ch'}, dimensions={0} | all-to-all | bytes 131072 | tf_op jit(solution)/shard_map/all_to_all | solution.py:623
  140.8 0.2 reduce_sum.9
  140.9 0.6 subtract_add_fusion
  (6 shorter events, 0.1 us)
Async XLA Ops:
  0.6 33.8 %copy-start = (f32[1280,640]{1,0:T(8,128)S(1)}, f32[1280,640]{1,0:T(8,128)}, u32[]{:S(2)}) copy-start(f32[1280,640]{1,0:T(8,128)} %param.22) | copy-start | bytes 9830404
  3.6 17.4 %collective-permute-start = (bf16[2,2,80,96]{3,2,1,0:T(8,128)(2,1)}, bf16[2,2,80,96]{3,2,1,0:T(8,128)(2,1)S(1)}, u32[]{:S(2)}, u32[]{:S(2)}) collective-permute-start(bf16[2,2,80,96]{3,2,1,0:T(8,128)(2,1)} %get-tuple-element.21.one_ref), channel_id=1, source_target_pairs={{0,8},{8,0},{16,24},{24,16},{32,40},{40,32},{48,56},{56,48},{64,72... | collective-permute-start | bytes 184328 | tf_op jit(solution)/shard_map/ppermute | solution.py:631
  5.1 15.9 %collective-permute-start.1 = (bf16[2,2,80,96]{3,2,1,0:T(8,128)(2,1)}, bf16[2,2,80,96]{3,2,1,0:T(8,128)(2,1)S(1)}, u32[]{:S(2)}, u32[]{:S(2)}) collective-permute-start(bf16[2,2,80,96]{3,2,1,0:T(8,128)(2,1)} %get-tuple-element.22.other_ref), channel_id=1, source_target_pairs={{0,120},{8,16},{16,8},{24,32},{32,24},{40,48},{48,40},{56,64},{64,... | collective-permute-start | bytes 184328 | tf_op jit(solution)/shard_map/ppermute | solution.py:631
  6.4 14.6 %all-to-all-start = ((f32[16,1,128]{2,1,0:T(1,128)}), f32[16,1,128]{2,1,0:T(1,128)S(1)}, u32[]{:S(2)}, u32[]{:S(2)}) async-start(f32[16,1,128]{2,1,0:T(1,128)} %bitcast.43), calls=%async_computation | async-start | bytes 16384 | tf_op jit(solution)/shard_map/all_to_all | solution.py:623
  21.0 0.6 copy-start.5
  21.0 0.6 copy-start.2
  21.0 0.7 copy-start.3
  24.1 5.3 %copy-start.9 = (s32[2]{0:T(128)S(1)}, s32[2]{0:T(128)}, u32[]{:S(2)}) copy-start(s32[2]{0:T(128)} %param.15) | copy-start | bytes 28
  24.1 5.4 %copy-start.10 = (s32[2]{0:T(128)S(1)}, s32[2]{0:T(128)}, u32[]{:S(2)}) copy-start(s32[2]{0:T(128)} %param.16) | copy-start | bytes 28
  24.1 5.5 %copy-start.8 = (f32[2,640]{1,0:T(2,128)S(1)}, f32[2,640]{1,0:T(2,128)}, u32[]{:S(2)}) copy-start(f32[2,640]{1,0:T(2,128)} %param.19) | copy-start | bytes 15364
  24.2 37.7 %all-to-all-start.1 = ((bf16[8,16,80,128]{3,2,1,0:T(8,128)(2,1)}), bf16[8,16,80,128]{3,2,1,0:T(8,128)(2,1)}, u32[]{:S(2)}, u32[]{:S(2)}) async-start(bf16[8,16,80,128]{3,2,1,0:T(8,128)(2,1)} %pack_halo.1), calls=%async_computation.1 | async-start | bytes 5242880 | tf_op jit(solution)/shard_map/all_to_all | solution.py:635
  29.5 4.1 %copy-start.1 = (f32[320,1280]{1,0:T(8,128)S(1)}, f32[320,1280]{1,0:T(8,128)}, u32[]{:S(2)}) copy-start(f32[320,1280]{1,0:T(8,128)} %param.21) | copy-start | bytes 4915204
  33.6 2.5 %copy-start.6 = (f32[2,640]{1,0:T(2,128)S(1)}, f32[2,640]{1,0:T(2,128)}, u32[]{:S(2)}) copy-start(f32[2,640]{1,0:T(2,128)} %param.18) | copy-start | bytes 15364
  33.6 2.5 %copy-start.7 = (f32[2,640]{1,0:T(2,128)S(1)}, f32[2,640]{1,0:T(2,128)}, u32[]{:S(2)}) copy-start(f32[2,640]{1,0:T(2,128)} %param.20) | copy-start | bytes 15364
  83.9 21.0 %collective-permute-start.2 = (bf16[640,128]{1,0:T(8,128)(2,1)}, bf16[640,128]{1,0:T(8,128)(2,1)S(1)}, u32[]{:S(2)}, u32[]{:S(2)}) collective-permute-start(bf16[640,128]{1,0:T(8,128)(2,1)} %get-tuple-element.31), channel_id=1, source_target_pairs={{0,1},{1,0},{2,3},{3,2},{4,5},{5,4},{6,7},{7,6},{8,9},{9,8},{10,11... | collective-permute-start | bytes 491528 | tf_op jit(solution)/shard_map/ppermute | solution.py:631
  84.0 20.9 %collective-permute-start.3 = (bf16[640,128]{1,0:T(8,128)(2,1)}, bf16[640,128]{1,0:T(8,128)(2,1)}, u32[]{:S(2)}, u32[]{:S(2)}) collective-permute-start(bf16[640,128]{1,0:T(8,128)(2,1)} %get-tuple-element.32), channel_id=1, source_target_pairs={{0,7},{1,2},{2,1},{3,4},{4,3},{5,6},{6,5},{7,0},{8,15},{9,10},{10,... | collective-permute-start | bytes 491528 | tf_op jit(solution)/shard_map/ppermute | solution.py:631
  86.0 18.9 %all-to-all-start.2 = ((f32[128,1,128]{2,1,0:T(1,128)}), f32[128,1,128]{2,1,0:T(1,128)S(1)}, u32[]{:S(2)}, u32[]{:S(2)}) async-start(f32[128,1,128]{2,1,0:T(1,128)} %bitcast.40), calls=%async_computation.2 | async-start | bytes 131072 | tf_op jit(solution)/shard_map/all_to_all | solution.py:623
  104.9 0.6 copy-start.4
  104.9 0.7 copy-start.11

commit v6 on v5

--- a/solution.py
+++ b/solution.py
@@ -362,14 +362,14 @@
 def first_kernel(
     part_ref, par_ref, pick_ref, taps_ref, recv_hbm, w_hbm,
     hid_hbm, out_sums, one, other, out_halo,
-    xs, wv, scale, offset, recv, hid, sides, xh, sems,
+    xs, wv, scale, offset, recv, hid, sides, xh, added, sems,
 ):
     fetches = [
         pltpu.make_async_copy(recv_hbm.at[:, 8 * s : 8 * s + 8], recv.at[s], sems.at[s])
         for s in range(2)
     ]
     weights = pltpu.make_async_copy(w_hbm, wv, sems.at[2])
-    for copy in (fetches[0], weights, fetches[1]):
+    for copy in (*fetches, weights):
         copy.start()
     part = part_ref[0]
     lane = lanes(C)
@@ -399,6 +399,8 @@
         tiles = [act(recv[s, b, q], a, o) for q in range(7)]
         spread_taps(xs.at[s], at, tiles[:6], tiles[6], sides.at[s], part)
 
+    for s in range(2):
+        added[s] = jnp.broadcast_to(par_ref[:, 5 + s : 6 + s], (C, 128))
     halo = columns(0)
 
     @pl.loop(0, SRC)
@@ -416,7 +418,8 @@
 
     def put(s, n, value):
         part = hid.at[s, :, n : n + 256]
-        part[...] = value + par_ref[:, 5 + s : 6 + s]
+        for h in range(0, 256, 128):
+            hid[s, :, n + h : n + h + 128] = value[:, h : h + 128] + added[s]
         store = pltpu.make_async_copy(
             part, hid_hbm.at[s, :, n : n + 256], sems.at[3 + 3 * s + n // 256]
         )
@@ -432,7 +435,7 @@
     put(1, 256, product(wv, xs.at[1], 256))
     out = product(wv, xs.at[1], 512, xh[...])
     put(1, 512, out[:, 0:256])
-    bias = jnp.where(lane < 32, par_ref[:, 5:6], par_ref[:, 6:7])
+    bias = jnp.where(lane < 32, added[0], added[1])
     out_halo[...] = (out[:, 256:384] + bias).astype(BF16)
 
     row = jnp.zeros((1, 128), F32)
@@ -475,6 +478,7 @@
             pltpu.VMEM((2, C, 768), F32),
             pltpu.VMEM((2, C, 128), BF16),
             pltpu.VMEM((TAPS * C, 128), BF16),
+            pltpu.VMEM((2, C, 128), F32),
             pltpu.SemaphoreType.DMA((9,)),
         ],
         compiler_params=PARAMS,
@@ -489,7 +493,7 @@
     part_ref, coef_ref, sums_ref, par_ref, pick_ref, near_ref, one_ref, other_ref,
     hid_hbm, w_hbm, recv_hbm, target_hbm,
     noise_hbm, out_ref,
-    xs, wv, hid, lat, target, noise_out, sides, scale, offset, sems,
+    xs, wv, hid, lat, target, noise_out, sides, scale, offset, added, sems,
 ):
     weights = pltpu.make_async_copy(w_hbm, wv, sems.at[6])
     fetches, later = [], []
@@ -534,11 +538,11 @@
 
     def finish(s, n, acc):
         keep, gain = coef_ref[2 * s], coef_ref[2 * s + 1]
-        out = product(wv, xs.at[s], n) + par_ref[:, 4:5]
+        out = product(wv, xs.at[s], n)
         for h in range(2):
             q = n // 128 + h
             mine = lat[s, :, q].reshape(C, 128).astype(F32)
-            noise = (out[:, 128 * h : 128 * h + 128] + mine).astype(BF16)
+            noise = (out[:, 128 * h : 128 * h + 128] + added[...] + mine).astype(BF16)
             center = keep * mine + gain * noise.astype(F32)
             diff = target[s, q].astype(F32) - center
             acc += jnp.sum((diff * diff).reshape(C // 8, 8, 128), axis=0)
@@ -547,6 +551,7 @@
             noise_out[s, q + 6] = plain[64:128]
         return acc
 
+    added[...] = jnp.broadcast_to(par_ref[:, 4:5], added.shape)
     columns(0)
 
     @pl.loop(0, SRC)
@@ -595,6 +600,7 @@
             pltpu.VMEM((2, C, 128), BF16),
             pltpu.VMEM((2, C, 128), F32),
             pltpu.VMEM((2, C, 128), F32),
+            pltpu.VMEM((C, 128), F32),
             pltpu.SemaphoreType.DMA((9,)),
         ],
         compiler_params=PARAMS,

time: 142 us -> 142 us (level)
  no operation moved by 1% of the time
where the time goes in v6:
time: 142 us; the launch traced here: 141 us
  Pallas kernels  71.4 us (50%)
  starting transfers between devices  27 us (19%)
  waiting for transfers between devices  19.8 us (14%)
  blocking collectives  14.1 us (10%)
  local copies, waits for them, and re-layouts  4.84 us (3%)
  matrix products  2.51 us (2%)
    pallas_call x1, Pallas kernels, first_conv(): pl.pallas_call(first_kernel, in_specs=[SMEM] + [VMEM] * 3 + [ANY] * 2, ou...  22 us
    pallas_call x1, Pallas kernels, second_conv(): pl.pallas_call(second_kernel, in_specs=[SMEM, SMEM] + [VMEM] * 6 + [ANY]...  21 us
    all_to_all x2, starting transfers between devices, everywhere(): got = lax.all_to_all(rows.reshape(-1, 1, 128), axes, 0, 0, tiled=True)  16.7 us
    all_to_all x1, blocking collectives, everywhere(): got = lax.all_to_all(rows.reshape(-1, 1, 128), axes, 0, 0, tiled=True)  14.1 us
    pallas_call x2, Pallas kernels, turn_weights(): pl.pallas_call(functools.partial(weight_kernel, j), in_specs=[ANY], out_s...  12.7 us
    all_to_all x1, waiting for transfers between devices, swap(): return lax.all_to_all(array, axis, split_axis=0, concat_axis=0, tiled=True)  10.4 us
    all_to_all x2, waiting for transfers between devices, everywhere(): got = lax.all_to_all(rows.reshape(-1, 1, 128), axes, 0, 0, tiled=True)  9.41 us
    pallas_call x1, Pallas kernels, pack(): pl.pallas_call(pack_kernel, in_specs=[ANY], out_specs=ANY, out_shape=jax....  6.45 us
  transfers between devices with their start and end apart: 7, of which 3 were waited for; matrix products, arithmetic and copies ran while one was open for 4% of the time, Pallas kernels for 16%

profile of v6, /device:TPU:1, one launch (start us, length us, event | category | flops | bytes accessed | tf_op | source)
XLA Modules:
  0.0 141.5 jit_solution(7158795760079846625)
XLA Ops:
  0.6 0.0 copy-start
  0.7 2.9 %local_sums.1 = (f32[16,128]{1,0:T(8,128)}, bf16[2,2,80,96]{3,2,1,0:T(8,128)(2,1)}, bf16[2,2,80,96]{3,2,1,0:T(8,128)(2,1)}) custom-call(s32[1]{0:T(128)} %bitcast.8.place_ref, bf16[2,64,80,96]{3,2,1,0:T(8,128)(2,1)} %bitcast.37), custom_call_target="tpu_custom_call" | custom-call | tf_op jit(solution)/shard_map/local_sums/pallas_call | solution.py:120
  3.6 1.5 %collective-permute-start = (bf16[2,2,80,96]{3,2,1,0:T(8,128)(2,1)}, bf16[2,2,80,96]{3,2,1,0:T(8,128)(2,1)S(1)}, u32[]{:S(2)}, u32[]{:S(2)}) collective-permute-start(bf16[2,2,80,96]{3,2,1,0:T(8,128)(2,1)} %get-tuple-element.21.one_ref), channel_id=1, source_target_pairs={{0,8},{8,0},{16,24},{24,16},{32,40},{40,32},{48,56},{56,48},{64,72... | collective-permute-start | bytes 184328 | tf_op jit(solution)/shard_map/ppermute | solution.py:637
  5.1 1.3 collective-permute-start.1
  6.4 7.6 %all-to-all-start = ((f32[16,1,128]{2,1,0:T(1,128)}), f32[16,1,128]{2,1,0:T(1,128)S(1)}, u32[]{:S(2)}, u32[]{:S(2)}) async-start(f32[16,1,128]{2,1,0:T(1,128)} %bitcast.43), calls=%async_computation | async-start | bytes 16384 | tf_op jit(solution)/shard_map/all_to_all | solution.py:629
  14.0 6.4 %pack_latents.1._ = bf16[8,16,80,128]{3,2,1,0:T(8,128)(2,1)} custom-call(bf16[2,64,80,96]{3,2,1,0:T(8,128)(2,1)} %bitcast.38), custom_call_target="tpu_custom_call" | custom-call | flops 1000000000 | bytes 8000000 | tf_op jit(solution)/shard_map/pack_latents/pallas_call | solution.py:181
  20.4 0.6 all-to-all-done
  21.0 0.0 copy-start.5
  21.0 0.0 collective-permute-done.from_one
  21.0 0.0 copy-start.2
  21.0 0.0 collective-permute-done.1.from_other
  21.0 0.0 copy-start.3
  21.0 0.6 copy-done.5
  21.6 0.1 copy-done.2
  21.7 0.0 copy-done.3
  21.7 2.4 %pack_halo.1 = bf16[8,16,80,128]{3,2,1,0:T(8,128)(2,1)} custom-call(s32[1]{0:T(128)} %bitcast.8.place_ref, f32[16,128]{1,0:T(8,128)} %bitcast.42, bf16[2,2,80,96]{3,2,1,0:T(8,128)(2,1)} %get-tuple-element.21.one_ref, bf16[2,2,80,96]{3,2,1,0:T(8,128)(2,1)} %get-tuple-element.22.other_ref, ...), custom_call_target="tpu_custom_call", output_to_operand_aliasing={{}: (6, {})} | custom-call | tf_op jit(solution)/shard_map/pack_halo/pallas_call | solution.py:239
  24.1 0.0 copy-start.9
  24.1 0.0 copy-start.10
  24.1 0.0 copy-start.8
  24.2 5.3 %all-to-all-start.1 = ((bf16[8,16,80,128]{3,2,1,0:T(8,128)(2,1)}), bf16[8,16,80,128]{3,2,1,0:T(8,128)(2,1)}, u32[]{:S(2)}, u32[]{:S(2)}) async-start(bf16[8,16,80,128]{3,2,1,0:T(8,128)(2,1)} %pack_halo.1), calls=%async_computation.1 | async-start | bytes 5242880 | tf_op jit(solution)/shard_map/all_to_all | solution.py:641
  29.5 0.0 copy-done.9
  29.5 0.0 copy-start.1
  29.5 0.0 copy-done.10
  29.5 0.1 fusion.11
  29.6 0.1 multiply_cosine_fusion
  29.7 0.0 copy-done.8
  29.7 3.9 %turn_target.1.target_hbm = bf16[2,6,640,128]{3,2,1,0:T(8,128)(2,1)} custom-call(bf16[12,2,64,640]{3,2,1,0:T(8,128)(2,1)} %target_hbm), custom_call_target="tpu_custom_call" | custom-call | tf_op jit(solution)/shard_map/turn_target/pallas_call | solution.py:305
  33.6 0.0 copy-start.6
  33.6 0.0 copy-start.7
  33.6 0.0 copy-done.1
  33.6 0.8 fusion.5
  34.4 0.0 copy-done
  34.4 1.7 %fusion = f32[2,640]{1,0:T(2,128)S(1)} fusion(f32[1280,640]{1,0:T(8,128)S(1)} %copy-done, f32[2,1280]{1,0:T(2,128)S(1)} %fusion.5), kind=kOutput, calls=%fused_computation.1 | convolution fusion | flops 19671040 | bytes 3292160 | tf_op jit(solution)/shard_map/dot_general | solution.py:620
  36.1 0.0 copy-done.6
  36.1 0.0 copy-done.7
  36.2 0.9 copy.27
  37.1 1.7 %pad.4.par_ref = f32[640,128]{1,0:T(8,128)} pad(f32[640,7]{1,0:T(8,128)} %copy.27, f32[]{:T(128)} %constant.46.clone.1), padding=0_0x0_121 | pad | bytes 345604 | tf_op jit(solution)/shard_map/jit(_pad)/pad | solution.py:681
  38.8 6.3 %turn_weights_0.1.w_hbm = bf16[640,5760]{1,0:T(8,128)(2,1)} custom-call(bf16[2,9,640,640]{3,2,1,0:T(8,128)(2,1)} %bitcast.35), custom_call_target="tpu_custom_call" | custom-call | flops 1887436800 | bytes 15000000 | tf_op jit(solution)/shard_map/turn_weights_0/pallas_call | solution.py:271
  45.2 6.4 %turn_weights_1.1.w_hbm = bf16[640,5760]{1,0:T(8,128)(2,1)} custom-call(bf16[2,9,640,640]{3,2,1,0:T(8,128)(2,1)} %bitcast.36), custom_call_target="tpu_custom_call" | custom-call | flops 1887436800 | bytes 15000000 | tf_op jit(solution)/shard_map/turn_weights_1/pallas_call | solution.py:271
  51.5 10.4 %all-to-all-done.1.recv_hbm = bf16[8,16,80,128]{3,2,1,0:T(8,128)(2,1)} async-done(((bf16[8,16,80,128]{3,2,1,0:T(8,128)(2,1)}), bf16[8,16,80,128]{3,2,1,0:T(8,128)(2,1)}, u32[]{:S(2)}, u32[]{:S(2)}) %all-to-all-start.1) | async-done | bytes 2621472 | tf_op jit(solution)/shard_map/all_to_all | solution.py:641
  61.9 22.0 %first_conv.1 = (f32[2,640,768]{2,1,0:T(8,128)}, f32[128,128]{1,0:T(8,128)}, bf16[640,128]{1,0:T(8,128)(2,1)}, bf16[640,128]{1,0:T(8,128)(2,1)}, bf16[640,128]{1,0:T(8,128)(2,1)}) custom-call(s32[1]{0:T(128)} %bitcast.part_ref, f32[640,128]{1,0:T(8,128)} %pad.4.par_ref, bf16[128,128]{1,0:T(8,128)(2,1)} %constant.51.clone.pick_ref, ...), custom_call_target="tpu_custom_call" | custom-call | flops 11324620800 | bytes 20000000 | tf_op jit(solution)/shard_map/first_conv/pallas_call | solution.py:463
  83.9 0.1 collective-permute-start.2
  84.0 2.2 %collective-permute-start.3 = (bf16[640,128]{1,0:T(8,128)(2,1)}, bf16[640,128]{1,0:T(8,128)(2,1)}, u32[]{:S(2)}, u32[]{:S(2)}) collective-permute-start(bf16[640,128]{1,0:T(8,128)(2,1)} %get-tuple-element.32), channel_id=1, source_target_pairs={{0,7},{1,2},{2,1},{3,4},{4,3},{5,6},{6,5},{7,0},{8,15},{9,10},{10,... | collective-permute-start | bytes 491528 | tf_op jit(solution)/shard_map/ppermute | solution.py:637
  86.2 0.1 subtract_bitcast_fusion
  86.2 9.1 %all-to-all-start.2 = ((f32[128,1,128]{2,1,0:T(1,128)}), f32[128,1,128]{2,1,0:T(1,128)S(1)}, u32[]{:S(2)}, u32[]{:S(2)}) async-start(f32[128,1,128]{2,1,0:T(1,128)} %bitcast.40), calls=%async_computation.2 | async-start | bytes 131072 | tf_op jit(solution)/shard_map/all_to_all | solution.py:629
  95.3 0.1 copy.25
  95.4 0.7 reshape.76.coef_ref
  96.1 8.8 %all-to-all-done.2 = f32[128,1,128]{2,1,0:T(1,128)S(1)} async-done(((f32[128,1,128]{2,1,0:T(1,128)}), f32[128,1,128]{2,1,0:T(1,128)S(1)}, u32[]{:S(2)}, u32[]{:S(2)}) %all-to-all-start.2) | async-done | bytes 65568 | tf_op jit(solution)/shard_map/all_to_all | solution.py:629
  104.9 0.0 copy-start.4
  104.9 0.0 collective-permute-done.2.one_ref
  104.9 0.0 copy-start.11
  104.9 0.0 collective-permute-done.3.other_ref
  104.9 0.6 copy-done.4
  105.5 0.1 copy-done.11
  105.6 21.0 %second_conv.1 = (bf16[12,2,64,640]{3,2,1,0:T(8,128)(2,1)}, f32[128,128]{1,0:T(8,128)}) custom-call(s32[1]{0:T(128)} %bitcast.part_ref, f32[4]{0:T(128)} %reshape.76.coef_ref, f32[128,128]{1,0:T(8,128)} %bitcast.39, f32[640,128]{1,0:T(8,128)} %pad.4.par_ref, bf16[2,128,128]{2,1,0:T(8,128)(2,1)} %constant.52.clone.pick_ref, ...), custom_call_target="tpu_custom_call" | custom-call | flops 11324620800 | bytes 20000000 | tf_op jit(solution)/shard_map/second_conv/pallas_call | solution.py:585
  126.7 14.1 %all_to_all.20 = f32[128,1,128]{2,1,0:T(1,128)S(1)} all-to-all(f32[128,1,128]{2,1,0:T(1,128)} %bitcast.41), channel_id=1, replica_groups=mesh['lon'=16,'ch'=8] {'lon','ch'}, dimensions={0} | all-to-all | bytes 131072 | tf_op jit(solution)/shard_map/all_to_all | solution.py:629
  140.7 0.2 reduce_sum.9
  140.9 0.6 subtract_add_fusion
  (6 shorter events, 0.1 us)
Async XLA Ops:
  0.6 33.8 %copy-start = (f32[1280,640]{1,0:T(8,128)S(1)}, f32[1280,640]{1,0:T(8,128)}, u32[]{:S(2)}) copy-start(f32[1280,640]{1,0:T(8,128)} %param.22) | copy-start | bytes 9830404
  3.6 17.4 %collective-permute-start = (bf16[2,2,80,96]{3,2,1,0:T(8,128)(2,1)}, bf16[2,2,80,96]{3,2,1,0:T(8,128)(2,1)S(1)}, u32[]{:S(2)}, u32[]{:S(2)}) collective-permute-start(bf16[2,2,80,96]{3,2,1,0:T(8,128)(2,1)} %get-tuple-element.21.one_ref), channel_id=1, source_target_pairs={{0,8},{8,0},{16,24},{24,16},{32,40},{40,32},{48,56},{56,48},{64,72... | collective-permute-start | bytes 184328 | tf_op jit(solution)/shard_map/ppermute | solution.py:637
  5.1 15.9 %collective-permute-start.1 = (bf16[2,2,80,96]{3,2,1,0:T(8,128)(2,1)}, bf16[2,2,80,96]{3,2,1,0:T(8,128)(2,1)S(1)}, u32[]{:S(2)}, u32[]{:S(2)}) collective-permute-start(bf16[2,2,80,96]{3,2,1,0:T(8,128)(2,1)} %get-tuple-element.22.other_ref), channel_id=1, source_target_pairs={{0,120},{8,16},{16,8},{24,32},{32,24},{40,48},{48,40},{56,64},{64,... | collective-permute-start | bytes 184328 | tf_op jit(solution)/shard_map/ppermute | solution.py:637
  6.4 14.6 %all-to-all-start = ((f32[16,1,128]{2,1,0:T(1,128)}), f32[16,1,128]{2,1,0:T(1,128)S(1)}, u32[]{:S(2)}, u32[]{:S(2)}) async-start(f32[16,1,128]{2,1,0:T(1,128)} %bitcast.43), calls=%async_computation | async-start | bytes 16384 | tf_op jit(solution)/shard_map/all_to_all | solution.py:629
  21.0 0.6 copy-start.5
  21.0 0.6 copy-start.2
  21.0 0.7 copy-start.3
  24.1 5.3 %copy-start.9 = (s32[2]{0:T(128)S(1)}, s32[2]{0:T(128)}, u32[]{:S(2)}) copy-start(s32[2]{0:T(128)} %param.15) | copy-start | bytes 28
  24.1 5.4 %copy-start.10 = (s32[2]{0:T(128)S(1)}, s32[2]{0:T(128)}, u32[]{:S(2)}) copy-start(s32[2]{0:T(128)} %param.16) | copy-start | bytes 28
  24.1 5.5 %copy-start.8 = (f32[2,640]{1,0:T(2,128)S(1)}, f32[2,640]{1,0:T(2,128)}, u32[]{:S(2)}) copy-start(f32[2,640]{1,0:T(2,128)} %param.19) | copy-start | bytes 15364
  24.2 37.7 %all-to-all-start.1 = ((bf16[8,16,80,128]{3,2,1,0:T(8,128)(2,1)}), bf16[8,16,80,128]{3,2,1,0:T(8,128)(2,1)}, u32[]{:S(2)}, u32[]{:S(2)}) async-start(bf16[8,16,80,128]{3,2,1,0:T(8,128)(2,1)} %pack_halo.1), calls=%async_computation.1 | async-start | bytes 5242880 | tf_op jit(solution)/shard_map/all_to_all | solution.py:641
  29.5 4.1 %copy-start.1 = (f32[320,1280]{1,0:T(8,128)S(1)}, f32[320,1280]{1,0:T(8,128)}, u32[]{:S(2)}) copy-start(f32[320,1280]{1,0:T(8,128)} %param.21) | copy-start | bytes 4915204
  33.6 2.5 %copy-start.6 = (f32[2,640]{1,0:T(2,128)S(1)}, f32[2,640]{1,0:T(2,128)}, u32[]{:S(2)}) copy-start(f32[2,640]{1,0:T(2,128)} %param.18) | copy-start | bytes 15364
  33.6 2.5 %copy-start.7 = (f32[2,640]{1,0:T(2,128)S(1)}, f32[2,640]{1,0:T(2,128)}, u32[]{:S(2)}) copy-start(f32[2,640]{1,0:T(2,128)} %param.20) | copy-start | bytes 15364
  83.9 21.0 %collective-permute-start.2 = (bf16[640,128]{1,0:T(8,128)(2,1)}, bf16[640,128]{1,0:T(8,128)(2,1)S(1)}, u32[]{:S(2)}, u32[]{:S(2)}) collective-permute-start(bf16[640,128]{1,0:T(8,128)(2,1)} %get-tuple-element.31), channel_id=1, source_target_pairs={{0,1},{1,0},{2,3},{3,2},{4,5},{5,4},{6,7},{7,6},{8,9},{9,8},{10,11... | collective-permute-start | bytes 491528 | tf_op jit(solution)/shard_map/ppermute | solution.py:637
  84.0 20.9 %collective-permute-start.3 = (bf16[640,128]{1,0:T(8,128)(2,1)}, bf16[640,128]{1,0:T(8,128)(2,1)}, u32[]{:S(2)}, u32[]{:S(2)}) collective-permute-start(bf16[640,128]{1,0:T(8,128)(2,1)} %get-tuple-element.32), channel_id=1, source_target_pairs={{0,7},{1,2},{2,1},{3,4},{4,3},{5,6},{6,5},{7,0},{8,15},{9,10},{10,... | collective-permute-start | bytes 491528 | tf_op jit(solution)/shard_map/ppermute | solution.py:637
  86.2 18.7 %all-to-all-start.2 = ((f32[128,1,128]{2,1,0:T(1,128)}), f32[128,1,128]{2,1,0:T(1,128)S(1)}, u32[]{:S(2)}, u32[]{:S(2)}) async-start(f32[128,1,128]{2,1,0:T(1,128)} %bitcast.40), calls=%async_computation.2 | async-start | bytes 131072 | tf_op jit(solution)/shard_map/all_to_all | solution.py:629
  104.9 0.6 copy-start.4
  104.9 0.7 copy-start.11

commit v7 on v6

--- a/solution.py
+++ b/solution.py
@@ -81,21 +81,21 @@
 
 
 def sums_kernel(place_ref, cells_hbm, sums_ref, one_ref, other_ref, x, sems):
-    half = COLS // 2
+    half = COLS // 4
     copies = []
     for s in range(2):
-        for c in range(2):
+        for c in range(4):
             cut = slice(c * half, (c + 1) * half)
             copies.append(
-                pltpu.make_async_copy(cells_hbm.at[s, cut], x.at[s, cut], sems.at[2 * s + c])
+                pltpu.make_async_copy(cells_hbm.at[s, cut], x.at[s, cut], sems.at[4 * s + c])
             )
             copies[-1].start()
     row = jnp.zeros((1, 128), F32)
     for s in range(2):
         total = jnp.zeros((PART, LAT), F32)
         square = jnp.zeros((PART, LAT), F32)
-        for c in range(2):
-            copies[2 * s + c].wait()
+        for c in range(4):
+            copies[4 * s + c].wait()
 
             def add(i, carry):
                 total, square = carry
@@ -126,7 +126,7 @@
             jax.ShapeDtypeStruct((2, 2, PART, LAT), BF16),
             jax.ShapeDtypeStruct((2, 2, PART, LAT), BF16),
         ],
-        scratch_shapes=[pltpu.VMEM((2, COLS, PART, LAT), BF16), pltpu.SemaphoreType.DMA((4,))],
+        scratch_shapes=[pltpu.VMEM((2, COLS, PART, LAT), BF16), pltpu.SemaphoreType.DMA((8,))],
         compiler_params=PARAMS,
         name="local_sums",
     )(place, cells)

time: 142 us -> 142 us (level)
  no operation moved by 1% of the time
where the time goes in v7:
time: 142 us; the launch traced here: 141 us
  Pallas kernels  71.3 us (50%)
  starting transfers between devices  27 us (19%)
  waiting for transfers between devices  19.8 us (14%)
  blocking collectives  14.1 us (10%)
  local copies, waits for them, and re-layouts  4.84 us (3%)
  matrix products  2.51 us (2%)
    pallas_call x1, Pallas kernels, first_conv(): pl.pallas_call(first_kernel, in_specs=[SMEM] + [VMEM] * 3 + [ANY] * 2, ou...  22 us
    pallas_call x1, Pallas kernels, second_conv(): pl.pallas_call(second_kernel, in_specs=[SMEM, SMEM] + [VMEM] * 6 + [ANY]...  21 us
    all_to_all x2, starting transfers between devices, everywhere(): got = lax.all_to_all(rows.reshape(-1, 1, 128), axes, 0, 0, tiled=True)  16.7 us
    all_to_all x1, blocking collectives, everywhere(): got = lax.all_to_all(rows.reshape(-1, 1, 128), axes, 0, 0, tiled=True)  14.1 us
    pallas_call x2, Pallas kernels, turn_weights(): pl.pallas_call(functools.partial(weight_kernel, j), in_specs=[ANY], out_s...  12.7 us
    all_to_all x1, waiting for transfers between devices, swap(): return lax.all_to_all(array, axis, split_axis=0, concat_axis=0, tiled=True)  10.4 us
    all_to_all x2, waiting for transfers between devices, everywhere(): got = lax.all_to_all(rows.reshape(-1, 1, 128), axes, 0, 0, tiled=True)  9.41 us
    pallas_call x1, Pallas kernels, pack(): pl.pallas_call(pack_kernel, in_specs=[ANY], out_specs=ANY, out_shape=jax....  6.45 us
  transfers between devices with their start and end apart: 7, of which 3 were waited for; matrix products, arithmetic and copies ran while one was open for 4% of the time, Pallas kernels for 16%

profile of v7, /device:TPU:1, one launch (start us, length us, event | category | flops | bytes accessed | tf_op | source)
XLA Modules:
  0.0 141.4 jit_solution(106098694042876651)
XLA Ops:
  0.6 0.0 copy-start
  0.7 2.9 %local_sums.1 = (f32[16,128]{1,0:T(8,128)}, bf16[2,2,80,96]{3,2,1,0:T(8,128)(2,1)}, bf16[2,2,80,96]{3,2,1,0:T(8,128)(2,1)}) custom-call(s32[1]{0:T(128)} %bitcast.8.place_ref, bf16[2,64,80,96]{3,2,1,0:T(8,128)(2,1)} %bitcast.37), custom_call_target="tpu_custom_call" | custom-call | tf_op jit(solution)/shard_map/local_sums/pallas_call | solution.py:120
  3.5 1.5 %collective-permute-start = (bf16[2,2,80,96]{3,2,1,0:T(8,128)(2,1)}, bf16[2,2,80,96]{3,2,1,0:T(8,128)(2,1)S(1)}, u32[]{:S(2)}, u32[]{:S(2)}) collective-permute-start(bf16[2,2,80,96]{3,2,1,0:T(8,128)(2,1)} %get-tuple-element.21.one_ref), channel_id=1, source_target_pairs={{0,8},{8,0},{16,24},{24,16},{32,40},{40,32},{48,56},{56,48},{64,72... | collective-permute-start | bytes 184328 | tf_op jit(solution)/shard_map/ppermute | solution.py:637
  5.0 1.3 collective-permute-start.1
  6.3 7.6 %all-to-all-start = ((f32[16,1,128]{2,1,0:T(1,128)}), f32[16,1,128]{2,1,0:T(1,128)S(1)}, u32[]{:S(2)}, u32[]{:S(2)}) async-start(f32[16,1,128]{2,1,0:T(1,128)} %bitcast.43), calls=%async_computation | async-start | bytes 16384 | tf_op jit(solution)/shard_map/all_to_all | solution.py:629
  13.9 6.4 %pack_latents.1._ = bf16[8,16,80,128]{3,2,1,0:T(8,128)(2,1)} custom-call(bf16[2,64,80,96]{3,2,1,0:T(8,128)(2,1)} %bitcast.38), custom_call_target="tpu_custom_call" | custom-call | flops 1000000000 | bytes 8000000 | tf_op jit(solution)/shard_map/pack_latents/pallas_call | solution.py:181
  20.3 0.6 all-to-all-done
  20.9 0.0 copy-start.5
  20.9 0.0 collective-permute-done.from_one
  20.9 0.0 copy-start.2
  20.9 0.0 collective-permute-done.1.from_other
  21.0 0.0 copy-start.3
  21.0 0.6 copy-done.5
  21.5 0.1 copy-done.2
  21.6 0.0 copy-done.3
  21.6 2.4 %pack_halo.1 = bf16[8,16,80,128]{3,2,1,0:T(8,128)(2,1)} custom-call(s32[1]{0:T(128)} %bitcast.8.place_ref, f32[16,128]{1,0:T(8,128)} %bitcast.42, bf16[2,2,80,96]{3,2,1,0:T(8,128)(2,1)} %get-tuple-element.21.one_ref, bf16[2,2,80,96]{3,2,1,0:T(8,128)(2,1)} %get-tuple-element.22.other_ref, ...), custom_call_target="tpu_custom_call", output_to_operand_aliasing={{}: (6, {})} | custom-call | tf_op jit(solution)/shard_map/pack_halo/pallas_call | solution.py:239
  24.0 0.0 copy-start.9
  24.1 0.0 copy-start.10
  24.1 0.0 copy-start.8
  24.1 5.3 %all-to-all-start.1 = ((bf16[8,16,80,128]{3,2,1,0:T(8,128)(2,1)}), bf16[8,16,80,128]{3,2,1,0:T(8,128)(2,1)}, u32[]{:S(2)}, u32[]{:S(2)}) async-start(bf16[8,16,80,128]{3,2,1,0:T(8,128)(2,1)} %pack_halo.1), calls=%async_computation.1 | async-start | bytes 5242880 | tf_op jit(solution)/shard_map/all_to_all | solution.py:641
  29.4 0.0 copy-done.9
  29.4 0.0 copy-start.1
  29.4 0.0 copy-done.10
  29.4 0.1 fusion.11
  29.5 0.1 multiply_cosine_fusion
  29.6 0.0 copy-done.8
  29.6 3.9 %turn_target.1.target_hbm = bf16[2,6,640,128]{3,2,1,0:T(8,128)(2,1)} custom-call(bf16[12,2,64,640]{3,2,1,0:T(8,128)(2,1)} %target_hbm), custom_call_target="tpu_custom_call" | custom-call | tf_op jit(solution)/shard_map/turn_target/pallas_call | solution.py:305
  33.5 0.0 copy-start.6
  33.5 0.0 copy-start.7
  33.5 0.0 copy-done.1
  33.5 0.8 fusion.5
  34.4 0.0 copy-done
  34.4 1.7 %fusion = f32[2,640]{1,0:T(2,128)S(1)} fusion(f32[1280,640]{1,0:T(8,128)S(1)} %copy-done, f32[2,1280]{1,0:T(2,128)S(1)} %fusion.5), kind=kOutput, calls=%fused_computation.1 | convolution fusion | flops 19671040 | bytes 3292160 | tf_op jit(solution)/shard_map/dot_general | solution.py:620
  36.1 0.0 copy-done.6
  36.1 0.0 copy-done.7
  36.1 0.9 copy.27
  37.0 1.7 %pad.4.par_ref = f32[640,128]{1,0:T(8,128)} pad(f32[640,7]{1,0:T(8,128)} %copy.27, f32[]{:T(128)} %constant.46.clone.1), padding=0_0x0_121 | pad | bytes 345604 | tf_op jit(solution)/shard_map/jit(_pad)/pad | solution.py:681
  38.8 6.3 %turn_weights_0.1.w_hbm = bf16[640,5760]{1,0:T(8,128)(2,1)} custom-call(bf16[2,9,640,640]{3,2,1,0:T(8,128)(2,1)} %bitcast.35), custom_call_target="tpu_custom_call" | custom-call | flops 1887436800 | bytes 15000000 | tf_op jit(solution)/shard_map/turn_weights_0/pallas_call | solution.py:271
  45.1 6.4 %turn_weights_1.1.w_hbm = bf16[640,5760]{1,0:T(8,128)(2,1)} custom-call(bf16[2,9,640,640]{3,2,1,0:T(8,128)(2,1)} %bitcast.36), custom_call_target="tpu_custom_call" | custom-call | flops 1887436800 | bytes 15000000 | tf_op jit(solution)/shard_map/turn_weights_1/pallas_call | solution.py:271
  51.5 10.4 %all-to-all-done.1.recv_hbm = bf16[8,16,80,128]{3,2,1,0:T(8,128)(2,1)} async-done(((bf16[8,16,80,128]{3,2,1,0:T(8,128)(2,1)}), bf16[8,16,80,128]{3,2,1,0:T(8,128)(2,1)}, u32[]{:S(2)}, u32[]{:S(2)}) %all-to-all-start.1) | async-done | bytes 2621472 | tf_op jit(solution)/shard_map/all_to_all | solution.py:641
  61.8 22.0 %first_conv.1 = (f32[2,640,768]{2,1,0:T(8,128)}, f32[128,128]{1,0:T(8,128)}, bf16[640,128]{1,0:T(8,128)(2,1)}, bf16[640,128]{1,0:T(8,128)(2,1)}, bf16[640,128]{1,0:T(8,128)(2,1)}) custom-call(s32[1]{0:T(128)} %bitcast.part_ref, f32[640,128]{1,0:T(8,128)} %pad.4.par_ref, bf16[128,128]{1,0:T(8,128)(2,1)} %constant.51.clone.pick_ref, ...), custom_call_target="tpu_custom_call" | custom-call | flops 11324620800 | bytes 20000000 | tf_op jit(solution)/shard_map/first_conv/pallas_call | solution.py:463
  83.8 0.1 collective-permute-start.2
  83.9 2.2 %collective-permute-start.3 = (bf16[640,128]{1,0:T(8,128)(2,1)}, bf16[640,128]{1,0:T(8,128)(2,1)}, u32[]{:S(2)}, u32[]{:S(2)}) collective-permute-start(bf16[640,128]{1,0:T(8,128)(2,1)} %get-tuple-element.32), channel_id=1, source_target_pairs={{0,7},{1,2},{2,1},{3,4},{4,3},{5,6},{6,5},{7,0},{8,15},{9,10},{10,... | collective-permute-start | bytes 491528 | tf_op jit(solution)/shard_map/ppermute | solution.py:637
  86.1 0.1 subtract_bitcast_fusion
  86.2 9.1 %all-to-all-start.2 = ((f32[128,1,128]{2,1,0:T(1,128)}), f32[128,1,128]{2,1,0:T(1,128)S(1)}, u32[]{:S(2)}, u32[]{:S(2)}) async-start(f32[128,1,128]{2,1,0:T(1,128)} %bitcast.40), calls=%async_computation.2 | async-start | bytes 131072 | tf_op jit(solution)/shard_map/all_to_all | solution.py:629
  95.3 0.1 copy.25
  95.4 0.7 reshape.76.coef_ref
  96.0 8.8 %all-to-all-done.2 = f32[128,1,128]{2,1,0:T(1,128)S(1)} async-done(((f32[128,1,128]{2,1,0:T(1,128)}), f32[128,1,128]{2,1,0:T(1,128)S(1)}, u32[]{:S(2)}, u32[]{:S(2)}) %all-to-all-start.2) | async-done | bytes 65568 | tf_op jit(solution)/shard_map/all_to_all | solution.py:629
  104.8 0.0 copy-start.4
  104.8 0.0 collective-permute-done.2.one_ref
  104.9 0.0 copy-start.11
  104.9 0.0 collective-permute-done.3.other_ref
  104.9 0.6 copy-done.4
  105.5 0.1 copy-done.11
  105.6 21.0 %second_conv.1 = (bf16[12,2,64,640]{3,2,1,0:T(8,128)(2,1)}, f32[128,128]{1,0:T(8,128)}) custom-call(s32[1]{0:T(128)} %bitcast.part_ref, f32[4]{0:T(128)} %reshape.76.coef_ref, f32[128,128]{1,0:T(8,128)} %bitcast.39, f32[640,128]{1,0:T(8,128)} %pad.4.par_ref, bf16[2,128,128]{2,1,0:T(8,128)(2,1)} %constant.52.clone.pick_ref, ...), custom_call_target="tpu_custom_call" | custom-call | flops 11324620800 | bytes 20000000 | tf_op jit(solution)/shard_map/second_conv/pallas_call | solution.py:585
  126.6 14.1 %all_to_all.20 = f32[128,1,128]{2,1,0:T(1,128)S(1)} all-to-all(f32[128,1,128]{2,1,0:T(1,128)} %bitcast.41), channel_id=1, replica_groups=mesh['lon'=16,'ch'=8] {'lon','ch'}, dimensions={0} | all-to-all | bytes 131072 | tf_op jit(solution)/shard_map/all_to_all | solution.py:629
  140.7 0.2 reduce_sum.9
  140.8 0.6 subtract_add_fusion
  (6 shorter events, 0.1 us)
Async XLA Ops:
  0.6 33.7 %copy-start = (f32[1280,640]{1,0:T(8,128)S(1)}, f32[1280,640]{1,0:T(8,128)}, u32[]{:S(2)}) copy-start(f32[1280,640]{1,0:T(8,128)} %param.22) | copy-start | bytes 9830404
  3.5 17.4 %collective-permute-start = (bf16[2,2,80,96]{3,2,1,0:T(8,128)(2,1)}, bf16[2,2,80,96]{3,2,1,0:T(8,128)(2,1)S(1)}, u32[]{:S(2)}, u32[]{:S(2)}) collective-permute-start(bf16[2,2,80,96]{3,2,1,0:T(8,128)(2,1)} %get-tuple-element.21.one_ref), channel_id=1, source_target_pairs={{0,8},{8,0},{16,24},{24,16},{32,40},{40,32},{48,56},{56,48},{64,72... | collective-permute-start | bytes 184328 | tf_op jit(solution)/shard_map/ppermute | solution.py:637
  5.0 15.9 %collective-permute-start.1 = (bf16[2,2,80,96]{3,2,1,0:T(8,128)(2,1)}, bf16[2,2,80,96]{3,2,1,0:T(8,128)(2,1)S(1)}, u32[]{:S(2)}, u32[]{:S(2)}) collective-permute-start(bf16[2,2,80,96]{3,2,1,0:T(8,128)(2,1)} %get-tuple-element.22.other_ref), channel_id=1, source_target_pairs={{0,120},{8,16},{16,8},{24,32},{32,24},{40,48},{48,40},{56,64},{64,... | collective-permute-start | bytes 184328 | tf_op jit(solution)/shard_map/ppermute | solution.py:637
  6.3 14.6 %all-to-all-start = ((f32[16,1,128]{2,1,0:T(1,128)}), f32[16,1,128]{2,1,0:T(1,128)S(1)}, u32[]{:S(2)}, u32[]{:S(2)}) async-start(f32[16,1,128]{2,1,0:T(1,128)} %bitcast.43), calls=%async_computation | async-start | bytes 16384 | tf_op jit(solution)/shard_map/all_to_all | solution.py:629
  20.9 0.6 copy-start.5
  20.9 0.6 copy-start.2
  21.0 0.7 copy-start.3
  24.0 5.3 %copy-start.9 = (s32[2]{0:T(128)S(1)}, s32[2]{0:T(128)}, u32[]{:S(2)}) copy-start(s32[2]{0:T(128)} %param.15) | copy-start | bytes 28
  24.1 5.4 %copy-start.10 = (s32[2]{0:T(128)S(1)}, s32[2]{0:T(128)}, u32[]{:S(2)}) copy-start(s32[2]{0:T(128)} %param.16) | copy-start | bytes 28
  24.1 5.5 %copy-start.8 = (f32[2,640]{1,0:T(2,128)S(1)}, f32[2,640]{1,0:T(2,128)}, u32[]{:S(2)}) copy-start(f32[2,640]{1,0:T(2,128)} %param.19) | copy-start | bytes 15364
  24.1 37.7 %all-to-all-start.1 = ((bf16[8,16,80,128]{3,2,1,0:T(8,128)(2,1)}), bf16[8,16,80,128]{3,2,1,0:T(8,128)(2,1)}, u32[]{:S(2)}, u32[]{:S(2)}) async-start(bf16[8,16,80,128]{3,2,1,0:T(8,128)(2,1)} %pack_halo.1), calls=%async_computation.1 | async-start | bytes 5242880 | tf_op jit(solution)/shard_map/all_to_all | solution.py:641
  29.4 4.1 %copy-start.1 = (f32[320,1280]{1,0:T(8,128)S(1)}, f32[320,1280]{1,0:T(8,128)}, u32[]{:S(2)}) copy-start(f32[320,1280]{1,0:T(8,128)} %param.21) | copy-start | bytes 4915204
  33.5 2.5 %copy-start.6 = (f32[2,640]{1,0:T(2,128)S(1)}, f32[2,640]{1,0:T(2,128)}, u32[]{:S(2)}) copy-start(f32[2,640]{1,0:T(2,128)} %param.18) | copy-start | bytes 15364
  33.5 2.5 %copy-start.7 = (f32[2,640]{1,0:T(2,128)S(1)}, f32[2,640]{1,0:T(2,128)}, u32[]{:S(2)}) copy-start(f32[2,640]{1,0:T(2,128)} %param.20) | copy-start | bytes 15364
  83.8 21.0 %collective-permute-start.2 = (bf16[640,128]{1,0:T(8,128)(2,1)}, bf16[640,128]{1,0:T(8,128)(2,1)S(1)}, u32[]{:S(2)}, u32[]{:S(2)}) collective-permute-start(bf16[640,128]{1,0:T(8,128)(2,1)} %get-tuple-element.31), channel_id=1, source_target_pairs={{0,1},{1,0},{2,3},{3,2},{4,5},{5,4},{6,7},{7,6},{8,9},{9,8},{10,11... | collective-permute-start | bytes 491528 | tf_op jit(solution)/shard_map/ppermute | solution.py:637
  83.9 20.9 %collective-permute-start.3 = (bf16[640,128]{1,0:T(8,128)(2,1)}, bf16[640,128]{1,0:T(8,128)(2,1)}, u32[]{:S(2)}, u32[]{:S(2)}) collective-permute-start(bf16[640,128]{1,0:T(8,128)(2,1)} %get-tuple-element.32), channel_id=1, source_target_pairs={{0,7},{1,2},{2,1},{3,4},{4,3},{5,6},{6,5},{7,0},{8,15},{9,10},{10,... | collective-permute-start | bytes 491528 | tf_op jit(solution)/shard_map/ppermute | solution.py:637
  86.2 18.7 %all-to-all-start.2 = ((f32[128,1,128]{2,1,0:T(1,128)}), f32[128,1,128]{2,1,0:T(1,128)S(1)}, u32[]{:S(2)}, u32[]{:S(2)}) async-start(f32[128,1,128]{2,1,0:T(1,128)} %bitcast.40), calls=%async_computation.2 | async-start | bytes 131072 | tf_op jit(solution)/shard_map/all_to_all | solution.py:629
  104.8 0.6 copy-start.4
  104.9 0.7 copy-start.11
